TPU v7x, 32 devices: a whole 2x2x4 slice. The times are simulated.
32 devices in a mesh: dp: 16 (over z, y, x), sub: 2 (over core).
Axes of the slice: x: 2, y: 2, z: 4, core: 2. Of those that a mesh axis runs over, the one named last changes fastest.
Arguments:
- queries: bfloat16 [6144, 4096], P('dp', 'sub'), may hold values from -32 to 32
- passages: bfloat16 [6144, 4096], P('dp', 'sub'), may hold values from -8 to 8
- positive: int32 [16, 384], P('dp'), may hold values from 0 to 383, each once within a row
- pair_on: int32 [16, 3], replicated, may hold values from 0 to 1, as said below
Outputs:
- loss: float32 [1], replicated
- query_grad: float32 [6144, 4096], P('dp', 'sub')
- passage_grad: float32 [6144, 4096], P('dp', 'sub')
Inputs may be any that keep to these rules, and one draw needn't show every extreme that they name: pair_on[s, k] equals pair_on[s xor 2 ** (log2(16) - 3 + k), k]; shards 0 and 2 ** (log2(16) - 3) - 1 pair at every level.
All inputs are finite; a program needn't handle non-finite values.
Results may differ from a plain program's by a relative error of at most 0.0016.
Values may be sent and summed in bfloat16 or wider, within the bound.
No kernel may reach another device: no remote copies, remote signals or barrier semaphores. Data moves between devices by JAX's collectives and lax.ppermute only.
A program may use at most 128 MiB of HBM per device.

v0:
```python
import math

import jax
import jax.numpy as jnp
from jax import lax
from jax.sharding import PartitionSpec as P

D = 4096


def swapped(block, axis, bit):
    count = lax.axis_size(axis)
    route = []
    for low in range(count):
        high = low | 1 << bit
        if high != low and high < count:
            route += [(low, high), (high, low)]
    return lax.ppermute(block, axis, route)


def tile_logits(left, right):
    return lax.dot_general(
        left, right, (((1,), (1,)), ((), ())), preferred_element_type=jnp.float32
    ) / math.sqrt(D)


def transposed_product(grad, block):
    return lax.dot_general(
        grad, block, (((0,), (0,)), ((), ())), preferred_element_type=jnp.float32
    )


def lse_axis(values, axis):
    return jax.scipy.special.logsumexp(values, axis=axis)


def local(queries, passages, positive, pair_on):
    rows, width = queries.shape
    levels = pair_on.shape[1]
    me = lax.axis_index("dp")
    depth = lax.axis_size("dp").bit_length() - 1
    level_bits = []
    actives = []
    far_blocks = []
    partial_tiles = [tile_logits(queries, passages)]
    for level in range(levels):
        bit = depth - levels + level
        active = pair_on[me, level] > 0
        received = swapped(jnp.stack([queries, passages]), "dp", bit)
        far_q = received[0]
        far_p = received[1]
        pair_tile = lax.cond(
            active,
            lambda: tile_logits(queries, far_p),
            lambda: jnp.zeros((rows, rows), jnp.float32),
        )
        partial_tiles.append(pair_tile)
        level_bits.append(bit)
        actives.append(active)
        far_blocks.append((far_q, far_p))
    summed = lax.psum(jnp.stack(partial_tiles), "sub")
    own = summed[0]
    columns = jnp.arange(rows, dtype=jnp.int32)
    onehot = (positive[0][:, None] == columns[None, :]).astype(jnp.float32)
    row_lse = lse_axis(own, 1)
    col_lse = lse_axis(own, 0)
    for level in range(levels):
        tile = summed[1 + level]
        active = actives[level]
        row_lse = jnp.where(active, jnp.logaddexp(row_lse, lse_axis(tile, 1)), row_lse)
        outgoing = jnp.where(active, lse_axis(tile, 0), -jnp.inf)
        incoming = swapped(outgoing, "dp", level_bits[level])
        col_lse = jnp.where(active, jnp.logaddexp(col_lse, incoming), col_lse)
    grad_own = (
        jnp.exp(own - row_lse[:, None]) + jnp.exp(own - col_lse[None, :]) - 2.0 * onehot
    ).astype(jnp.bfloat16)
    query_grad = jnp.dot(grad_own, passages, preferred_element_type=jnp.float32)
    passage_grad = transposed_product(grad_own, queries)
    for level in range(levels):
        bit = level_bits[level]
        active = actives[level]
        far_q, far_p = far_blocks[level]
        tile = summed[1 + level]
        far_cols = swapped(col_lse, "dp", bit)
        g_tile = jnp.exp(tile - row_lse[:, None]) + jnp.exp(tile - far_cols[None, :])
        g_tile = jnp.where(active, g_tile, 0.0).astype(jnp.bfloat16)
        near_term = lax.cond(
            active,
            lambda: jnp.dot(g_tile, far_p, preferred_element_type=jnp.float32),
            lambda: jnp.zeros((rows, width), jnp.float32),
        )
        query_grad = query_grad + near_term
        back = lax.cond(
            active,
            lambda: transposed_product(g_tile, queries),
            lambda: jnp.zeros((rows, width), jnp.float32),
        )
        returned = swapped(back, "dp", bit)
        passage_grad = passage_grad + jnp.where(active, returned, 0.0)
    local_total = jnp.sum(row_lse) + jnp.sum(col_lse) - 2.0 * jnp.sum(own * onehot)
    total = lax.psum(local_total, "dp")
    loss = jnp.reshape(total / (2.0 * rows * lax.axis_size("dp")), (1,))
    return (loss, query_grad, passage_grad)


def solution(mesh):
    placed = (P("dp", "sub"), P("dp", "sub"), P("dp", None), P())
    return jax.shard_map(
        local,
        mesh=mesh,
        in_specs=placed,
        out_specs=(P(), P("dp", "sub"), P("dp", "sub")),
        check_vma=False,
    )
```

profile of v0, /device:TPU:0, one launch (start us, length us, event | category | flops | bytes accessed | tf_op | source)
XLA Modules:
  0.0 425.0 jit_solution(181881432458428615)
XLA Ops:
  7.2 4.0 pad_maximum_fusion
  11.2 4.0 collective-permute-start.2
  15.3 1.6 collective-permute-start.1
  16.8 1.5 collective-permute-start
  21.0 1.8 fusion.3
  22.8 128.4 %collective-permute-done.2 = bf16[2,384,2048]{2,1,0:T(8,128)(2,1)} collective-permute-done((bf16[2,384,2048]{2,1,0:T(8,128)(2,1)}, bf16[2,384,2048]{2,1,0:T(8,128)(2,1)}, u32[]{:S(2)}, u32[]{:S(2)}) %collective-permute-start.2) | collective-permute-done | bytes 3145760 | tf_op jit(solution)/shard_map/ppermute | solution.py:18
  151.2 2.7 slice_bitcast_fusion
  153.9 2.8 slice_bitcast_fusion.1
  156.7 1.5 slice_bitcast_fusion.2
  158.2 3.3 conditional.11
  158.2 3.3 fusion.2
  161.5 3.2 conditional.10
  161.5 3.2 fusion.1
  164.7 1.8 conditional.9
  164.7 1.8 fusion
  166.5 3.2 pad_maximum_fusion.1
  169.7 0.7 copy-done.5
  170.4 20.3 %all-reduce.2.cloned.1.call-done = f32[4,384,384]{2,1,0:T(8,128)} async-done(((f32[4,384,384]{2,1,0:T(8,128)}), f32[4,384,384]{2,1,0:T(8,128)}) %all-reduce.2.cloned.1.call-update) | async-done | bytes 2359312 | tf_op jit(solution)/shard_map/psum | solution.py:61
  190.7 2.0 slice_reduce_fusion.6
  193.1 1.7 fusion.35
  194.8 2.7 collective-permute-start.5
  197.5 1.5 collective-permute-start.4
  199.0 1.5 collective-permute-start.3
  201.1 1.5 collective-permute-done.3
  202.6 0.7 fusion.45
  203.3 1.5 collective-permute-start.6
  205.9 0.7 fusion.46
  206.9 1.5 collective-permute-done.7
  208.4 1.4 collective-permute-done.8
  209.8 1.4 fusion.29
  211.2 3.7 conditional.17
  211.2 3.7 fusion.52
  215.4 3.6 conditional.16
  215.4 3.6 fusion.51
  219.1 1.5 collective-permute-start.10
  220.6 2.7 conditional.15
  220.6 2.7 fusion.50
  225.2 157.5 %psum.15 = f32[]{:T(128)} all-reduce(f32[]{:T(128)S(6)} %sub.180), channel_id=1, replica_groups=mesh['dp'=16,'sub'=2] {'dp'}, use_global_device_ids=true, to_apply=%region_26.27 | all-reduce | flops 1 | bytes 8 | tf_op jit(solution)/shard_map/psum | solution.py:101
  383.3 4.4 %fusion.43 = f32[384,2048]{1,0:T(8,128)} fusion(bf16[384,2048]{1,0:T(8,128)(2,1)} %param.23, f32[4,384,384]{2,1,0:T(8,128)} %all-reduce.2.cloned.1.call-done, f32[384]{0:T(512)S(1)} %get-tuple-element.105, f32[384]{0:T(512)S(1)} %get-tuple-element.107, s32[384]{0:T(512)S(1)} %reduce.8), kind=kOutput, calls=%fused_computation.104 | convolution fusion | flops 605011968 | bytes 5313024 | tf_op jit(solution)/shard_map/dot_general | solution.py:77
  387.7 3.9 fusion.41
  391.5 4.3 %conditional.14 = (f32[384,2048]{1,0:T(8,128)}) conditional(s32[]{:T(128)} %convert_element_type.30, () %tuple.78, (bf16[384,384]{1,0:T(8,128)(2,1)}, bf16[384,2048]{1,0:T(8,128)(2,1)}) %tuple.79), branch_computations={%region_31.32_spmd, %region_32.33_spmd} | conditional | flops 603979776 | bytes 5013512 | solution.py:87
  391.5 4.3 %fusion.49 = f32[384,2048]{1,0:T(8,128)} fusion(bf16[384,384]{1,0:T(8,128)(2,1)} %get-tuple-element.76, bf16[384,2048]{1,0:T(8,128)(2,1)} %get-tuple-element.77), kind=kOutput, calls=%fused_computation.109 | convolution fusion | flops 603979776 | bytes 5013504 | tf_op jit(solution)/shard_map/cond/branch_1_fun/dot_general | solution.py:89
  395.8 3.6 conditional.13
  395.8 3.6 fusion.48
  399.4 2.6 conditional.12
  399.4 2.6 fusion.47
  402.1 8.1 %add_add_fusion = f32[384,2048]{1,0:T(8,128)} fusion(f32[384,2048]{1,0:T(8,128)} %get-tuple-element.127, f32[384,2048]{1,0:T(8,128)} %get-tuple-element.126, f32[384,2048]{1,0:T(8,128)} %fusion.43, f32[384,2048]{1,0:T(8,128)} %get-tuple-element.125), kind=kLoop, calls=%fused_computation.8 | loop fusion | flops 2359296 | bytes 15728640 | tf_op jit(solution)/shard_map/add | solution.py:92
  410.2 6.8 %select_add_fusion = f32[384,2048]{1,0:T(8,128)} fusion(f32[384,2048]{1,0:T(8,128)} %collective-permute-done.11, f32[384,2048]{1,0:T(8,128)} %collective-permute-done.10, f32[384,2048]{1,0:T(8,128)S(1)} %copy-done.2, f32[384,2048]{1,0:T(8,128)} %collective-permute-done.9, pred[]{:T(512)} %bitcast.3, pred[]{:T(512)} %bitcast.4, pred[]{:T(512)} %bitcast.5), kind=kLoop, calls=%fused_computation.7 | loop fusion | flops 4718592 | bytes 15728643 | tf_op jit(solution)/shard_map/add | solution.py:99
  (36 shorter events, 3.6 us)
Async XLA Ops:
  7.2 183.5 %all-reduce.2.cloned.1.call-start = ((), (), s32[]{:S(2)}) async-start(), calls=%async_computation | async-start | bytes 4718592 | tf_op jit(solution)/shard_map/psum | solution.py:61
  7.2 11.2 %copy-start.6 = (s32[16,3]{0,1:T(4,128)S(1)}, s32[16,3]{0,1:T(4,128)}, u32[]{:S(2)}) copy-start(s32[16,3]{0,1:T(4,128)} %param.25) | copy-start | bytes 580
  7.2 13.7 %copy-start = (bf16[384,2048]{1,0:T(8,128)(2,1)S(1)}, bf16[384,2048]{1,0:T(8,128)(2,1)}, u32[]{:S(2)}) copy-start(bf16[384,2048]{1,0:T(8,128)(2,1)} %param.22) | copy-start | bytes 4718596
  7.2 13.7 %copy-start.4 = (bf16[384,2048]{1,0:T(8,128)(2,1)S(1)}, bf16[384,2048]{1,0:T(8,128)(2,1)}, u32[]{:S(2)}) copy-start(bf16[384,2048]{1,0:T(8,128)(2,1)} %param.23) | copy-start | bytes 4718596
  11.2 140.0 %collective-permute-start.2 = (bf16[2,384,2048]{2,1,0:T(8,128)(2,1)}, bf16[2,384,2048]{2,1,0:T(8,128)(2,1)}, u32[]{:S(2)}, u32[]{:S(2)}) collective-permute-start(bf16[2,384,2048]{2,1,0:T(8,128)(2,1)} %pad_maximum_fusion), channel_id=1, source_target_pairs={{0,16},{16,0},{2,18},{18,2},{4,20},{20,4},{6,22},{22,6},{8,24},{24... | collective-permute-start | bytes 9437192 | tf_op jit(solution)/shard_map/ppermute | solution.py:18
  15.3 138.7 %collective-permute-start.1 = (bf16[2,384,2048]{2,1,0:T(8,128)(2,1)}, bf16[2,384,2048]{2,1,0:T(8,128)(2,1)}, u32[]{:S(2)}, u32[]{:S(2)}) collective-permute-start(bf16[2,384,2048]{2,1,0:T(8,128)(2,1)} %pad_maximum_fusion), channel_id=1, source_target_pairs={{0,8},{8,0},{2,10},{10,2},{4,12},{12,4},{6,14},{14,6},{16,24},{24,... | collective-permute-start | bytes 9437192 | tf_op jit(solution)/shard_map/ppermute | solution.py:18
  16.8 139.9 %collective-permute-start = (bf16[2,384,2048]{2,1,0:T(8,128)(2,1)}, bf16[2,384,2048]{2,1,0:T(8,128)(2,1)}, u32[]{:S(2)}, u32[]{:S(2)}) collective-permute-start(bf16[2,384,2048]{2,1,0:T(8,128)(2,1)} %pad_maximum_fusion), channel_id=1, source_target_pairs={{0,4},{4,0},{2,6},{6,2},{8,12},{12,8},{10,14},{14,10},{16,20},{20,... | collective-permute-start | bytes 9437192 | tf_op jit(solution)/shard_map/ppermute | solution.py:18
  169.7 0.7 copy-start.5
  190.7 2.4 copy-start.1
  194.8 5.7 %collective-permute-start.5 = (f32[384]{0:T(512)S(1)}, f32[384]{0:T(512)S(1)}, u32[]{:S(2)}, u32[]{:S(2)}) collective-permute-start(f32[384]{0:T(512)S(1)} %add_select_fusion), channel_id=1, source_target_pairs={{0,16},{16,0},{2,18},{18,2},{4,20},{20,4},{6,22},{22,6},{8,24},{24... | collective-permute-start | bytes 4616 | tf_op jit(solution)/shard_map/ppermute | solution.py:18
  197.5 3.6 collective-permute-start.4
  199.0 3.6 collective-permute-start.3
  203.3 3.6 collective-permute-start.6
  204.8 3.6 collective-permute-start.7
  205.3 4.5 %collective-permute-start.8 = (f32[384]{0:T(512)S(1)}, f32[384]{0:T(512)S(1)}, u32[]{:S(2)}, u32[]{:S(2)}) collective-permute-start(f32[384]{0:T(512)S(1)} %get-tuple-element.105), channel_id=1, source_target_pairs={{0,16},{16,0},{2,18},{18,2},{4,20},{20,4},{6,22},{22,6},{8,24},{24... | collective-permute-start | bytes 4616 | tf_op jit(solution)/shard_map/ppermute | solution.py:18
  214.9 195.2 %collective-permute-start.11 = (f32[384,2048]{1,0:T(8,128)}, f32[384,2048]{1,0:T(8,128)}, u32[]{:S(2)}, u32[]{:S(2)}) collective-permute-start(f32[384,2048]{1,0:T(8,128)} %get-tuple-element.130), channel_id=1, source_target_pairs={{0,16},{16,0},{2,18},{18,2},{4,20},{20,4},{6,22},{22,6},{8,24},{24... | collective-permute-start | bytes 9437192 | tf_op jit(solution)/shard_map/ppermute | solution.py:18
  219.1 191.1 %collective-permute-start.10 = (f32[384,2048]{1,0:T(8,128)}, f32[384,2048]{1,0:T(8,128)}, u32[]{:S(2)}, u32[]{:S(2)}) collective-permute-start(f32[384,2048]{1,0:T(8,128)} %get-tuple-element.129), channel_id=1, source_target_pairs={{0,8},{8,0},{2,10},{10,2},{4,12},{12,4},{6,14},{14,6},{16,24},{24,... | collective-permute-start | bytes 9437192 | tf_op jit(solution)/shard_map/ppermute | solution.py:18
  223.3 186.9 %collective-permute-start.9 = (f32[384,2048]{1,0:T(8,128)}, f32[384,2048]{1,0:T(8,128)}, u32[]{:S(2)}, u32[]{:S(2)}) collective-permute-start(f32[384,2048]{1,0:T(8,128)} %get-tuple-element.128), channel_id=1, source_target_pairs={{0,4},{4,0},{2,6},{6,2},{8,12},{12,8},{10,14},{14,10},{16,20},{20,... | collective-permute-start | bytes 9437192 | tf_op jit(solution)/shard_map/ppermute | solution.py:18
  391.5 4.3 %copy-start.3 = (bf16[384,2048]{1,0:T(8,128)(2,1)S(1)}, bf16[384,2048]{1,0:T(8,128)(2,1)}, u32[]{:S(2)}) copy-start(bf16[384,2048]{1,0:T(8,128)(2,1)} %slice_bitcast_fusion.1) | copy-start | bytes 4718596
  402.1 8.1 %copy-start.2 = (f32[384,2048]{1,0:T(8,128)S(1)}, f32[384,2048]{1,0:T(8,128)}, u32[]{:S(2)}) copy-start(f32[384,2048]{1,0:T(8,128)} %fusion.41) | copy-start | bytes 9437188
Sparse Core Ops, SparseCore 0:
  169.8 20.8 all-reduce.1
where the time goes:
time: 425 us
  blocking collectives  157 us (37%)
  waiting for transfers between devices  154 us (36%)
  matrix products  38.9 us (9%)
  other arithmetic  28.7 us (7%)
  between operations  19.8 us (5%)
  starting transfers between devices  17.4 us (4%)
  local copies, waits for them, and re-layouts  8.6 us (2%)
    psum x1, blocking collectives, local(): total = lax.psum(local_total, 'dp')  157 us
    ppermute x12, waiting for transfers between devices, swapped(): return lax.ppermute(block, axis, route)  134 us
    psum x1, waiting for transfers between devices, local(): summed = lax.psum(jnp.stack(partial_tiles), 'sub')  20.3 us
    ppermute x12, starting transfers between devices, swapped(): return lax.ppermute(block, axis, route)  17.3 us
    dot_general x4, matrix products, transposed_product(): lax.dot_general(grad, block, (((0,), (0,)), ((), ())), preferred_element_...  13.9 us
    dot_general x3, matrix products, local(): jnp.dot(g_tile, far_p, preferred_element_type=jnp.float32)  10.5 us
    dot_general x4, matrix products, tile_logits(): lax.dot_general(left, right, (((1,), (1,)), ((), ())), preferred_element_...  10.1 us
  transfers between devices with their start and end apart: 13, of which 7 were waited for; matrix products, arithmetic and copies ran while one was open for 10% of the time, Pallas kernels for 0%

commit v1 on v0

v1 whole, which is shorter than its diff:
```python
import functools
import math

import jax
import jax.numpy as jnp
from jax import lax
from jax.experimental import pallas as pl
from jax.experimental.pallas import tpu as pltpu
from jax.sharding import PartitionSpec as P

D = 4096
ABSENT = -1e30


def exchanged(block, axis, offset):
    count = lax.axis_size(axis)
    return lax.ppermute(block, axis, [(i, i ^ offset) for i in range(count)])


def call(kernel, out_shape, operands, **kwargs):
    scalars, unread = kwargs.pop("scalars", 0), kwargs.pop("unread", 0)
    flops = kwargs.pop("flops", 0)
    kwargs["in_specs"] = (
        [pl.BlockSpec(memory_space=pltpu.SMEM)] * scalars
        + [pl.BlockSpec(memory_space=pltpu.VMEM)] * (len(operands) - scalars - unread)
        + [pl.BlockSpec(memory_space=pl.ANY)] * unread
    )
    if "out_specs" not in kwargs:
        kwargs["out_specs"] = jax.tree.map(
            lambda _: pl.BlockSpec(memory_space=pltpu.VMEM), out_shape
        )
    return pl.pallas_call(
        kernel,
        out_shape=out_shape,
        compiler_params=pltpu.CompilerParams(vmem_limit_bytes=20 * 1024 * 1024),
        cost_estimate=pl.CostEstimate(flops=flops, bytes_accessed=0, transcendentals=0),
        **kwargs,
    )(*operands)


def f32(*shape):
    return jax.ShapeDtypeStruct(shape, jnp.float32)


def bf16(*shape):
    return jax.ShapeDtypeStruct(shape, jnp.bfloat16)


def rows_kernel(count, right_ref, *refs):
    for ref, out_ref in zip(refs[:count], refs[-count:]):
        out_ref[...] = lax.dot_general(
            ref[...],
            right_ref[...],
            (((1,), (1,)), ((), ())),
            preferred_element_type=jnp.float32,
        )


def partial_rows(right, blocks, after=()):
    return call(
        functools.partial(rows_kernel, len(blocks)),
        [f32(block.shape[0], right.shape[0]) for block in blocks],
        [right, *blocks, *after],
        unread=len(after),
    )


def tiles_kernel(count, left_ref, *refs):
    out_ref = refs[-1]
    for k, ref in enumerate(refs[:count]):
        out_ref[k] = lax.dot_general(
            left_ref[...],
            ref[...],
            (((1,), (1,)), ((), ())),
            preferred_element_type=jnp.float32,
        )


def partial_tiles(left, blocks, after=()):
    rows, count = left.shape[0], len(blocks)
    return call(
        functools.partial(tiles_kernel, count),
        f32(count, rows, rows),
        [left, *blocks, *after],
        unread=len(after),
    )


def copy_kernel(first, array_ref, *refs):
    refs[-1][...] = array_ref[first : first + refs[-1].shape[0], :]


def rows_after(array, first, count, earlier):
    return call(
        functools.partial(copy_kernel, first),
        jax.ShapeDtypeStruct((count, array.shape[1]), array.dtype),
        [array, *earlier],
        unread=len(earlier),
    )


def pass_kernel(*refs):
    pass


def held_until(array, earlier):
    count = 1 + len(earlier)
    return pl.pallas_call(
        pass_kernel,
        out_shape=jax.ShapeDtypeStruct(array.shape, array.dtype),
        in_specs=[pl.BlockSpec(memory_space=pl.ANY)] * count,
        out_specs=pl.BlockSpec(memory_space=pl.ANY),
        input_output_aliases={0: 0},
        cost_estimate=pl.CostEstimate(flops=0, bytes_accessed=0, transcendentals=0),
    )(array, *earlier)


def join_kernel(upper_ref, lower_ref, out_ref):
    out_ref[: upper_ref.shape[0], :] = upper_ref[...]
    out_ref[upper_ref.shape[0] :, :] = lower_ref[...]


def joined(upper, lower):
    shape = (upper.shape[0] + lower.shape[0], upper.shape[1])
    return call(join_kernel, jax.ShapeDtypeStruct(shape, upper.dtype), [upper, lower])


def stack_kernel(count, *refs):
    for k in range(count):
        refs[-1][k] = refs[k][...]


def as_row(column, rows):
    i = lax.broadcasted_iota(jnp.int32, (rows, rows), 0)
    j = lax.broadcasted_iota(jnp.int32, (rows, rows), 1)
    return jnp.sum(jnp.where(i == j, column, 0.0), axis=0, keepdims=True)


def as_column(row, rows):
    i = lax.broadcasted_iota(jnp.int32, (rows, rows), 0)
    j = lax.broadcasted_iota(jnp.int32, (rows, rows), 1)
    return jnp.sum(jnp.where(i == j, row, 0.0), axis=1, keepdims=True)


def stats_kernel(levels, slots, unread, act_ref, *refs):
    *refs, tile_ref, row_ref, pack_ref = refs
    *part_refs, pos_ref = refs[: len(refs) - unread]
    rows = tile_ref.shape[1]
    scale = 1.0 / math.sqrt(D)
    slots = iter(slots)
    for mine_ref, other_ref in zip(part_refs[0::2], part_refs[1::2]):
        for k in range(mine_ref.shape[0]):
            tile_ref[next(slots)] = (mine_ref[k] + other_ref[k]) * scale
    top = jnp.max(tile_ref[0], axis=1, keepdims=True)
    for k in range(levels):
        seen = jnp.max(tile_ref[k + 1], axis=1, keepdims=True)
        top = jnp.where(act_ref[k] > 0, jnp.maximum(top, seen), top)
    total = jnp.sum(jnp.exp(tile_ref[0] - top), axis=1, keepdims=True)
    for k in range(levels):
        seen = jnp.sum(jnp.exp(tile_ref[k + 1] - top), axis=1, keepdims=True)
        total = jnp.where(act_ref[k] > 0, total + seen, total)
    row_lse = top + jnp.log(total)
    row_ref[...] = row_lse
    pack_ref[...] = jnp.zeros_like(pack_ref)
    for k in range(levels + 1):
        tile = tile_ref[k]
        high = jnp.max(tile, axis=0, keepdims=True)
        col = high + jnp.log(jnp.sum(jnp.exp(tile - high), axis=0, keepdims=True))
        if k == 0:
            pack_ref[levels : levels + 1, :] = col
        else:
            pack_ref[k - 1 : k, :] = jnp.where(act_ref[k - 1] > 0, col, ABSENT)
    pack_ref[levels + 1 : levels + 2, :] = as_row(row_lse, rows)
    columns = lax.broadcasted_iota(jnp.int32, (rows, rows), 1)
    picked = jnp.where(pos_ref[...] == columns, tile_ref[0], 0.0)
    picked = jnp.sum(jnp.sum(picked, axis=1, keepdims=True), axis=0, keepdims=True)
    pack_ref[levels + 2 : levels + 3, :] = jnp.broadcast_to(picked, (1, rows))


def grads_kernel(
    levels, act_ref, tile_ref, row_ref, pos_ref, *refs
):
    group = 1 << levels
    packs = refs[:group]
    grad_ref, back_ref, col_ref, far_ref, loss_ref = refs[group:]
    rows = tile_ref.shape[1]

    def columns_of(member):
        terms = [packs[member][levels : levels + 1, :]]
        for k in range(levels):
            terms.append(packs[member ^ 1 << k][k : k + 1, :])
        top = functools.reduce(jnp.maximum, terms)
        return top + jnp.log(sum(jnp.exp(term - top) for term in terms))

    col_lses = [columns_of(member) for member in range(group)]
    loss = jnp.zeros((1, 1), jnp.float32)
    for member in range(group):
        line = col_lses[member] + packs[member][levels + 1 : levels + 2, :]
        loss += jnp.sum(line, axis=1, keepdims=True)
        loss -= 2.0 * packs[member][levels + 2 : levels + 3, 0:1]
    loss_ref[...] = jnp.broadcast_to(loss, loss_ref.shape)

    far_ref[...] = jnp.zeros_like(far_ref)
    col_ref[...] = jnp.zeros_like(col_ref)
    for k in range(levels):
        far = packs[1 << k][levels + 1 : levels + 2, :]
        far = jnp.where(act_ref[k] > 0, far, -ABSENT)
        far_ref[:, k : k + 1] = as_column(far, rows)
        col_ref[k : k + 1, :] = jnp.where(act_ref[k] > 0, col_lses[0], -ABSENT)
    row_lse = row_ref[...]
    own = tile_ref[0]
    columns = lax.broadcasted_iota(jnp.int32, (rows, rows), 1)
    onehot = jnp.where(pos_ref[...] == columns, 2.0, 0.0)
    grad = jnp.exp(own - row_lse) + jnp.exp(own - col_lses[0]) - onehot
    grad_ref[0] = grad.astype(jnp.bfloat16)
    back_ref[...] = grad.T.astype(jnp.bfloat16)
    for k in range(levels):
        tile = tile_ref[k + 1]
        grad = jnp.exp(tile - row_lse) + jnp.exp(tile - col_lses[1 << k])
        grad_ref[k + 1] = jnp.where(act_ref[k] > 0, grad, 0.0).astype(jnp.bfloat16)


def dot(left, right):
    return jnp.dot(left, right, preferred_element_type=jnp.float32)


STEP = 512


def column_blocks(width):
    return [slice(first, first + STEP) for first in range(0, width, STEP)]


def copied_out(buffer_ref, out_ref, sems, j, cols):
    return pltpu.make_async_copy(buffer_ref.at[j], out_ref.at[:, cols], sems.at[j])


def copy_scratch(rows, width):
    steps = width // STEP
    return [pltpu.VMEM((steps, rows, STEP), jnp.float32), pltpu.SemaphoreType.DMA((steps,))]


def query_kernel(count, grad_ref, *refs):
    out_ref, token_ref, buffer_ref, sems = refs[count:]
    token_ref[...] = jnp.zeros_like(token_ref)
    blocks = column_blocks(out_ref.shape[1])
    for j, cols in enumerate(blocks):
        total = dot(grad_ref[0], refs[0][:, cols])
        for k in range(1, count):
            total += dot(grad_ref[k], refs[k][:, cols])
        buffer_ref[j] = total
        copied_out(buffer_ref, out_ref, sems, j, cols).start()
    for j, cols in enumerate(blocks):
        copied_out(buffer_ref, out_ref, sems, j, cols).wait()


def query_product(grads, blocks):
    count, rows, width = len(blocks), *blocks[0].shape
    return call(
        functools.partial(query_kernel, count),
        (f32(rows, width), f32(8, 128)),
        [grads, *blocks],
        out_specs=(
            pl.BlockSpec(memory_space=pl.ANY),
            pl.BlockSpec(memory_space=pltpu.VMEM),
        ),
        scratch_shapes=copy_scratch(rows, width),
    )


def passage_kernel(pieces, last, col_ref, far_ref, *refs):
    count = len(pieces)
    parts, refs = refs[: 2 * count], refs[2 * count :]
    heads = 1 if last else 2
    head, blocks = refs[:heads], refs[heads : heads + count]
    out_ref, *scratch = refs[heads + count :]
    grads = scratch[:count]
    for n, (k, start) in enumerate(pieces):
        rows = blocks[n].shape[0]
        tile = (parts[2 * n][...] + parts[2 * n + 1][...]) * (1.0 / math.sqrt(D))
        far = far_ref[start : start + rows, k : k + 1]
        grad = jnp.exp(tile - far) + jnp.exp(tile - col_ref[k : k + 1, :])
        grads[n][...] = grad.T.astype(jnp.bfloat16)

    columns = column_blocks(out_ref.shape[1])
    for j, cols in enumerate(columns):
        if last:
            total = head[0][:, cols]
        else:
            total = dot(head[0][...], head[1][:, cols])
        for grad_ref, block in zip(grads, blocks):
            total += dot(grad_ref[...], block[:, cols])
        if last:
            buffer_ref, sems = scratch[count:]
            buffer_ref[j] = total
            copied_out(buffer_ref, out_ref, sems, j, cols).start()
        else:
            out_ref[:, cols] = total
    if last:
        for j, cols in enumerate(columns):
            copied_out(buffer_ref, out_ref, sems, j, cols).wait()


def passage_product(col, far, head, parts, pieces, blocks, last):
    rows, width = far.shape[0], blocks[0].shape[1]
    scratch = [pltpu.VMEM((rows, block.shape[0]), jnp.bfloat16) for block in blocks]
    if last:
        scratch += copy_scratch(rows, width)
    return call(
        functools.partial(passage_kernel, pieces, last),
        f32(rows, width),
        [col, far, *parts, *head, *blocks],
        out_specs=pl.BlockSpec(memory_space=pl.ANY if last else pltpu.VMEM),
        scratch_shapes=scratch,
    )


def local(queries, passages, positive, pair_on):
    rows, _ = queries.shape
    levels = pair_on.shape[1]
    me = lax.axis_index("dp")
    shards = lax.axis_size("dp")
    low = shards.bit_length() - 1 - levels
    masks = [1 << low + k for k in range(levels)]
    active = pair_on[me]
    place = positive.reshape(rows, 1)

    first = rows // 2
    upper = list(reversed(range(1, levels)))
    far_p = [None] * levels
    for k in reversed(range(levels)):
        far_p[k] = exchanged(passages, "dp", masks[k])
    part = 5 * rows // 6
    far_upper = exchanged(queries[:part], "dp", masks[0])
    far_q = joined(far_upper, exchanged(queries[part:], "dp", masks[0]))
    head = held_until(rows_after(queries, 0, first, []), [far_upper])
    heads = [exchanged(head, "dp", masks[k]) for k in upper]

    early = partial_tiles(queries, [passages, far_p[0]])
    early_other = exchanged(early, "sub", 1)
    late = [
        partial_tiles(queries, [block], [early_other])
        for block in [far_p[k] for k in upper]
    ]
    late_parts = []
    for part in late:
        late_parts += [part, exchanged(part, "sub", 1)]
    (near,) = partial_rows(passages, [far_q])
    near = [near, exchanged(near, "sub", 1)]
    tiles, row_lse, pack = call(
        functools.partial(stats_kernel, levels, [0, 1] + [k + 1 for k in upper], 1),
        (f32(levels + 1, rows, rows), f32(rows, 1), f32(8, rows)),
        [
            active,
            early, early_other,
            *late_parts,
            place,
            near[1],
        ],
        scalars=1,
        unread=1,
    )

    group = 1 << levels
    packs = [None] * group
    packs[0] = pack
    for member in range(3, group, 2):
        offset = sum(masks[k] for k in range(levels) if member >> k & 1)
        packs[member] = exchanged(pack, "dp", offset)
    come = [packs[member | (member > 1)] for member in range(0, group, 2)]
    tails = [
        exchanged(rows_after(queries, first, rows - first, [pack, piece]), "dp", masks[k])
        for k, piece in zip(upper, heads)
    ]
    bundle = call(
        functools.partial(stack_kernel, len(come)),
        f32(len(come), *pack.shape),
        come,
    )
    swapped = exchanged(bundle, "dp", masks[0])
    for n in range(group // 2):
        packs[2 * n if n else 1] = swapped[n]

    grads, back, col_lse, far_lse, total = call(
        functools.partial(grads_kernel, levels),
        (
            bf16(levels + 1, rows, rows),
            bf16(rows, rows),
            f32(8, rows),
            f32(rows, 8),
            f32(8, 128),
        ),
        [active, tiles, row_lse, place, *packs],
        scalars=1,
        flops=5405000000,
    )
    total = total[0, :1]
    for bit in range(low):
        total = total + exchanged(total, "dp", 1 << bit)
    loss = total / (2.0 * rows * shards)

    query_grad, token = query_product(grads, [passages, *far_p])

    parts = near
    for part in partial_rows(passages, heads, [bundle]):
        parts += [part, exchanged(part, "sub", 1)]
    passage_grad = passage_product(
        col_lse,
        far_lse,
        [back, queries],
        parts,
        [(0, 0)] + [(k, 0) for k in upper],
        [far_q, *heads],
        last=False,
    )
    ends = []
    for tail in tails:
        (part,) = partial_rows(passages, [tail], ends[-2:-1] or [token, passage_grad, loss])
        ends += [part, exchanged(part, "sub", 1)]
    passage_grad = passage_product(
        col_lse,
        far_lse,
        [passage_grad],
        ends,
        [(k, first) for k in upper],
        tails,
        last=True,
    )
    return (loss, query_grad, passage_grad)


def solution(mesh):
    placed = (P("dp", "sub"), P("dp", "sub"), P("dp", None), P())
    return jax.shard_map(
        local,
        mesh=mesh,
        in_specs=placed,
        out_specs=(P(), P("dp", "sub"), P("dp", "sub")),
        check_vma=False,
    )
```

time: 425 us -> 152 us (0.36)
  blocking collectives: 157 us -> 0 us
  waiting for transfers between devices: 154 us -> 83.9 us
  matrix products: 38.9 us -> 0 us
  Pallas kernels: 0 us -> 34 us
  other arithmetic: 28.7 us -> 0 us
  between operations: 19.8 us -> 3.29 us
  starting transfers between devices: 17.4 us -> 22.6 us
    psum x1 -> x0, blocking collectives: 157 us -> none  [local(): total = lax.psum(local_total, 'dp')]
    ppermute x12 -> x22, waiting for transfers between devices: 134 us -> 83.9 us  [exchanged(): return lax.ppermute(block, axis, [(i, i ^ offset) for i in range(count)])]
    dot_general x12 -> x0, matrix products: 38.9 us -> none  [the longest x4 13.9 us: transposed_product(): lax.dot_general(grad, block, (((0,), (0,)), ((), ())), preferred_element_...]
    pallas_call x0 -> x18, Pallas kernels: none -> 34 us  [the longest x17 34 us: call(): pl.pallas_call(kernel, out_shape=out_shape, compiler_params=pltpu.Compile...]
    psum x1 -> x0, waiting for transfers between devices: 20.3 us -> none  [local(): summed = lax.psum(jnp.stack(partial_tiles), 'sub')]
    add x2 -> x0, other arithmetic: 14.9 us -> none  [the longest x1 8.09 us: local(): query_grad = query_grad + near_term]
    another operation x2 -> x0, other arithmetic: 7.14 us -> none  [the longest x1 3.98 us: local(): received = swapped(jnp.stack([queries, passages]), 'dp', bit)]
    squeeze x3 -> x1, local copies, waits for them, and re-layouts: 7.01 us -> 0.01 us  [local(): packs[2 * n if n else 1] = swapped[n]]
  transfers between devices with their start and end apart: 13 -> 22, of which waited for: 7 -> 10; matrix products, arithmetic and copies ran while one was open for 10% -> 2% of each run, Pallas kernels for 0% -> 20%
where the time goes in v1:
time: 152 us
  waiting for transfers between devices  83.9 us (55%)
  Pallas kernels  34 us (22%)
  starting transfers between devices  22.6 us (15%)
  local copies, waits for them, and re-layouts  7.71 us (5%)
  between operations  3.29 us (2%)
    ppermute x22, waiting for transfers between devices, exchanged(): return lax.ppermute(block, axis, [(i, i ^ offset) for i in range(count)])  83.9 us
    pallas_call x17, Pallas kernels, call(): pl.pallas_call(kernel, out_shape=out_shape, compiler_params=pltpu.Compile...  34 us
    ppermute x22, starting transfers between devices, exchanged(): return lax.ppermute(block, axis, [(i, i ^ offset) for i in range(count)])  22.6 us
    unnamed x24, local copies, waits for them, and re-layouts  4.68 us
  transfers between devices with their start and end apart: 22, of which 10 were waited for; matrix products, arithmetic and copies ran while one was open for 2% of the time, Pallas kernels for 20%

profile of v1, /device:TPU:0, one launch (start us, length us, event | category | flops | bytes accessed | tf_op | source)
XLA Modules:
  0.0 151.5 jit_solution(12895125820534580184)
XLA Ops:
  0.7 3.0 %collective-permute-start = (bf16[384,2048]{1,0:T(8,128)(2,1)}, bf16[384,2048]{1,0:T(8,128)(2,1)S(1)}, u32[]{:S(2)}, u32[]{:S(2)}) collective-permute-start(bf16[384,2048]{1,0:T(8,128)(2,1)} %right_ref.7), channel_id=1, source_target_pairs={{0,4},{2,6},{4,0},{6,2},{8,12},{10,14},{12,8},{14,10},{16,20},{18,... | collective-permute-start | bytes 4718600 | tf_op jit(solution)/shard_map/ppermute | solution.py:17
  3.7 2.6 %collective-permute-start.2 = (bf16[384,2048]{1,0:T(8,128)(2,1)}, bf16[384,2048]{1,0:T(8,128)(2,1)}, u32[]{:S(2)}, u32[]{:S(2)}) collective-permute-start(bf16[384,2048]{1,0:T(8,128)(2,1)} %right_ref.7), channel_id=1, source_target_pairs={{0,16},{2,18},{4,20},{6,22},{8,24},{10,26},{12,28},{14,30},{16,0},... | collective-permute-start | bytes 4718600 | tf_op jit(solution)/shard_map/ppermute | solution.py:17
  6.3 1.6 %collective-permute-start.4 = (bf16[384,2048]{1,0:T(8,128)(2,1)}, bf16[384,2048]{1,0:T(8,128)(2,1)}, u32[]{:S(2)}, u32[]{:S(2)}) collective-permute-start(bf16[384,2048]{1,0:T(8,128)(2,1)} %right_ref.7), channel_id=1, source_target_pairs={{0,8},{2,10},{4,12},{6,14},{8,0},{10,2},{12,4},{14,6},{16,24},{18,... | collective-permute-start | bytes 4718600 | tf_op jit(solution)/shard_map/ppermute | solution.py:17
  7.9 1.4 slice.21
  9.3 0.6 collective-permute-start.6
  9.9 29.2 %collective-permute-done.refs_1_ = bf16[384,2048]{1,0:T(8,128)(2,1)S(1)} collective-permute-done((bf16[384,2048]{1,0:T(8,128)(2,1)}, bf16[384,2048]{1,0:T(8,128)(2,1)S(1)}, u32[]{:S(2)}, u32[]{:S(2)}) %collective-permute-start) | collective-permute-done | bytes 1572896 | tf_op jit(solution)/shard_map/ppermute | solution.py:17
  39.1 1.4 copy-done.2
  40.5 2.8 %shard_map.67.refs_0_ = f32[2,384,384]{2,1,0:T(8,128)} custom-call(bf16[384,2048]{1,0:T(8,128)(2,1)S(1)} %copy-done.1, bf16[384,2048]{1,0:T(8,128)(2,1)S(1)} %copy-done.2, bf16[384,2048]{1,0:T(8,128)(2,1)S(1)} %collective-permute-done.refs_1_), custom_call_target="tpu_custom_call" | custom-call | tf_op jit(solution)/shard_map/pallas_call | solution.py:32
  43.4 0.7 slice.22
  44.1 2.1 %collective-permute-start.7 = (bf16[64,2048]{1,0:T(8,128)(2,1)}, bf16[64,2048]{1,0:T(8,128)(2,1)S(1)}, u32[]{:S(2)}, u32[]{:S(2)}) collective-permute-start(bf16[64,2048]{1,0:T(8,128)(2,1)} %slice.22), channel_id=1, source_target_pairs={{0,4},{2,6},{4,0},{6,2},{8,12},{10,14},{12,8},{14,10},{16,20},{18,... | collective-permute-start | bytes 786440 | tf_op jit(solution)/shard_map/ppermute | solution.py:17
  46.2 0.9 copy-done.10
  47.1 20.1 %collective-permute-done.6.upper_ref.refs_1_ = bf16[320,2048]{1,0:T(8,128)(2,1)S(1)} collective-permute-done((bf16[320,2048]{1,0:T(8,128)(2,1)S(1)}, bf16[320,2048]{1,0:T(8,128)(2,1)S(1)}, u32[]{:S(2)}, u32[]{:S(2)}) %collective-permute-start.6) | collective-permute-done | bytes 1310752 | tf_op jit(solution)/shard_map/ppermute | solution.py:17
  67.2 1.1 copy-done.8
  68.3 3.1 %collective-permute-start.14 = (bf16[192,2048]{1,0:T(8,128)(2,1)}, bf16[192,2048]{1,0:T(8,128)(2,1)}, u32[]{:S(2)}, u32[]{:S(2)}) collective-permute-start(bf16[192,2048]{1,0:T(8,128)(2,1)} %shard_map.77), channel_id=1, source_target_pairs={{0,16},{2,18},{4,20},{6,22},{8,24},{10,26},{12,28},{14,30},{16,0},... | collective-permute-start | bytes 2359304 | tf_op jit(solution)/shard_map/ppermute | solution.py:17
  71.4 0.6 collective-permute-done.7.lower_ref
  72.0 1.8 %collective-permute-start.16 = (bf16[192,2048]{1,0:T(8,128)(2,1)}, bf16[192,2048]{1,0:T(8,128)(2,1)}, u32[]{:S(2)}, u32[]{:S(2)}) collective-permute-start(bf16[192,2048]{1,0:T(8,128)(2,1)} %shard_map.77), channel_id=1, source_target_pairs={{0,8},{2,10},{4,12},{6,14},{8,0},{10,2},{12,4},{14,6},{16,24},{18,... | collective-permute-start | bytes 2359304 | tf_op jit(solution)/shard_map/ppermute | solution.py:17
  73.8 1.3 copy-done.9
  75.1 0.1 shard_map.70.refs_0_.refs_8_
  75.2 1.8 %shard_map.71.refs_0_ = f32[384,384]{1,0:T(8,128)} custom-call(bf16[384,2048]{1,0:T(8,128)(2,1)S(1)} %copy-done.3, bf16[384,2048]{1,0:T(8,128)(2,1)S(1)} %shard_map.70.refs_0_.refs_8_), custom_call_target="tpu_custom_call" | custom-call | tf_op jit(solution)/shard_map/pallas_call | solution.py:32
  77.1 14.2 %collective-permute-done.2.refs_0_.refs_3_ = bf16[384,2048]{1,0:T(8,128)(2,1)} collective-permute-done((bf16[384,2048]{1,0:T(8,128)(2,1)}, bf16[384,2048]{1,0:T(8,128)(2,1)}, u32[]{:S(2)}, u32[]{:S(2)}) %collective-permute-start.2) | collective-permute-done | bytes 1572896 | tf_op jit(solution)/shard_map/ppermute | solution.py:17
  91.2 3.2 %shard_map.68.refs_2_ = f32[1,384,384]{2,1,0:T(8,128)} custom-call(bf16[384,2048]{1,0:T(8,128)(2,1)S(1)} %copy-done.1, bf16[384,2048]{1,0:T(8,128)(2,1)} %collective-permute-done.2.refs_0_.refs_3_, f32[2,384,384]{2,1,0:T(8,128)} %collective-permute-done.1.refs_1_), custom_call_target="tpu_custom_call" | custom-call | tf_op jit(solution)/shard_map/pallas_call | solution.py:32
  94.5 0.5 collective-permute-start.3
  95.0 3.2 %shard_map.69.refs_4_ = f32[1,384,384]{2,1,0:T(8,128)} custom-call(bf16[384,2048]{1,0:T(8,128)(2,1)S(1)} %copy-done.1, bf16[384,2048]{1,0:T(8,128)(2,1)} %collective-permute-done.4.refs_0_.refs_2_, f32[2,384,384]{2,1,0:T(8,128)} %collective-permute-done.1.refs_1_), custom_call_target="tpu_custom_call" | custom-call | tf_op jit(solution)/shard_map/pallas_call | solution.py:32
  98.2 0.1 copy.8.refs_6_.pos_ref
  98.4 0.2 dynamic-slice_reduce_fusion.act_ref
  98.6 2.0 %collective-permute-done.5.refs_5_ = f32[1,384,384]{2,1,0:T(8,128)} collective-permute-done((f32[1,384,384]{2,1,0:T(8,128)}, f32[1,384,384]{2,1,0:T(8,128)}, u32[]{:S(2)}, u32[]{:S(2)}) %collective-permute-start.5) | collective-permute-done | bytes 589856 | tf_op jit(solution)/shard_map/ppermute | solution.py:17
  100.6 3.7 %shard_map.72 = (f32[4,384,384]{2,1,0:T(8,128)S(1)}, f32[384,1]{1,0:T(8,128)S(1)}, f32[8,384]{1,0:T(8,128)S(1)}) custom-call(s32[3]{0:T(128)S(1)} %dynamic-slice_reduce_fusion.act_ref, f32[2,384,384]{2,1,0:T(8,128)} %shard_map.67.refs_0_, f32[2,384,384]{2,1,0:T(8,128)} %collective-permute-done.1.refs_1_, f32[1,384,384]{2,1,0:T(8,128)} %shard_map.68.refs_2_, ...), custom_call_target="tpu_custom_call" | custom-call | tf_op jit(solution)/shard_map/pallas_call | solution.py:32
  104.2 0.1 collective-permute-start.10
  104.4 0.1 collective-permute-start.9
  104.5 4.3 %collective-permute-done.14.refs_1_.refs_0_.refs_9_ = bf16[192,2048]{1,0:T(8,128)(2,1)} collective-permute-done((bf16[192,2048]{1,0:T(8,128)(2,1)}, bf16[192,2048]{1,0:T(8,128)(2,1)}, u32[]{:S(2)}, u32[]{:S(2)}) %collective-permute-start.14) | collective-permute-done | bytes 786464 | tf_op jit(solution)/shard_map/ppermute | solution.py:17
  108.9 0.9 collective-permute-start.15
  109.8 3.1 %collective-permute-start.20 = (bf16[192,2048]{1,0:T(8,128)(2,1)S(1)}, bf16[192,2048]{1,0:T(8,128)(2,1)S(1)}, u32[]{:S(2)}, u32[]{:S(2)}) collective-permute-start(bf16[192,2048]{1,0:T(8,128)(2,1)S(1)} %shard_map.82), channel_id=1, source_target_pairs={{0,8},{2,10},{4,12},{6,14},{8,0},{10,2},{12,4},{14,6},{16,24},{18,... | collective-permute-start | bytes 2359304 | tf_op jit(solution)/shard_map/ppermute | solution.py:17
  112.9 0.5 collective-permute-start.12
  113.5 2.5 %shard_map.79 = (f32[192,384]{1,0:T(8,128)S(1)}, f32[192,384]{1,0:T(8,128)S(1)}) custom-call(bf16[384,2048]{1,0:T(8,128)(2,1)S(1)} %copy-done.3, bf16[192,2048]{1,0:T(8,128)(2,1)} %collective-permute-done.14.refs_1_.refs_0_.refs_9_, bf16[192,2048]{1,0:T(8,128)(2,1)} %collective-permute-done.16.refs_1_.refs_10_, f32[4,8,384]{2,1,0:T(8,128)S(1)} %shard_map.73.refs_2_), custom_call_target="tpu_custom_call" | custom-call | tf_op jit(solution)/shard_map/pallas_call | solution.py:32
  116.1 0.5 collective-permute-start.18
  116.6 0.5 collective-permute-done.12
  117.1 1.6 %shard_map.74 = (bf16[4,384,384]{2,1,0:T(8,128)(2,1)S(1)}, bf16[384,384]{1,0:T(8,128)(2,1)S(1)}, f32[8,384]{1,0:T(8,128)S(1)}, f32[384,8]{1,0:T(8,128)S(1)}, f32[8,128]{1,0:T(8,128)S(1)}) custom-call(s32[3]{0:T(128)S(1)} %dynamic-slice_reduce_fusion.act_ref, f32[4,384,384]{2,1,0:T(8,128)S(1)} %get-tuple-element.15.tile_ref, ...), custom_call_target="tpu_custom_call" | custom-call | flops 5405000192 | tf_op jit(solution)/shard_map/pallas_call | solution.py:32
  118.7 0.5 slice.27
  119.3 1.5 collective-permute-start.13
  120.8 6.3 %shard_map.75 = (f32[384,2048]{1,0:T(8,128)}, f32[8,128]{1,0:T(8,128)S(1)}) custom-call(bf16[4,384,384]{2,1,0:T(8,128)(2,1)S(1)} %get-tuple-element.19.grad_ref, bf16[384,2048]{1,0:T(8,128)(2,1)S(1)} %copy-done.3, bf16[384,2048]{1,0:T(8,128)(2,1)S(1)} %copy-done.7, bf16[384,2048]{1,0:T(8,128)(2,1)} %collective-permute-done.4.refs_0_.refs_2_, ...), custom_call_target="tpu_custom_call" | custom-call | tf_op jit(solution)/shard_map/pallas_call | solution.py:32
  128.4 4.8 %shard_map.80.refs_2_.refs_4_ = f32[384,2048]{1,0:T(8,128)S(1)} custom-call(f32[8,384]{1,0:T(8,128)S(1)} %get-tuple-element.21.col_ref, f32[384,8]{1,0:T(8,128)S(1)} %get-tuple-element.22.far_ref, f32[384,384]{1,0:T(8,128)} %shard_map.71.refs_0_, f32[384,384]{1,0:T(8,128)} %collective-permute-done.8.refs_7_.refs_1_, ...), custom_call_target="tpu_custom_call" | custom-call | tf_op jit(solution)/shard_map/pallas_call | solution.py:32
  133.2 11.4 %collective-permute-done.15.refs_0_.refs_5_ = bf16[192,2048]{1,0:T(8,128)(2,1)S(1)} collective-permute-done((bf16[192,2048]{1,0:T(8,128)(2,1)S(1)}, bf16[192,2048]{1,0:T(8,128)(2,1)S(1)}, u32[]{:S(2)}, u32[]{:S(2)}) %collective-permute-start.15) | collective-permute-done | bytes 786464 | tf_op jit(solution)/shard_map/ppermute | solution.py:17
  144.6 0.7 shard_map.81.refs_1_.refs_0_
  145.3 0.7 shard_map.83.refs_2_
  146.1 0.5 collective-permute-start.19
  146.6 1.1 collective-permute-done.21.refs_3_
  147.7 0.4 collective-permute-done.19.refs_1_
  148.1 2.3 %shard_map.84 = f32[384,2048]{1,0:T(8,128)} custom-call(f32[8,384]{1,0:T(8,128)S(1)} %get-tuple-element.21.col_ref, f32[384,8]{1,0:T(8,128)S(1)} %get-tuple-element.22.far_ref, f32[192,384]{1,0:T(8,128)S(1)} %shard_map.81.refs_1_.refs_0_, f32[192,384]{1,0:T(8,128)S(1)} %collective-permute-done.19.refs_1_, f32[192,384]{1,0:T(8,128)S(1)} %shard_map.83.refs_2_, ...), custom_call_target="tpu_custom_call" | custom-call | tf_op jit(solution)/shard_map/pallas_call | solution.py:32
  (44 shorter events, 0.5 us)
Async XLA Ops:
  0.6 97.7 %copy-start = (s32[16,3]{0,1:T(4,128)S(1)}, s32[16,3]{0,1:T(4,128)}, u32[]{:S(2)}) copy-start(s32[16,3]{0,1:T(4,128)} %param.7) | copy-start | bytes 580
  0.6 38.5 %copy-start.1 = (bf16[384,2048]{1,0:T(8,128)(2,1)S(1)}, bf16[384,2048]{1,0:T(8,128)(2,1)}, u32[]{:S(2)}) copy-start(bf16[384,2048]{1,0:T(8,128)(2,1)} %array_ref.5) | copy-start | bytes 4718596
  0.7 38.5 %collective-permute-start = (bf16[384,2048]{1,0:T(8,128)(2,1)}, bf16[384,2048]{1,0:T(8,128)(2,1)S(1)}, u32[]{:S(2)}, u32[]{:S(2)}) collective-permute-start(bf16[384,2048]{1,0:T(8,128)(2,1)} %right_ref.7), channel_id=1, source_target_pairs={{0,4},{2,6},{4,0},{6,2},{8,12},{10,14},{12,8},{14,10},{16,20},{18,... | collective-permute-start | bytes 4718600 | tf_op jit(solution)/shard_map/ppermute | solution.py:17
  3.7 87.6 %collective-permute-start.2 = (bf16[384,2048]{1,0:T(8,128)(2,1)}, bf16[384,2048]{1,0:T(8,128)(2,1)}, u32[]{:S(2)}, u32[]{:S(2)}) collective-permute-start(bf16[384,2048]{1,0:T(8,128)(2,1)} %right_ref.7), channel_id=1, source_target_pairs={{0,16},{2,18},{4,20},{6,22},{8,24},{10,26},{12,28},{14,30},{16,0},... | collective-permute-start | bytes 4718600 | tf_op jit(solution)/shard_map/ppermute | solution.py:17
  6.3 88.7 %collective-permute-start.4 = (bf16[384,2048]{1,0:T(8,128)(2,1)}, bf16[384,2048]{1,0:T(8,128)(2,1)}, u32[]{:S(2)}, u32[]{:S(2)}) collective-permute-start(bf16[384,2048]{1,0:T(8,128)(2,1)} %right_ref.7), channel_id=1, source_target_pairs={{0,8},{2,10},{4,12},{6,14},{8,0},{10,2},{12,4},{14,6},{16,24},{18,... | collective-permute-start | bytes 4718600 | tf_op jit(solution)/shard_map/ppermute | solution.py:17
  9.3 57.9 %collective-permute-start.6 = (bf16[320,2048]{1,0:T(8,128)(2,1)S(1)}, bf16[320,2048]{1,0:T(8,128)(2,1)S(1)}, u32[]{:S(2)}, u32[]{:S(2)}) collective-permute-start(bf16[320,2048]{1,0:T(8,128)(2,1)S(1)} %slice.21), channel_id=1, source_target_pairs={{0,4},{2,6},{4,0},{6,2},{8,12},{10,14},{12,8},{14,10},{16,20},{18,... | collective-permute-start | bytes 3932168 | tf_op jit(solution)/shard_map/ppermute | solution.py:17
  39.1 1.4 copy-start.2
  40.5 2.8 %copy-start.6 = (bf16[384,2048]{1,0:T(8,128)(2,1)}, bf16[384,2048]{1,0:T(8,128)(2,1)S(1)}, u32[]{:S(2)}) copy-start(bf16[384,2048]{1,0:T(8,128)(2,1)S(1)} %collective-permute-done.refs_1_) | copy-start | bytes 4718596
  43.4 47.9 %collective-permute-start.1 = (f32[2,384,384]{2,1,0:T(8,128)}, f32[2,384,384]{2,1,0:T(8,128)}, u32[]{:S(2)}, u32[]{:S(2)}) collective-permute-start(f32[2,384,384]{2,1,0:T(8,128)} %shard_map.67.refs_0_), channel_id=1, source_target_pairs={{0,1},{1,0},{2,3},{3,2},{4,5},{5,4},{6,7},{7,6},{8,9},{9,8},{10,11... | collective-permute-start | bytes 3538952 | tf_op jit(solution)/shard_map/ppermute | solution.py:17
  44.1 27.9 %collective-permute-start.7 = (bf16[64,2048]{1,0:T(8,128)(2,1)}, bf16[64,2048]{1,0:T(8,128)(2,1)S(1)}, u32[]{:S(2)}, u32[]{:S(2)}) collective-permute-start(bf16[64,2048]{1,0:T(8,128)(2,1)} %slice.22), channel_id=1, source_target_pairs={{0,4},{2,6},{4,0},{6,2},{8,12},{10,14},{12,8},{14,10},{16,20},{18,... | collective-permute-start | bytes 786440 | tf_op jit(solution)/shard_map/ppermute | solution.py:17
  46.2 0.9 copy-start.10
  67.2 1.1 copy-start.8
  68.3 7.0 %copy-start.3 = (bf16[384,2048]{1,0:T(8,128)(2,1)S(1)}, bf16[384,2048]{1,0:T(8,128)(2,1)}, u32[]{:S(2)}) copy-start(bf16[384,2048]{1,0:T(8,128)(2,1)} %right_ref.7) | copy-start | bytes 4718596
  68.3 40.5 %collective-permute-start.14 = (bf16[192,2048]{1,0:T(8,128)(2,1)}, bf16[192,2048]{1,0:T(8,128)(2,1)}, u32[]{:S(2)}, u32[]{:S(2)}) collective-permute-start(bf16[192,2048]{1,0:T(8,128)(2,1)} %shard_map.77), channel_id=1, source_target_pairs={{0,16},{2,18},{4,20},{6,22},{8,24},{10,26},{12,28},{14,30},{16,0},... | collective-permute-start | bytes 2359304 | tf_op jit(solution)/shard_map/ppermute | solution.py:17
  72.0 37.8 %collective-permute-start.16 = (bf16[192,2048]{1,0:T(8,128)(2,1)}, bf16[192,2048]{1,0:T(8,128)(2,1)}, u32[]{:S(2)}, u32[]{:S(2)}) collective-permute-start(bf16[192,2048]{1,0:T(8,128)(2,1)} %shard_map.77), channel_id=1, source_target_pairs={{0,8},{2,10},{4,12},{6,14},{8,0},{10,2},{12,4},{14,6},{16,24},{18,... | collective-permute-start | bytes 2359304 | tf_op jit(solution)/shard_map/ppermute | solution.py:17
  73.8 1.3 copy-start.9
  75.2 1.8 %copy-start.4 = (bf16[384,2048]{1,0:T(8,128)(2,1)}, bf16[384,2048]{1,0:T(8,128)(2,1)S(1)}, u32[]{:S(2)}) copy-start(bf16[384,2048]{1,0:T(8,128)(2,1)S(1)} %shard_map.70.refs_0_.refs_8_) | copy-start | bytes 4718596
  91.2 7.3 %collective-permute-start.8 = (f32[384,384]{1,0:T(8,128)}, f32[384,384]{1,0:T(8,128)}, u32[]{:S(2)}, u32[]{:S(2)}) collective-permute-start(f32[384,384]{1,0:T(8,128)} %shard_map.71.refs_0_), channel_id=1, source_target_pairs={{0,1},{1,0},{2,3},{3,2},{4,5},{5,4},{6,7},{7,6},{8,9},{9,8},{10,11... | collective-permute-start | bytes 1769480 | tf_op jit(solution)/shard_map/ppermute | solution.py:17
  94.5 3.7 %copy-start.11 = (s32[1,384]{1,0:T(1,128)S(1)}, s32[1,384]{1,0:T(1,128)}, u32[]{:S(2)}) copy-start(s32[1,384]{1,0:T(1,128)} %param.6) | copy-start | bytes 4612
  94.5 4.1 %collective-permute-start.3 = (f32[1,384,384]{2,1,0:T(8,128)}, f32[1,384,384]{2,1,0:T(8,128)}, u32[]{:S(2)}, u32[]{:S(2)}) collective-permute-start(f32[1,384,384]{2,1,0:T(8,128)} %shard_map.68.refs_2_), channel_id=1, source_target_pairs={{0,1},{1,0},{2,3},{3,2},{4,5},{5,4},{6,7},{7,6},{8,9},{9,8},{10,11... | collective-permute-start | bytes 1769480 | tf_op jit(solution)/shard_map/ppermute | solution.py:17
  98.2 2.3 %collective-permute-start.5 = (f32[1,384,384]{2,1,0:T(8,128)}, f32[1,384,384]{2,1,0:T(8,128)}, u32[]{:S(2)}, u32[]{:S(2)}) collective-permute-start(f32[1,384,384]{2,1,0:T(8,128)} %shard_map.69.refs_4_), channel_id=1, source_target_pairs={{0,1},{1,0},{2,3},{3,2},{4,5},{5,4},{6,7},{7,6},{8,9},{9,8},{10,11... | collective-permute-start | bytes 1769480 | tf_op jit(solution)/shard_map/ppermute | solution.py:17
  104.2 8.7 %collective-permute-start.10 = (f32[8,384]{1,0:T(8,128)S(1)}, f32[8,384]{1,0:T(8,128)S(1)}, u32[]{:S(2)}, u32[]{:S(2)}) collective-permute-start(f32[8,384]{1,0:T(8,128)S(1)} %get-tuple-element.17.refs_0_), channel_id=1, source_target_pairs={{0,20},{2,22},{4,16},{6,18},{8,28},{10,30},{12,24},{14,26},{16,4},... | collective-permute-start | bytes 36872 | tf_op jit(solution)/shard_map/ppermute | solution.py:17
  104.3 8.6 %collective-permute-start.11 = (f32[8,384]{1,0:T(8,128)S(1)}, f32[8,384]{1,0:T(8,128)S(1)}, u32[]{:S(2)}, u32[]{:S(2)}) collective-permute-start(f32[8,384]{1,0:T(8,128)S(1)} %get-tuple-element.17.refs_0_), channel_id=1, source_target_pairs={{0,28},{2,30},{4,24},{6,26},{8,20},{10,22},{12,16},{14,18},{16,12}... | collective-permute-start | bytes 36872 | tf_op jit(solution)/shard_map/ppermute | solution.py:17
  104.4 8.5 %collective-permute-start.9 = (f32[8,384]{1,0:T(8,128)S(1)}, f32[8,384]{1,0:T(8,128)S(1)}, u32[]{:S(2)}, u32[]{:S(2)}) collective-permute-start(f32[8,384]{1,0:T(8,128)S(1)} %get-tuple-element.17.refs_0_), channel_id=1, source_target_pairs={{0,12},{2,14},{4,8},{6,10},{8,4},{10,6},{12,0},{14,2},{16,28},{18,... | collective-permute-start | bytes 36872 | tf_op jit(solution)/shard_map/ppermute | solution.py:17
  108.9 35.8 %collective-permute-start.15 = (bf16[192,2048]{1,0:T(8,128)(2,1)S(1)}, bf16[192,2048]{1,0:T(8,128)(2,1)S(1)}, u32[]{:S(2)}, u32[]{:S(2)}) collective-permute-start(bf16[192,2048]{1,0:T(8,128)(2,1)S(1)} %shard_map.78), channel_id=1, source_target_pairs={{0,16},{2,18},{4,20},{6,22},{8,24},{10,26},{12,28},{14,30},{16,0},... | collective-permute-start | bytes 2359304 | tf_op jit(solution)/shard_map/ppermute | solution.py:17
  109.8 35.5 %collective-permute-start.20 = (bf16[192,2048]{1,0:T(8,128)(2,1)S(1)}, bf16[192,2048]{1,0:T(8,128)(2,1)S(1)}, u32[]{:S(2)}, u32[]{:S(2)}) collective-permute-start(bf16[192,2048]{1,0:T(8,128)(2,1)S(1)} %shard_map.82), channel_id=1, source_target_pairs={{0,8},{2,10},{4,12},{6,14},{8,0},{10,2},{12,4},{14,6},{16,24},{18,... | collective-permute-start | bytes 2359304 | tf_op jit(solution)/shard_map/ppermute | solution.py:17
  112.9 4.2 %collective-permute-start.12 = (f32[4,8,384]{2,1,0:T(8,128)S(1)}, f32[4,8,384]{2,1,0:T(8,128)S(1)}, u32[]{:S(2)}, u32[]{:S(2)}) collective-permute-start(f32[4,8,384]{2,1,0:T(8,128)S(1)} %shard_map.73.refs_2_), channel_id=1, source_target_pairs={{0,4},{2,6},{4,0},{6,2},{8,12},{10,14},{12,8},{14,10},{16,20},{18,... | collective-permute-start | bytes 147464 | tf_op jit(solution)/shard_map/ppermute | solution.py:17
  116.0 12.4 %collective-permute-start.17 = (f32[192,384]{1,0:T(8,128)S(1)}, f32[192,384]{1,0:T(8,128)S(1)}, u32[]{:S(2)}, u32[]{:S(2)}) collective-permute-start(f32[192,384]{1,0:T(8,128)S(1)} %get-tuple-element.24.refs_2_), channel_id=1, source_target_pairs={{0,1},{1,0},{2,3},{3,2},{4,5},{5,4},{6,7},{7,6},{8,9},{9,8},{10,11... | collective-permute-start | bytes 884744 | tf_op jit(solution)/shard_map/ppermute | solution.py:17
  116.1 12.3 %collective-permute-start.18 = (f32[192,384]{1,0:T(8,128)S(1)}, f32[192,384]{1,0:T(8,128)S(1)}, u32[]{:S(2)}, u32[]{:S(2)}) collective-permute-start(f32[192,384]{1,0:T(8,128)S(1)} %get-tuple-element.25.refs_4_), channel_id=1, source_target_pairs={{0,1},{1,0},{2,3},{3,2},{4,5},{5,4},{6,7},{7,6},{8,9},{9,8},{10,11... | collective-permute-start | bytes 884744 | tf_op jit(solution)/shard_map/ppermute | solution.py:17
  117.1 3.6 %copy-start.7 = (bf16[384,2048]{1,0:T(8,128)(2,1)S(1)}, bf16[384,2048]{1,0:T(8,128)(2,1)}, u32[]{:S(2)}) copy-start(bf16[384,2048]{1,0:T(8,128)(2,1)} %copy-done.6) | copy-start | bytes 4718596
  119.3 7.8 %collective-permute-start.13 = (f32[1]{0:T(128)}, f32[1]{0:T(128)}, u32[]{:S(2)}, u32[]{:S(2)}) collective-permute-start(f32[1]{0:T(128)} %bitcast.5), channel_id=1, source_target_pairs={{0,2},{2,0},{4,6},{6,4},{8,10},{10,8},{12,14},{14,12},{16,18},{18,... | collective-permute-start | bytes 20 | tf_op jit(solution)/shard_map/ppermute | solution.py:17
  120.8 7.7 %copy-start.5 = (bf16[384,2048]{1,0:T(8,128)(2,1)S(1)}, bf16[384,2048]{1,0:T(8,128)(2,1)}, u32[]{:S(2)}) copy-start(bf16[384,2048]{1,0:T(8,128)(2,1)} %copy-done.4) | copy-start | bytes 4718596
  146.0 1.6 %collective-permute-start.21 = (f32[192,384]{1,0:T(8,128)S(1)}, f32[192,384]{1,0:T(8,128)S(1)}, u32[]{:S(2)}, u32[]{:S(2)}) collective-permute-start(f32[192,384]{1,0:T(8,128)S(1)} %shard_map.83.refs_2_), channel_id=1, source_target_pairs={{0,1},{1,0},{2,3},{3,2},{4,5},{5,4},{6,7},{7,6},{8,9},{9,8},{10,11... | collective-permute-start | bytes 884744 | tf_op jit(solution)/shard_map/ppermute | solution.py:17
  146.1 2.0 %collective-permute-start.19 = (f32[192,384]{1,0:T(8,128)S(1)}, f32[192,384]{1,0:T(8,128)S(1)}, u32[]{:S(2)}, u32[]{:S(2)}) collective-permute-start(f32[192,384]{1,0:T(8,128)S(1)} %shard_map.81.refs_1_.refs_0_), channel_id=1, source_target_pairs={{0,1},{1,0},{2,3},{3,2},{4,5},{5,4},{6,7},{7,6},{8,9},{9,8},{10,11... | collective-permute-start | bytes 884744 | tf_op jit(solution)/shard_map/ppermute | solution.py:17

commit v2 on v1

--- a/solution.py
+++ b/solution.py
@@ -32,7 +32,7 @@
     return pl.pallas_call(
         kernel,
         out_shape=out_shape,
-        compiler_params=pltpu.CompilerParams(vmem_limit_bytes=20 * 1024 * 1024),
+        compiler_params=pltpu.CompilerParams(vmem_limit_bytes=12 * 1024 * 1024),
         cost_estimate=pl.CostEstimate(flops=flops, bytes_accessed=0, transcendentals=0),
         **kwargs,
     )(*operands)
@@ -60,6 +60,25 @@
     return call(
         functools.partial(rows_kernel, len(blocks)),
         [f32(block.shape[0], right.shape[0]) for block in blocks],
+        [right, *blocks, *after],
+        unread=len(after),
+    )
+
+
+def stacked_rows_kernel(count, right_ref, *refs):
+    for n in range(count):
+        refs[-1][n] = lax.dot_general(
+            refs[n][...],
+            right_ref[...],
+            (((1,), (1,)), ((), ())),
+            preferred_element_type=jnp.float32,
+        )
+
+
+def partial_stack(right, blocks, after):
+    return call(
+        functools.partial(stacked_rows_kernel, len(blocks)),
+        f32(len(blocks), blocks[0].shape[0], right.shape[0]),
         [right, *blocks, *after],
         unread=len(after),
     )
@@ -270,7 +289,11 @@
 
 def passage_kernel(pieces, last, col_ref, far_ref, *refs):
     count = len(pieces)
-    parts, refs = refs[: 2 * count], refs[2 * count :]
+    if last:
+        stacks, refs = refs[:2], refs[2:]
+        parts = [stack.at[n] for n in range(count) for stack in stacks]
+    else:
+        parts, refs = refs[: 2 * count], refs[2 * count :]
     heads = 1 if last else 2
     head, blocks = refs[:heads], refs[heads : heads + count]
     out_ref, *scratch = refs[heads + count :]
@@ -325,7 +348,7 @@
     active = pair_on[me]
     place = positive.reshape(rows, 1)
 
-    first = rows // 2
+    first = 13 * rows // 24
     upper = list(reversed(range(1, levels)))
     far_p = [None] * levels
     for k in reversed(range(levels)):
@@ -392,7 +415,7 @@
         ),
         [active, tiles, row_lse, place, *packs],
         scalars=1,
-        flops=5405000000,
+        flops=4715000000,
     )
     total = total[0, :1]
     for bit in range(low):
@@ -413,15 +436,12 @@
         [far_q, *heads],
         last=False,
     )
-    ends = []
-    for tail in tails:
-        (part,) = partial_rows(passages, [tail], ends[-2:-1] or [token, passage_grad, loss])
-        ends += [part, exchanged(part, "sub", 1)]
+    end = partial_stack(passages, tails, [token, passage_grad, loss])
     passage_grad = passage_product(
         col_lse,
         far_lse,
         [passage_grad],
-        ends,
+        [end, exchanged(end, "sub", 1)],
         [(k, first) for k in upper],
         tails,
         last=True,

time: 152 us -> 152 us (level)
    ppermute x22 -> x21, waiting for transfers between devices: 83.9 us -> 84.5 us  [exchanged(): return lax.ppermute(block, axis, [(i, i ^ offset) for i in range(count)])]
    ppermute x22 -> x21, starting transfers between devices: 22.6 us -> 22.1 us  [exchanged(): return lax.ppermute(block, axis, [(i, i ^ offset) for i in range(count)])]
    pallas_call x17 -> x16, Pallas kernels: 34 us -> 33.8 us  [call(): pl.pallas_call(kernel, out_shape=out_shape, compiler_params=pltpu.Compile...]
  transfers between devices with their start and end apart: 22 -> 21, of which waited for: 10 -> 10; matrix products, arithmetic and copies ran while one was open for 2% -> 2% of each run, Pallas kernels for 20% -> 20%
where the time goes in v2:
time: 152 us; the launch traced here: 151 us
  waiting for transfers between devices  84.5 us (56%)
  Pallas kernels  33.8 us (22%)
  starting transfers between devices  22.1 us (15%)
  local copies, waits for them, and re-layouts  7.75 us (5%)
  between operations  3.3 us (2%)
    ppermute x21, waiting for transfers between devices, exchanged(): return lax.ppermute(block, axis, [(i, i ^ offset) for i in range(count)])  84.5 us
    pallas_call x16, Pallas kernels, call(): pl.pallas_call(kernel, out_shape=out_shape, compiler_params=pltpu.Compile...  33.8 us
    ppermute x21, starting transfers between devices, exchanged(): return lax.ppermute(block, axis, [(i, i ^ offset) for i in range(count)])  22.1 us
    unnamed x24, local copies, waits for them, and re-layouts  4.71 us
  transfers between devices with their start and end apart: 21, of which 10 were waited for; matrix products, arithmetic and copies ran while one was open for 2% of the time, Pallas kernels for 20%

profile of v2, /device:TPU:0, one launch (start us, length us, event | category | flops | bytes accessed | tf_op | source)
XLA Modules:
  0.0 151.4 jit_solution(3151586214403922158)
XLA Ops:
  0.7 3.0 %collective-permute-start = (bf16[384,2048]{1,0:T(8,128)(2,1)}, bf16[384,2048]{1,0:T(8,128)(2,1)S(1)}, u32[]{:S(2)}, u32[]{:S(2)}) collective-permute-start(bf16[384,2048]{1,0:T(8,128)(2,1)} %right_ref.5), channel_id=1, source_target_pairs={{0,4},{2,6},{4,0},{6,2},{8,12},{10,14},{12,8},{14,10},{16,20},{18,... | collective-permute-start | bytes 4718600 | tf_op jit(solution)/shard_map/ppermute | solution.py:17
  3.7 2.6 %collective-permute-start.2 = (bf16[384,2048]{1,0:T(8,128)(2,1)}, bf16[384,2048]{1,0:T(8,128)(2,1)}, u32[]{:S(2)}, u32[]{:S(2)}) collective-permute-start(bf16[384,2048]{1,0:T(8,128)(2,1)} %right_ref.5), channel_id=1, source_target_pairs={{0,16},{2,18},{4,20},{6,22},{8,24},{10,26},{12,28},{14,30},{16,0},... | collective-permute-start | bytes 4718600 | tf_op jit(solution)/shard_map/ppermute | solution.py:17
  6.3 1.6 %collective-permute-start.4 = (bf16[384,2048]{1,0:T(8,128)(2,1)}, bf16[384,2048]{1,0:T(8,128)(2,1)}, u32[]{:S(2)}, u32[]{:S(2)}) collective-permute-start(bf16[384,2048]{1,0:T(8,128)(2,1)} %right_ref.5), channel_id=1, source_target_pairs={{0,8},{2,10},{4,12},{6,14},{8,0},{10,2},{12,4},{14,6},{16,24},{18,... | collective-permute-start | bytes 4718600 | tf_op jit(solution)/shard_map/ppermute | solution.py:17
  7.9 1.4 slice.21
  9.3 0.6 collective-permute-start.6
  9.9 29.2 %collective-permute-done.refs_1_ = bf16[384,2048]{1,0:T(8,128)(2,1)S(1)} collective-permute-done((bf16[384,2048]{1,0:T(8,128)(2,1)}, bf16[384,2048]{1,0:T(8,128)(2,1)S(1)}, u32[]{:S(2)}, u32[]{:S(2)}) %collective-permute-start) | collective-permute-done | bytes 1572896 | tf_op jit(solution)/shard_map/ppermute | solution.py:17
  39.1 1.4 copy-done.2
  40.5 2.8 %shard_map.67.refs_0_ = f32[2,384,384]{2,1,0:T(8,128)} custom-call(bf16[384,2048]{1,0:T(8,128)(2,1)S(1)} %copy-done.1, bf16[384,2048]{1,0:T(8,128)(2,1)S(1)} %copy-done.2, bf16[384,2048]{1,0:T(8,128)(2,1)S(1)} %collective-permute-done.refs_1_), custom_call_target="tpu_custom_call" | custom-call | tf_op jit(solution)/shard_map/pallas_call | solution.py:32
  43.4 0.7 slice.22
  44.1 2.1 %collective-permute-start.7 = (bf16[64,2048]{1,0:T(8,128)(2,1)}, bf16[64,2048]{1,0:T(8,128)(2,1)S(1)}, u32[]{:S(2)}, u32[]{:S(2)}) collective-permute-start(bf16[64,2048]{1,0:T(8,128)(2,1)} %slice.22), channel_id=1, source_target_pairs={{0,4},{2,6},{4,0},{6,2},{8,12},{10,14},{12,8},{14,10},{16,20},{18,... | collective-permute-start | bytes 786440 | tf_op jit(solution)/shard_map/ppermute | solution.py:17
  46.3 0.9 copy-done.10
  47.1 20.1 %collective-permute-done.6.upper_ref.refs_1_ = bf16[320,2048]{1,0:T(8,128)(2,1)S(1)} collective-permute-done((bf16[320,2048]{1,0:T(8,128)(2,1)S(1)}, bf16[320,2048]{1,0:T(8,128)(2,1)S(1)}, u32[]{:S(2)}, u32[]{:S(2)}) %collective-permute-start.6) | collective-permute-done | bytes 1310752 | tf_op jit(solution)/shard_map/ppermute | solution.py:17
  67.2 1.1 copy-done.8
  68.3 3.1 %collective-permute-start.14 = (bf16[208,2048]{1,0:T(8,128)(2,1)}, bf16[208,2048]{1,0:T(8,128)(2,1)}, u32[]{:S(2)}, u32[]{:S(2)}) collective-permute-start(bf16[208,2048]{1,0:T(8,128)(2,1)} %shard_map.77), channel_id=1, source_target_pairs={{0,16},{2,18},{4,20},{6,22},{8,24},{10,26},{12,28},{14,30},{16,0},... | collective-permute-start | bytes 2555912 | tf_op jit(solution)/shard_map/ppermute | solution.py:17
  71.4 0.6 collective-permute-done.7.lower_ref
  72.0 1.8 %collective-permute-start.16 = (bf16[208,2048]{1,0:T(8,128)(2,1)}, bf16[208,2048]{1,0:T(8,128)(2,1)}, u32[]{:S(2)}, u32[]{:S(2)}) collective-permute-start(bf16[208,2048]{1,0:T(8,128)(2,1)} %shard_map.77), channel_id=1, source_target_pairs={{0,8},{2,10},{4,12},{6,14},{8,0},{10,2},{12,4},{14,6},{16,24},{18,... | collective-permute-start | bytes 2555912 | tf_op jit(solution)/shard_map/ppermute | solution.py:17
  73.8 1.3 copy-done.9
  75.1 0.1 shard_map.70.refs_0_.refs_8_
  75.2 1.8 %shard_map.71.refs_0_ = f32[384,384]{1,0:T(8,128)} custom-call(bf16[384,2048]{1,0:T(8,128)(2,1)S(1)} %copy-done.3, bf16[384,2048]{1,0:T(8,128)(2,1)S(1)} %shard_map.70.refs_0_.refs_8_), custom_call_target="tpu_custom_call" | custom-call | tf_op jit(solution)/shard_map/pallas_call | solution.py:32
  77.1 15.6 %collective-permute-done.2.refs_0_.refs_3_ = bf16[384,2048]{1,0:T(8,128)(2,1)} collective-permute-done((bf16[384,2048]{1,0:T(8,128)(2,1)}, bf16[384,2048]{1,0:T(8,128)(2,1)}, u32[]{:S(2)}, u32[]{:S(2)}) %collective-permute-start.2) | collective-permute-done | bytes 1572896 | tf_op jit(solution)/shard_map/ppermute | solution.py:17
  92.7 3.2 %shard_map.68.refs_2_ = f32[1,384,384]{2,1,0:T(8,128)} custom-call(bf16[384,2048]{1,0:T(8,128)(2,1)S(1)} %copy-done.1, bf16[384,2048]{1,0:T(8,128)(2,1)} %collective-permute-done.2.refs_0_.refs_3_, f32[2,384,384]{2,1,0:T(8,128)} %collective-permute-done.1.refs_1_), custom_call_target="tpu_custom_call" | custom-call | tf_op jit(solution)/shard_map/pallas_call | solution.py:32
  95.9 0.5 collective-permute-start.3
  96.4 3.2 %shard_map.69.refs_4_ = f32[1,384,384]{2,1,0:T(8,128)} custom-call(bf16[384,2048]{1,0:T(8,128)(2,1)S(1)} %copy-done.1, bf16[384,2048]{1,0:T(8,128)(2,1)} %collective-permute-done.4.refs_0_.refs_2_, f32[2,384,384]{2,1,0:T(8,128)} %collective-permute-done.1.refs_1_), custom_call_target="tpu_custom_call" | custom-call | tf_op jit(solution)/shard_map/pallas_call | solution.py:32
  99.6 0.1 copy.8.refs_6_.pos_ref
  99.8 0.2 dynamic-slice_reduce_fusion.act_ref
  100.0 2.0 %collective-permute-done.5.refs_5_ = f32[1,384,384]{2,1,0:T(8,128)} collective-permute-done((f32[1,384,384]{2,1,0:T(8,128)}, f32[1,384,384]{2,1,0:T(8,128)}, u32[]{:S(2)}, u32[]{:S(2)}) %collective-permute-start.5) | collective-permute-done | bytes 589856 | tf_op jit(solution)/shard_map/ppermute | solution.py:17
  102.0 3.7 %shard_map.72 = (f32[4,384,384]{2,1,0:T(8,128)S(1)}, f32[384,1]{1,0:T(8,128)S(1)}, f32[8,384]{1,0:T(8,128)S(1)}) custom-call(s32[3]{0:T(128)S(1)} %dynamic-slice_reduce_fusion.act_ref, f32[2,384,384]{2,1,0:T(8,128)} %shard_map.67.refs_0_, f32[2,384,384]{2,1,0:T(8,128)} %collective-permute-done.1.refs_1_, f32[1,384,384]{2,1,0:T(8,128)} %shard_map.68.refs_2_, ...), custom_call_target="tpu_custom_call" | custom-call | tf_op jit(solution)/shard_map/pallas_call | solution.py:32
  105.7 0.1 collective-permute-start.10
  105.9 0.1 collective-permute-start.9
  105.9 5.7 %collective-permute-done.14.refs_1_.refs_0_.refs_9_ = bf16[208,2048]{1,0:T(8,128)(2,1)} collective-permute-done((bf16[208,2048]{1,0:T(8,128)(2,1)}, bf16[208,2048]{1,0:T(8,128)(2,1)}, u32[]{:S(2)}, u32[]{:S(2)}) %collective-permute-start.14) | collective-permute-done | bytes 852000 | tf_op jit(solution)/shard_map/ppermute | solution.py:17
  111.7 0.1 collective-permute-start.15
  111.8 3.9 %collective-permute-start.17 = (bf16[176,2048]{1,0:T(8,128)(2,1)S(1)}, bf16[176,2048]{1,0:T(8,128)(2,1)S(1)}, u32[]{:S(2)}, u32[]{:S(2)}) collective-permute-start(bf16[176,2048]{1,0:T(8,128)(2,1)S(1)} %shard_map.79), channel_id=1, source_target_pairs={{0,8},{2,10},{4,12},{6,14},{8,0},{10,2},{12,4},{14,6},{16,24},{18,... | collective-permute-start | bytes 2162696 | tf_op jit(solution)/shard_map/ppermute | solution.py:17
  115.7 0.6 collective-permute-start.12
  116.3 2.6 %shard_map.80 = (f32[208,384]{1,0:T(8,128)S(1)}, f32[208,384]{1,0:T(8,128)S(1)}) custom-call(bf16[384,2048]{1,0:T(8,128)(2,1)S(1)} %copy-done.3, bf16[208,2048]{1,0:T(8,128)(2,1)} %collective-permute-done.14.refs_1_.refs_0_.refs_9_, bf16[208,2048]{1,0:T(8,128)(2,1)} %collective-permute-done.16.refs_1_.refs_10_, f32[4,8,384]{2,1,0:T(8,128)S(1)} %shard_map.73.refs_2_), custom_call_target="tpu_custom_call" | custom-call | tf_op jit(solution)/shard_map/pallas_call | solution.py:32
  118.9 0.1 collective-permute-start.18
  118.9 0.5 collective-permute-start.19
  119.4 0.4 collective-permute-done.12
  119.9 1.6 %shard_map.74 = (bf16[4,384,384]{2,1,0:T(8,128)(2,1)S(1)}, bf16[384,384]{1,0:T(8,128)(2,1)S(1)}, f32[8,384]{1,0:T(8,128)S(1)}, f32[384,8]{1,0:T(8,128)S(1)}, f32[8,128]{1,0:T(8,128)S(1)}) custom-call(s32[3]{0:T(128)S(1)} %dynamic-slice_reduce_fusion.act_ref, f32[4,384,384]{2,1,0:T(8,128)S(1)} %get-tuple-element.15.tile_ref, ...), custom_call_target="tpu_custom_call" | custom-call | flops 4714999808 | tf_op jit(solution)/shard_map/pallas_call | solution.py:32
  121.5 0.5 slice.27
  122.0 1.5 collective-permute-start.13
  123.5 6.3 %shard_map.75 = (f32[384,2048]{1,0:T(8,128)}, f32[8,128]{1,0:T(8,128)S(1)}) custom-call(bf16[4,384,384]{2,1,0:T(8,128)(2,1)S(1)} %get-tuple-element.19.grad_ref, bf16[384,2048]{1,0:T(8,128)(2,1)S(1)} %copy-done.3, bf16[384,2048]{1,0:T(8,128)(2,1)S(1)} %copy-done.7, bf16[384,2048]{1,0:T(8,128)(2,1)} %collective-permute-done.4.refs_0_.refs_2_, ...), custom_call_target="tpu_custom_call" | custom-call | tf_op jit(solution)/shard_map/pallas_call | solution.py:32
  131.2 4.7 %shard_map.81.refs_3_.refs_2_ = f32[384,2048]{1,0:T(8,128)S(1)} custom-call(f32[8,384]{1,0:T(8,128)S(1)} %get-tuple-element.21.col_ref, f32[384,8]{1,0:T(8,128)S(1)} %get-tuple-element.22.far_ref, f32[384,384]{1,0:T(8,128)} %shard_map.71.refs_0_, f32[384,384]{1,0:T(8,128)} %collective-permute-done.8.refs_7_.refs_1_, ...), custom_call_target="tpu_custom_call" | custom-call | tf_op jit(solution)/shard_map/pallas_call | solution.py:32
  135.9 8.8 %collective-permute-done.15.refs_0_.refs_3_ = bf16[176,2048]{1,0:T(8,128)(2,1)S(1)} collective-permute-done((bf16[176,2048]{1,0:T(8,128)(2,1)S(1)}, bf16[176,2048]{1,0:T(8,128)(2,1)S(1)}, u32[]{:S(2)}, u32[]{:S(2)}) %collective-permute-start.15) | collective-permute-done | bytes 720928 | tf_op jit(solution)/shard_map/ppermute | solution.py:17
  144.6 0.2 collective-permute-done.17.refs_1_.refs_4_
  144.8 1.1 shard_map.82.refs_0_
  146.0 0.1 collective-permute-start.20
  146.0 1.9 %collective-permute-done.20.refs_1_ = f32[2,176,384]{2,1,0:T(8,128)S(1)} collective-permute-done((f32[2,176,384]{2,1,0:T(8,128)S(1)}, f32[2,176,384]{2,1,0:T(8,128)S(1)}, u32[]{:S(2)}, u32[]{:S(2)}) %collective-permute-start.20) | collective-permute-done | bytes 540704 | tf_op jit(solution)/shard_map/ppermute | solution.py:17
  148.0 2.3 %shard_map.83 = f32[384,2048]{1,0:T(8,128)} custom-call(f32[8,384]{1,0:T(8,128)S(1)} %get-tuple-element.21.col_ref, f32[384,8]{1,0:T(8,128)S(1)} %get-tuple-element.22.far_ref, f32[2,176,384]{2,1,0:T(8,128)S(1)} %shard_map.82.refs_0_, f32[2,176,384]{2,1,0:T(8,128)S(1)} %collective-permute-done.20.refs_1_, f32[384,2048]{1,0:T(8,128)S(1)} %shard_map.81.refs_3_.refs_2_, ...), custom_call_target="tpu_custom_call" | custom-call | tf_op jit(solution)/shard_map/pallas_call | solution.py:32
  (41 shorter events, 0.3 us)
Async XLA Ops:
  0.6 99.2 %copy-start = (s32[16,3]{0,1:T(4,128)S(1)}, s32[16,3]{0,1:T(4,128)}, u32[]{:S(2)}) copy-start(s32[16,3]{0,1:T(4,128)} %param.7) | copy-start | bytes 580
  0.6 38.5 %copy-start.1 = (bf16[384,2048]{1,0:T(8,128)(2,1)S(1)}, bf16[384,2048]{1,0:T(8,128)(2,1)}, u32[]{:S(2)}) copy-start(bf16[384,2048]{1,0:T(8,128)(2,1)} %refs_7_.1) | copy-start | bytes 4718596
  0.7 38.5 %collective-permute-start = (bf16[384,2048]{1,0:T(8,128)(2,1)}, bf16[384,2048]{1,0:T(8,128)(2,1)S(1)}, u32[]{:S(2)}, u32[]{:S(2)}) collective-permute-start(bf16[384,2048]{1,0:T(8,128)(2,1)} %right_ref.5), channel_id=1, source_target_pairs={{0,4},{2,6},{4,0},{6,2},{8,12},{10,14},{12,8},{14,10},{16,20},{18,... | collective-permute-start | bytes 4718600 | tf_op jit(solution)/shard_map/ppermute | solution.py:17
  3.7 89.0 %collective-permute-start.2 = (bf16[384,2048]{1,0:T(8,128)(2,1)}, bf16[384,2048]{1,0:T(8,128)(2,1)}, u32[]{:S(2)}, u32[]{:S(2)}) collective-permute-start(bf16[384,2048]{1,0:T(8,128)(2,1)} %right_ref.5), channel_id=1, source_target_pairs={{0,16},{2,18},{4,20},{6,22},{8,24},{10,26},{12,28},{14,30},{16,0},... | collective-permute-start | bytes 4718600 | tf_op jit(solution)/shard_map/ppermute | solution.py:17
  6.3 90.1 %collective-permute-start.4 = (bf16[384,2048]{1,0:T(8,128)(2,1)}, bf16[384,2048]{1,0:T(8,128)(2,1)}, u32[]{:S(2)}, u32[]{:S(2)}) collective-permute-start(bf16[384,2048]{1,0:T(8,128)(2,1)} %right_ref.5), channel_id=1, source_target_pairs={{0,8},{2,10},{4,12},{6,14},{8,0},{10,2},{12,4},{14,6},{16,24},{18,... | collective-permute-start | bytes 4718600 | tf_op jit(solution)/shard_map/ppermute | solution.py:17
  9.3 57.9 %collective-permute-start.6 = (bf16[320,2048]{1,0:T(8,128)(2,1)S(1)}, bf16[320,2048]{1,0:T(8,128)(2,1)S(1)}, u32[]{:S(2)}, u32[]{:S(2)}) collective-permute-start(bf16[320,2048]{1,0:T(8,128)(2,1)S(1)} %slice.21), channel_id=1, source_target_pairs={{0,4},{2,6},{4,0},{6,2},{8,12},{10,14},{12,8},{14,10},{16,20},{18,... | collective-permute-start | bytes 3932168 | tf_op jit(solution)/shard_map/ppermute | solution.py:17
  39.1 1.4 copy-start.2
  40.5 2.8 %copy-start.6 = (bf16[384,2048]{1,0:T(8,128)(2,1)}, bf16[384,2048]{1,0:T(8,128)(2,1)S(1)}, u32[]{:S(2)}) copy-start(bf16[384,2048]{1,0:T(8,128)(2,1)S(1)} %collective-permute-done.refs_1_) | copy-start | bytes 4718596
  43.4 49.3 %collective-permute-start.1 = (f32[2,384,384]{2,1,0:T(8,128)}, f32[2,384,384]{2,1,0:T(8,128)}, u32[]{:S(2)}, u32[]{:S(2)}) collective-permute-start(f32[2,384,384]{2,1,0:T(8,128)} %shard_map.67.refs_0_), channel_id=1, source_target_pairs={{0,1},{1,0},{2,3},{3,2},{4,5},{5,4},{6,7},{7,6},{8,9},{9,8},{10,11... | collective-permute-start | bytes 3538952 | tf_op jit(solution)/shard_map/ppermute | solution.py:17
  44.1 27.9 %collective-permute-start.7 = (bf16[64,2048]{1,0:T(8,128)(2,1)}, bf16[64,2048]{1,0:T(8,128)(2,1)S(1)}, u32[]{:S(2)}, u32[]{:S(2)}) collective-permute-start(bf16[64,2048]{1,0:T(8,128)(2,1)} %slice.22), channel_id=1, source_target_pairs={{0,4},{2,6},{4,0},{6,2},{8,12},{10,14},{12,8},{14,10},{16,20},{18,... | collective-permute-start | bytes 786440 | tf_op jit(solution)/shard_map/ppermute | solution.py:17
  46.2 0.9 copy-start.10
  67.2 1.1 copy-start.8
  68.3 7.0 %copy-start.3 = (bf16[384,2048]{1,0:T(8,128)(2,1)S(1)}, bf16[384,2048]{1,0:T(8,128)(2,1)}, u32[]{:S(2)}) copy-start(bf16[384,2048]{1,0:T(8,128)(2,1)} %right_ref.5) | copy-start | bytes 4718596
  68.3 43.3 %collective-permute-start.14 = (bf16[208,2048]{1,0:T(8,128)(2,1)}, bf16[208,2048]{1,0:T(8,128)(2,1)}, u32[]{:S(2)}, u32[]{:S(2)}) collective-permute-start(bf16[208,2048]{1,0:T(8,128)(2,1)} %shard_map.77), channel_id=1, source_target_pairs={{0,16},{2,18},{4,20},{6,22},{8,24},{10,26},{12,28},{14,30},{16,0},... | collective-permute-start | bytes 2555912 | tf_op jit(solution)/shard_map/ppermute | solution.py:17
  72.0 39.7 %collective-permute-start.16 = (bf16[208,2048]{1,0:T(8,128)(2,1)}, bf16[208,2048]{1,0:T(8,128)(2,1)}, u32[]{:S(2)}, u32[]{:S(2)}) collective-permute-start(bf16[208,2048]{1,0:T(8,128)(2,1)} %shard_map.77), channel_id=1, source_target_pairs={{0,8},{2,10},{4,12},{6,14},{8,0},{10,2},{12,4},{14,6},{16,24},{18,... | collective-permute-start | bytes 2555912 | tf_op jit(solution)/shard_map/ppermute | solution.py:17
  73.8 1.3 copy-start.9
  75.2 1.8 %copy-start.4 = (bf16[384,2048]{1,0:T(8,128)(2,1)}, bf16[384,2048]{1,0:T(8,128)(2,1)S(1)}, u32[]{:S(2)}) copy-start(bf16[384,2048]{1,0:T(8,128)(2,1)S(1)} %shard_map.70.refs_0_.refs_8_) | copy-start | bytes 4718596
  92.6 7.3 %collective-permute-start.8 = (f32[384,384]{1,0:T(8,128)}, f32[384,384]{1,0:T(8,128)}, u32[]{:S(2)}, u32[]{:S(2)}) collective-permute-start(f32[384,384]{1,0:T(8,128)} %shard_map.71.refs_0_), channel_id=1, source_target_pairs={{0,1},{1,0},{2,3},{3,2},{4,5},{5,4},{6,7},{7,6},{8,9},{9,8},{10,11... | collective-permute-start | bytes 1769480 | tf_op jit(solution)/shard_map/ppermute | solution.py:17
  95.9 3.8 %copy-start.11 = (s32[1,384]{1,0:T(1,128)S(1)}, s32[1,384]{1,0:T(1,128)}, u32[]{:S(2)}) copy-start(s32[1,384]{1,0:T(1,128)} %param.6) | copy-start | bytes 4612
  95.9 4.1 %collective-permute-start.3 = (f32[1,384,384]{2,1,0:T(8,128)}, f32[1,384,384]{2,1,0:T(8,128)}, u32[]{:S(2)}, u32[]{:S(2)}) collective-permute-start(f32[1,384,384]{2,1,0:T(8,128)} %shard_map.68.refs_2_), channel_id=1, source_target_pairs={{0,1},{1,0},{2,3},{3,2},{4,5},{5,4},{6,7},{7,6},{8,9},{9,8},{10,11... | collective-permute-start | bytes 1769480 | tf_op jit(solution)/shard_map/ppermute | solution.py:17
  99.6 2.3 %collective-permute-start.5 = (f32[1,384,384]{2,1,0:T(8,128)}, f32[1,384,384]{2,1,0:T(8,128)}, u32[]{:S(2)}, u32[]{:S(2)}) collective-permute-start(f32[1,384,384]{2,1,0:T(8,128)} %shard_map.69.refs_4_), channel_id=1, source_target_pairs={{0,1},{1,0},{2,3},{3,2},{4,5},{5,4},{6,7},{7,6},{8,9},{9,8},{10,11... | collective-permute-start | bytes 1769480 | tf_op jit(solution)/shard_map/ppermute | solution.py:17
  105.7 10.0 %collective-permute-start.10 = (f32[8,384]{1,0:T(8,128)S(1)}, f32[8,384]{1,0:T(8,128)S(1)}, u32[]{:S(2)}, u32[]{:S(2)}) collective-permute-start(f32[8,384]{1,0:T(8,128)S(1)} %get-tuple-element.17.refs_0_), channel_id=1, source_target_pairs={{0,20},{2,22},{4,16},{6,18},{8,28},{10,30},{12,24},{14,26},{16,4},... | collective-permute-start | bytes 36872 | tf_op jit(solution)/shard_map/ppermute | solution.py:17
  105.8 9.9 %collective-permute-start.11 = (f32[8,384]{1,0:T(8,128)S(1)}, f32[8,384]{1,0:T(8,128)S(1)}, u32[]{:S(2)}, u32[]{:S(2)}) collective-permute-start(f32[8,384]{1,0:T(8,128)S(1)} %get-tuple-element.17.refs_0_), channel_id=1, source_target_pairs={{0,28},{2,30},{4,24},{6,26},{8,20},{10,22},{12,16},{14,18},{16,12}... | collective-permute-start | bytes 36872 | tf_op jit(solution)/shard_map/ppermute | solution.py:17
  105.9 9.8 %collective-permute-start.9 = (f32[8,384]{1,0:T(8,128)S(1)}, f32[8,384]{1,0:T(8,128)S(1)}, u32[]{:S(2)}, u32[]{:S(2)}) collective-permute-start(f32[8,384]{1,0:T(8,128)S(1)} %get-tuple-element.17.refs_0_), channel_id=1, source_target_pairs={{0,12},{2,14},{4,8},{6,10},{8,4},{10,6},{12,0},{14,2},{16,28},{18,... | collective-permute-start | bytes 36872 | tf_op jit(solution)/shard_map/ppermute | solution.py:17
  111.7 33.0 %collective-permute-start.15 = (bf16[176,2048]{1,0:T(8,128)(2,1)S(1)}, bf16[176,2048]{1,0:T(8,128)(2,1)S(1)}, u32[]{:S(2)}, u32[]{:S(2)}) collective-permute-start(bf16[176,2048]{1,0:T(8,128)(2,1)S(1)} %shard_map.78), channel_id=1, source_target_pairs={{0,16},{2,18},{4,20},{6,22},{8,24},{10,26},{12,28},{14,30},{16,0},... | collective-permute-start | bytes 2162696 | tf_op jit(solution)/shard_map/ppermute | solution.py:17
  111.8 33.0 %collective-permute-start.17 = (bf16[176,2048]{1,0:T(8,128)(2,1)S(1)}, bf16[176,2048]{1,0:T(8,128)(2,1)S(1)}, u32[]{:S(2)}, u32[]{:S(2)}) collective-permute-start(bf16[176,2048]{1,0:T(8,128)(2,1)S(1)} %shard_map.79), channel_id=1, source_target_pairs={{0,8},{2,10},{4,12},{6,14},{8,0},{10,2},{12,4},{14,6},{16,24},{18,... | collective-permute-start | bytes 2162696 | tf_op jit(solution)/shard_map/ppermute | solution.py:17
  115.7 4.2 %collective-permute-start.12 = (f32[4,8,384]{2,1,0:T(8,128)S(1)}, f32[4,8,384]{2,1,0:T(8,128)S(1)}, u32[]{:S(2)}, u32[]{:S(2)}) collective-permute-start(f32[4,8,384]{2,1,0:T(8,128)S(1)} %shard_map.73.refs_2_), channel_id=1, source_target_pairs={{0,4},{2,6},{4,0},{6,2},{8,12},{10,14},{12,8},{14,10},{16,20},{18,... | collective-permute-start | bytes 147464 | tf_op jit(solution)/shard_map/ppermute | solution.py:17
  118.9 12.3 %collective-permute-start.18 = (f32[208,384]{1,0:T(8,128)S(1)}, f32[208,384]{1,0:T(8,128)S(1)}, u32[]{:S(2)}, u32[]{:S(2)}) collective-permute-start(f32[208,384]{1,0:T(8,128)S(1)} %get-tuple-element.24.refs_2_), channel_id=1, source_target_pairs={{0,1},{1,0},{2,3},{3,2},{4,5},{5,4},{6,7},{7,6},{8,9},{9,8},{10,11... | collective-permute-start | bytes 958472 | tf_op jit(solution)/shard_map/ppermute | solution.py:17
  118.9 12.2 %collective-permute-start.19 = (f32[208,384]{1,0:T(8,128)S(1)}, f32[208,384]{1,0:T(8,128)S(1)}, u32[]{:S(2)}, u32[]{:S(2)}) collective-permute-start(f32[208,384]{1,0:T(8,128)S(1)} %get-tuple-element.25.refs_4_), channel_id=1, source_target_pairs={{0,1},{1,0},{2,3},{3,2},{4,5},{5,4},{6,7},{7,6},{8,9},{9,8},{10,11... | collective-permute-start | bytes 958472 | tf_op jit(solution)/shard_map/ppermute | solution.py:17
  119.9 3.7 %copy-start.7 = (bf16[384,2048]{1,0:T(8,128)(2,1)S(1)}, bf16[384,2048]{1,0:T(8,128)(2,1)}, u32[]{:S(2)}) copy-start(bf16[384,2048]{1,0:T(8,128)(2,1)} %copy-done.6) | copy-start | bytes 4718596
  122.0 7.9 %collective-permute-start.13 = (f32[1]{0:T(128)}, f32[1]{0:T(128)}, u32[]{:S(2)}, u32[]{:S(2)}) collective-permute-start(f32[1]{0:T(128)} %bitcast.5), channel_id=1, source_target_pairs={{0,2},{2,0},{4,6},{6,4},{8,10},{10,8},{12,14},{14,12},{16,18},{18,... | collective-permute-start | bytes 20 | tf_op jit(solution)/shard_map/ppermute | solution.py:17
  123.5 7.7 %copy-start.5 = (bf16[384,2048]{1,0:T(8,128)(2,1)S(1)}, bf16[384,2048]{1,0:T(8,128)(2,1)}, u32[]{:S(2)}) copy-start(bf16[384,2048]{1,0:T(8,128)(2,1)} %copy-done.4) | copy-start | bytes 4718596
  146.0 2.0 %collective-permute-start.20 = (f32[2,176,384]{2,1,0:T(8,128)S(1)}, f32[2,176,384]{2,1,0:T(8,128)S(1)}, u32[]{:S(2)}, u32[]{:S(2)}) collective-permute-start(f32[2,176,384]{2,1,0:T(8,128)S(1)} %shard_map.82.refs_0_), channel_id=1, source_target_pairs={{0,1},{1,0},{2,3},{3,2},{4,5},{5,4},{6,7},{7,6},{8,9},{9,8},{10,11... | collective-permute-start | bytes 1622024 | tf_op jit(solution)/shard_map/ppermute | solution.py:17

commit v3 on v2

--- a/solution.py
+++ b/solution.py
@@ -130,6 +130,7 @@
         in_specs=[pl.BlockSpec(memory_space=pl.ANY)] * count,
         out_specs=pl.BlockSpec(memory_space=pl.ANY),
         input_output_aliases={0: 0},
+        compiler_params=pltpu.CompilerParams(vmem_limit_bytes=1024 * 1024),
         cost_estimate=pl.CostEstimate(flops=0, bytes_accessed=0, transcendentals=0),
     )(array, *earlier)
 

time: 152 us -> 152 us (level)
  waiting for transfers between devices: 84.5 us -> 90.1 us
  Pallas kernels: 33.8 us -> 28.4 us
    ppermute x21, waiting for transfers between devices: 84.5 us -> 90.1 us  [exchanged(): return lax.ppermute(block, axis, [(i, i ^ offset) for i in range(count)])]
    pallas_call x16, Pallas kernels: 33.8 us -> 28.4 us  [call(): pl.pallas_call(kernel, out_shape=out_shape, compiler_params=pltpu.Compile...]
    unnamed x24 -> x34, local copies, waits for them, and re-layouts: 4.71 us -> 5.14 us
  transfers between devices with their start and end apart: 21 -> 21, of which waited for: 10 -> 10; matrix products, arithmetic and copies ran while one was open for 2% -> 2% of each run, Pallas kernels for 20% -> 16%
where the time goes in v3:
time: 152 us; the launch traced here: 151 us
  waiting for transfers between devices  90.1 us (59%)
  Pallas kernels  28.4 us (19%)
  starting transfers between devices  22.2 us (15%)
  local copies, waits for them, and re-layouts  7.45 us (5%)
  between operations  3.33 us (2%)
    ppermute x21, waiting for transfers between devices, exchanged(): return lax.ppermute(block, axis, [(i, i ^ offset) for i in range(count)])  90.1 us
    pallas_call x16, Pallas kernels, call(): pl.pallas_call(kernel, out_shape=out_shape, compiler_params=pltpu.Compile...  28.4 us
    ppermute x21, starting transfers between devices, exchanged(): return lax.ppermute(block, axis, [(i, i ^ offset) for i in range(count)])  22.2 us
    unnamed x34, local copies, waits for them, and re-layouts  5.14 us
  transfers between devices with their start and end apart: 21, of which 10 were waited for; matrix products, arithmetic and copies ran while one was open for 2% of the time, Pallas kernels for 16%

profile of v3, /device:TPU:0, one launch (start us, length us, event | category | flops | bytes accessed | tf_op | source)
XLA Modules:
  0.0 151.4 jit_solution(6699119702872753556)
XLA Ops:
  0.7 3.0 %collective-permute-start = (bf16[384,2048]{1,0:T(8,128)(2,1)}, bf16[384,2048]{1,0:T(8,128)(2,1)S(1)}, u32[]{:S(2)}, u32[]{:S(2)}) collective-permute-start(bf16[384,2048]{1,0:T(8,128)(2,1)} %right_ref.5), channel_id=1, source_target_pairs={{0,4},{2,6},{4,0},{6,2},{8,12},{10,14},{12,8},{14,10},{16,20},{18,... | collective-permute-start | bytes 4718600 | tf_op jit(solution)/shard_map/ppermute | solution.py:17
  3.7 2.6 %collective-permute-start.2 = (bf16[384,2048]{1,0:T(8,128)(2,1)}, bf16[384,2048]{1,0:T(8,128)(2,1)S(1)}, u32[]{:S(2)}, u32[]{:S(2)}) collective-permute-start(bf16[384,2048]{1,0:T(8,128)(2,1)} %right_ref.5), channel_id=1, source_target_pairs={{0,16},{2,18},{4,20},{6,22},{8,24},{10,26},{12,28},{14,30},{16,0},... | collective-permute-start | bytes 4718600 | tf_op jit(solution)/shard_map/ppermute | solution.py:17
  6.3 1.6 %collective-permute-start.4 = (bf16[384,2048]{1,0:T(8,128)(2,1)}, bf16[384,2048]{1,0:T(8,128)(2,1)S(1)}, u32[]{:S(2)}, u32[]{:S(2)}) collective-permute-start(bf16[384,2048]{1,0:T(8,128)(2,1)} %right_ref.5), channel_id=1, source_target_pairs={{0,8},{2,10},{4,12},{6,14},{8,0},{10,2},{12,4},{14,6},{16,24},{18,... | collective-permute-start | bytes 4718600 | tf_op jit(solution)/shard_map/ppermute | solution.py:17
  7.9 1.4 slice.21
  9.3 0.6 collective-permute-start.6
  9.9 29.2 %collective-permute-done.refs_1_ = bf16[384,2048]{1,0:T(8,128)(2,1)S(1)} collective-permute-done((bf16[384,2048]{1,0:T(8,128)(2,1)}, bf16[384,2048]{1,0:T(8,128)(2,1)S(1)}, u32[]{:S(2)}, u32[]{:S(2)}) %collective-permute-start) | collective-permute-done | bytes 1572896 | tf_op jit(solution)/shard_map/ppermute | solution.py:17
  39.1 1.4 copy-done.2
  40.5 1.8 %shard_map.67.refs_0_ = f32[2,384,384]{2,1,0:T(8,128)S(1)} custom-call(bf16[384,2048]{1,0:T(8,128)(2,1)S(1)} %copy-done.1, bf16[384,2048]{1,0:T(8,128)(2,1)S(1)} %copy-done.2, bf16[384,2048]{1,0:T(8,128)(2,1)S(1)} %collective-permute-done.refs_1_), custom_call_target="tpu_custom_call" | custom-call | tf_op jit(solution)/shard_map/pallas_call | solution.py:32
  42.4 1.1 copy-done.8
  43.5 2.1 %collective-permute-start.7 = (bf16[64,2048]{1,0:T(8,128)(2,1)S(1)}, bf16[64,2048]{1,0:T(8,128)(2,1)S(1)}, u32[]{:S(2)}, u32[]{:S(2)}) collective-permute-start(bf16[64,2048]{1,0:T(8,128)(2,1)S(1)} %slice.22), channel_id=1, source_target_pairs={{0,4},{2,6},{4,0},{6,2},{8,12},{10,14},{12,8},{14,10},{16,20},{18,... | collective-permute-start | bytes 786440 | tf_op jit(solution)/shard_map/ppermute | solution.py:17
  45.6 1.0 shard_map.76.refs_0_
  46.7 20.5 %collective-permute-done.6.upper_ref.refs_1_ = bf16[320,2048]{1,0:T(8,128)(2,1)S(1)} collective-permute-done((bf16[320,2048]{1,0:T(8,128)(2,1)S(1)}, bf16[320,2048]{1,0:T(8,128)(2,1)S(1)}, u32[]{:S(2)}, u32[]{:S(2)}) %collective-permute-start.6) | collective-permute-done | bytes 1310752 | tf_op jit(solution)/shard_map/ppermute | solution.py:17
  67.2 3.1 %collective-permute-start.14 = (bf16[208,2048]{1,0:T(8,128)(2,1)}, bf16[208,2048]{1,0:T(8,128)(2,1)}, u32[]{:S(2)}, u32[]{:S(2)}) collective-permute-start(bf16[208,2048]{1,0:T(8,128)(2,1)} %shard_map.77), channel_id=1, source_target_pairs={{0,16},{2,18},{4,20},{6,22},{8,24},{10,26},{12,28},{14,30},{16,0},... | collective-permute-start | bytes 2555912 | tf_op jit(solution)/shard_map/ppermute | solution.py:17
  70.3 1.7 %collective-permute-done.7.lower_ref = bf16[64,2048]{1,0:T(8,128)(2,1)S(1)} collective-permute-done((bf16[64,2048]{1,0:T(8,128)(2,1)S(1)}, bf16[64,2048]{1,0:T(8,128)(2,1)S(1)}, u32[]{:S(2)}, u32[]{:S(2)}) %collective-permute-start.7) | collective-permute-done | bytes 262176 | tf_op jit(solution)/shard_map/ppermute | solution.py:17
  72.0 1.8 %collective-permute-start.16 = (bf16[208,2048]{1,0:T(8,128)(2,1)}, bf16[208,2048]{1,0:T(8,128)(2,1)}, u32[]{:S(2)}, u32[]{:S(2)}) collective-permute-start(bf16[208,2048]{1,0:T(8,128)(2,1)} %shard_map.77), channel_id=1, source_target_pairs={{0,8},{2,10},{4,12},{6,14},{8,0},{10,2},{12,4},{14,6},{16,24},{18,... | collective-permute-start | bytes 2555912 | tf_op jit(solution)/shard_map/ppermute | solution.py:17
  73.8 0.1 shard_map.70.refs_0_.refs_8_
  73.9 1.9 %shard_map.71.refs_0_ = f32[384,384]{1,0:T(8,128)} custom-call(bf16[384,2048]{1,0:T(8,128)(2,1)S(1)} %copy-done.3, bf16[384,2048]{1,0:T(8,128)(2,1)S(1)} %shard_map.70.refs_0_.refs_8_), custom_call_target="tpu_custom_call" | custom-call | tf_op jit(solution)/shard_map/pallas_call | solution.py:32
  75.8 16.7 %collective-permute-done.2.refs_0_.refs_3_ = bf16[384,2048]{1,0:T(8,128)(2,1)S(1)} collective-permute-done((bf16[384,2048]{1,0:T(8,128)(2,1)}, bf16[384,2048]{1,0:T(8,128)(2,1)S(1)}, u32[]{:S(2)}, u32[]{:S(2)}) %collective-permute-start.2) | collective-permute-done | bytes 1572896 | tf_op jit(solution)/shard_map/ppermute | solution.py:17
  92.6 1.8 %shard_map.68.refs_2_ = f32[1,384,384]{2,1,0:T(8,128)} custom-call(bf16[384,2048]{1,0:T(8,128)(2,1)S(1)} %copy-done.1, bf16[384,2048]{1,0:T(8,128)(2,1)S(1)} %collective-permute-done.2.refs_0_.refs_3_, f32[2,384,384]{2,1,0:T(8,128)S(1)} %collective-permute-done.1.refs_1_), custom_call_target="tpu_custom_call" | custom-call | tf_op jit(solution)/shard_map/pallas_call | solution.py:32
  94.4 0.5 collective-permute-start.3
  94.9 1.8 %shard_map.69.refs_4_ = f32[1,384,384]{2,1,0:T(8,128)} custom-call(bf16[384,2048]{1,0:T(8,128)(2,1)S(1)} %copy-done.1, bf16[384,2048]{1,0:T(8,128)(2,1)S(1)} %collective-permute-done.4.refs_0_.refs_2_, f32[2,384,384]{2,1,0:T(8,128)S(1)} %collective-permute-done.1.refs_1_), custom_call_target="tpu_custom_call" | custom-call | tf_op jit(solution)/shard_map/pallas_call | solution.py:32
  96.7 0.1 copy.8.refs_6_.pos_ref
  96.9 0.2 dynamic-slice_reduce_fusion.act_ref
  97.1 2.0 %collective-permute-done.5.refs_5_ = f32[1,384,384]{2,1,0:T(8,128)} collective-permute-done((f32[1,384,384]{2,1,0:T(8,128)}, f32[1,384,384]{2,1,0:T(8,128)}, u32[]{:S(2)}, u32[]{:S(2)}) %collective-permute-start.5) | collective-permute-done | bytes 589856 | tf_op jit(solution)/shard_map/ppermute | solution.py:17
  99.1 1.3 copy-done.7
  100.3 1.3 copy-done.15
  101.6 3.0 %shard_map.72 = (f32[4,384,384]{2,1,0:T(8,128)S(1)}, f32[384,1]{1,0:T(8,128)S(1)}, f32[8,384]{1,0:T(8,128)S(1)}) custom-call(s32[3]{0:T(128)S(1)} %dynamic-slice_reduce_fusion.act_ref, f32[2,384,384]{2,1,0:T(8,128)S(1)} %copy-done.15, f32[2,384,384]{2,1,0:T(8,128)S(1)} %copy-done.7, f32[1,384,384]{2,1,0:T(8,128)} %shard_map.68.refs_2_, ...), custom_call_target="tpu_custom_call" | custom-call | tf_op jit(solution)/shard_map/pallas_call | solution.py:32
  104.6 0.1 collective-permute-start.10
  104.8 0.1 collective-permute-start.9
  104.8 6.8 %collective-permute-done.14.refs_1_.refs_0_.refs_9_ = bf16[208,2048]{1,0:T(8,128)(2,1)} collective-permute-done((bf16[208,2048]{1,0:T(8,128)(2,1)}, bf16[208,2048]{1,0:T(8,128)(2,1)}, u32[]{:S(2)}, u32[]{:S(2)}) %collective-permute-start.14) | collective-permute-done | bytes 852000 | tf_op jit(solution)/shard_map/ppermute | solution.py:17
  111.7 0.1 collective-permute-start.15
  111.8 3.9 %collective-permute-start.17 = (bf16[176,2048]{1,0:T(8,128)(2,1)S(1)}, bf16[176,2048]{1,0:T(8,128)(2,1)S(1)}, u32[]{:S(2)}, u32[]{:S(2)}) collective-permute-start(bf16[176,2048]{1,0:T(8,128)(2,1)S(1)} %shard_map.79), channel_id=1, source_target_pairs={{0,8},{2,10},{4,12},{6,14},{8,0},{10,2},{12,4},{14,6},{16,24},{18,... | collective-permute-start | bytes 2162696 | tf_op jit(solution)/shard_map/ppermute | solution.py:17
  115.7 0.6 collective-permute-start.12
  116.3 2.6 %shard_map.80 = (f32[208,384]{1,0:T(8,128)S(1)}, f32[208,384]{1,0:T(8,128)S(1)}) custom-call(bf16[384,2048]{1,0:T(8,128)(2,1)S(1)} %copy-done.3, bf16[208,2048]{1,0:T(8,128)(2,1)} %collective-permute-done.14.refs_1_.refs_0_.refs_9_, bf16[208,2048]{1,0:T(8,128)(2,1)} %collective-permute-done.16.refs_1_.refs_10_, f32[4,8,384]{2,1,0:T(8,128)S(1)} %shard_map.73.refs_2_), custom_call_target="tpu_custom_call" | custom-call | tf_op jit(solution)/shard_map/pallas_call | solution.py:32
  118.8 0.1 collective-permute-start.18
  118.9 0.5 collective-permute-start.19
  119.4 0.4 collective-permute-done.12
  119.9 1.7 %shard_map.74 = (bf16[4,384,384]{2,1,0:T(8,128)(2,1)S(1)}, bf16[384,384]{1,0:T(8,128)(2,1)S(1)}, f32[8,384]{1,0:T(8,128)S(1)}, f32[384,8]{1,0:T(8,128)S(1)}, f32[8,128]{1,0:T(8,128)S(1)}) custom-call(s32[3]{0:T(128)S(1)} %dynamic-slice_reduce_fusion.act_ref, f32[4,384,384]{2,1,0:T(8,128)S(1)} %get-tuple-element.15.tile_ref, ...), custom_call_target="tpu_custom_call" | custom-call | flops 4714999808 | tf_op jit(solution)/shard_map/pallas_call | solution.py:32
  121.5 0.5 slice.27
  122.1 1.5 collective-permute-start.13
  123.6 4.3 %shard_map.75 = (f32[384,2048]{1,0:T(8,128)}, f32[8,128]{1,0:T(8,128)S(1)}) custom-call(bf16[4,384,384]{2,1,0:T(8,128)(2,1)S(1)} %get-tuple-element.19.grad_ref, bf16[384,2048]{1,0:T(8,128)(2,1)S(1)} %copy-done.3, bf16[384,2048]{1,0:T(8,128)(2,1)S(1)} %copy-done.9, bf16[384,2048]{1,0:T(8,128)(2,1)S(1)} %copy-done.13, bf16[384,2048]{1,0:T(8,128)(2,1)S(1)} %copy-done.11), custom_call_target="tpu_custom_call" | custom-call | tf_op jit(solution)/shard_map/pallas_call | solution.py:32
  129.2 4.8 %shard_map.81.refs_3_.refs_2_ = f32[384,2048]{1,0:T(8,128)S(1)} custom-call(f32[8,384]{1,0:T(8,128)S(1)} %get-tuple-element.21.col_ref, f32[384,8]{1,0:T(8,128)S(1)} %get-tuple-element.22.far_ref, f32[384,384]{1,0:T(8,128)} %shard_map.71.refs_0_, f32[384,384]{1,0:T(8,128)} %collective-permute-done.8.refs_7_.refs_1_, ...), custom_call_target="tpu_custom_call" | custom-call | tf_op jit(solution)/shard_map/pallas_call | solution.py:32
  134.1 10.6 %collective-permute-done.15.refs_0_.refs_3_ = bf16[176,2048]{1,0:T(8,128)(2,1)S(1)} collective-permute-done((bf16[176,2048]{1,0:T(8,128)(2,1)S(1)}, bf16[176,2048]{1,0:T(8,128)(2,1)S(1)}, u32[]{:S(2)}, u32[]{:S(2)}) %collective-permute-start.15) | collective-permute-done | bytes 720928 | tf_op jit(solution)/shard_map/ppermute | solution.py:17
  144.6 0.2 collective-permute-done.17.refs_1_.refs_4_
  144.8 1.1 shard_map.82.refs_0_
  146.0 0.1 collective-permute-start.20
  146.0 1.9 %collective-permute-done.20.refs_1_ = f32[2,176,384]{2,1,0:T(8,128)S(1)} collective-permute-done((f32[2,176,384]{2,1,0:T(8,128)S(1)}, f32[2,176,384]{2,1,0:T(8,128)S(1)}, u32[]{:S(2)}, u32[]{:S(2)}) %collective-permute-start.20) | collective-permute-done | bytes 540704 | tf_op jit(solution)/shard_map/ppermute | solution.py:17
  148.0 2.3 %shard_map.83 = f32[384,2048]{1,0:T(8,128)} custom-call(f32[8,384]{1,0:T(8,128)S(1)} %get-tuple-element.21.col_ref, f32[384,8]{1,0:T(8,128)S(1)} %get-tuple-element.22.far_ref, f32[2,176,384]{2,1,0:T(8,128)S(1)} %shard_map.82.refs_0_, f32[2,176,384]{2,1,0:T(8,128)S(1)} %collective-permute-done.20.refs_1_, f32[384,2048]{1,0:T(8,128)S(1)} %shard_map.81.refs_3_.refs_2_, ...), custom_call_target="tpu_custom_call" | custom-call | tf_op jit(solution)/shard_map/pallas_call | solution.py:32
  (51 shorter events, 0.3 us)
Async XLA Ops:
  0.6 96.3 %copy-start = (s32[16,3]{0,1:T(4,128)S(1)}, s32[16,3]{0,1:T(4,128)}, u32[]{:S(2)}) copy-start(s32[16,3]{0,1:T(4,128)} %param.7) | copy-start | bytes 580
  0.6 38.5 %copy-start.1 = (bf16[384,2048]{1,0:T(8,128)(2,1)S(1)}, bf16[384,2048]{1,0:T(8,128)(2,1)}, u32[]{:S(2)}) copy-start(bf16[384,2048]{1,0:T(8,128)(2,1)} %refs_7_.1) | copy-start | bytes 4718596
  0.7 38.5 %collective-permute-start = (bf16[384,2048]{1,0:T(8,128)(2,1)}, bf16[384,2048]{1,0:T(8,128)(2,1)S(1)}, u32[]{:S(2)}, u32[]{:S(2)}) collective-permute-start(bf16[384,2048]{1,0:T(8,128)(2,1)} %right_ref.5), channel_id=1, source_target_pairs={{0,4},{2,6},{4,0},{6,2},{8,12},{10,14},{12,8},{14,10},{16,20},{18,... | collective-permute-start | bytes 4718600 | tf_op jit(solution)/shard_map/ppermute | solution.py:17
  3.7 88.9 %collective-permute-start.2 = (bf16[384,2048]{1,0:T(8,128)(2,1)}, bf16[384,2048]{1,0:T(8,128)(2,1)S(1)}, u32[]{:S(2)}, u32[]{:S(2)}) collective-permute-start(bf16[384,2048]{1,0:T(8,128)(2,1)} %right_ref.5), channel_id=1, source_target_pairs={{0,16},{2,18},{4,20},{6,22},{8,24},{10,26},{12,28},{14,30},{16,0},... | collective-permute-start | bytes 4718600 | tf_op jit(solution)/shard_map/ppermute | solution.py:17
  6.3 88.6 %collective-permute-start.4 = (bf16[384,2048]{1,0:T(8,128)(2,1)}, bf16[384,2048]{1,0:T(8,128)(2,1)S(1)}, u32[]{:S(2)}, u32[]{:S(2)}) collective-permute-start(bf16[384,2048]{1,0:T(8,128)(2,1)} %right_ref.5), channel_id=1, source_target_pairs={{0,8},{2,10},{4,12},{6,14},{8,0},{10,2},{12,4},{14,6},{16,24},{18,... | collective-permute-start | bytes 4718600 | tf_op jit(solution)/shard_map/ppermute | solution.py:17
  9.3 57.9 %collective-permute-start.6 = (bf16[320,2048]{1,0:T(8,128)(2,1)S(1)}, bf16[320,2048]{1,0:T(8,128)(2,1)S(1)}, u32[]{:S(2)}, u32[]{:S(2)}) collective-permute-start(bf16[320,2048]{1,0:T(8,128)(2,1)S(1)} %slice.21), channel_id=1, source_target_pairs={{0,4},{2,6},{4,0},{6,2},{8,12},{10,14},{12,8},{14,10},{16,20},{18,... | collective-permute-start | bytes 3932168 | tf_op jit(solution)/shard_map/ppermute | solution.py:17
  39.1 1.4 copy-start.2
  42.3 1.1 copy-start.8
  43.5 23.7 %copy-start.14 = (f32[2,384,384]{2,1,0:T(8,128)}, f32[2,384,384]{2,1,0:T(8,128)S(1)}, u32[]{:S(2)}) copy-start(f32[2,384,384]{2,1,0:T(8,128)S(1)} %shard_map.67.refs_0_) | copy-start | bytes 3538948
  43.5 49.1 %collective-permute-start.1 = (f32[2,384,384]{2,1,0:T(8,128)S(1)}, f32[2,384,384]{2,1,0:T(8,128)S(1)}, u32[]{:S(2)}, u32[]{:S(2)}) collective-permute-start(f32[2,384,384]{2,1,0:T(8,128)S(1)} %shard_map.67.refs_0_), channel_id=1, source_target_pairs={{0,1},{1,0},{2,3},{3,2},{4,5},{5,4},{6,7},{7,6},{8,9},{9,8},{10,11... | collective-permute-start | bytes 3538952 | tf_op jit(solution)/shard_map/ppermute | solution.py:17
  43.5 28.5 %collective-permute-start.7 = (bf16[64,2048]{1,0:T(8,128)(2,1)S(1)}, bf16[64,2048]{1,0:T(8,128)(2,1)S(1)}, u32[]{:S(2)}, u32[]{:S(2)}) collective-permute-start(bf16[64,2048]{1,0:T(8,128)(2,1)S(1)} %slice.22), channel_id=1, source_target_pairs={{0,4},{2,6},{4,0},{6,2},{8,12},{10,14},{12,8},{14,10},{16,20},{18,... | collective-permute-start | bytes 786440 | tf_op jit(solution)/shard_map/ppermute | solution.py:17
  67.2 6.7 %copy-start.3 = (bf16[384,2048]{1,0:T(8,128)(2,1)S(1)}, bf16[384,2048]{1,0:T(8,128)(2,1)}, u32[]{:S(2)}) copy-start(bf16[384,2048]{1,0:T(8,128)(2,1)} %right_ref.5) | copy-start | bytes 4718596
  67.2 44.4 %collective-permute-start.14 = (bf16[208,2048]{1,0:T(8,128)(2,1)}, bf16[208,2048]{1,0:T(8,128)(2,1)}, u32[]{:S(2)}, u32[]{:S(2)}) collective-permute-start(bf16[208,2048]{1,0:T(8,128)(2,1)} %shard_map.77), channel_id=1, source_target_pairs={{0,16},{2,18},{4,20},{6,22},{8,24},{10,26},{12,28},{14,30},{16,0},... | collective-permute-start | bytes 2555912 | tf_op jit(solution)/shard_map/ppermute | solution.py:17
  72.0 39.7 %collective-permute-start.16 = (bf16[208,2048]{1,0:T(8,128)(2,1)}, bf16[208,2048]{1,0:T(8,128)(2,1)}, u32[]{:S(2)}, u32[]{:S(2)}) collective-permute-start(bf16[208,2048]{1,0:T(8,128)(2,1)} %shard_map.77), channel_id=1, source_target_pairs={{0,8},{2,10},{4,12},{6,14},{8,0},{10,2},{12,4},{14,6},{16,24},{18,... | collective-permute-start | bytes 2555912 | tf_op jit(solution)/shard_map/ppermute | solution.py:17
  73.9 1.9 %copy-start.4 = (bf16[384,2048]{1,0:T(8,128)(2,1)}, bf16[384,2048]{1,0:T(8,128)(2,1)S(1)}, u32[]{:S(2)}) copy-start(bf16[384,2048]{1,0:T(8,128)(2,1)S(1)} %shard_map.70.refs_0_.refs_8_) | copy-start | bytes 4718596
  92.5 1.8 %copy-start.10 = (bf16[384,2048]{1,0:T(8,128)(2,1)}, bf16[384,2048]{1,0:T(8,128)(2,1)S(1)}, u32[]{:S(2)}) copy-start(bf16[384,2048]{1,0:T(8,128)(2,1)S(1)} %collective-permute-done.2.refs_0_.refs_3_) | copy-start | bytes 4718596
  92.5 4.5 %collective-permute-start.8 = (f32[384,384]{1,0:T(8,128)}, f32[384,384]{1,0:T(8,128)}, u32[]{:S(2)}, u32[]{:S(2)}) collective-permute-start(f32[384,384]{1,0:T(8,128)} %shard_map.71.refs_0_), channel_id=1, source_target_pairs={{0,1},{1,0},{2,3},{3,2},{4,5},{5,4},{6,7},{7,6},{8,9},{9,8},{10,11... | collective-permute-start | bytes 1769480 | tf_op jit(solution)/shard_map/ppermute | solution.py:17
  92.5 2.3 %copy-start.6 = (f32[2,384,384]{2,1,0:T(8,128)}, f32[2,384,384]{2,1,0:T(8,128)S(1)}, u32[]{:S(2)}) copy-start(f32[2,384,384]{2,1,0:T(8,128)S(1)} %collective-permute-done.1.refs_1_) | copy-start | bytes 3538948
  94.4 2.4 %copy-start.16 = (s32[1,384]{1,0:T(1,128)S(1)}, s32[1,384]{1,0:T(1,128)}, u32[]{:S(2)}) copy-start(s32[1,384]{1,0:T(1,128)} %param.6) | copy-start | bytes 4612
  94.4 2.7 %collective-permute-start.3 = (f32[1,384,384]{2,1,0:T(8,128)}, f32[1,384,384]{2,1,0:T(8,128)}, u32[]{:S(2)}, u32[]{:S(2)}) collective-permute-start(f32[1,384,384]{2,1,0:T(8,128)} %shard_map.68.refs_2_), channel_id=1, source_target_pairs={{0,1},{1,0},{2,3},{3,2},{4,5},{5,4},{6,7},{7,6},{8,9},{9,8},{10,11... | collective-permute-start | bytes 1769480 | tf_op jit(solution)/shard_map/ppermute | solution.py:17
  94.9 1.8 %copy-start.12 = (bf16[384,2048]{1,0:T(8,128)(2,1)}, bf16[384,2048]{1,0:T(8,128)(2,1)S(1)}, u32[]{:S(2)}) copy-start(bf16[384,2048]{1,0:T(8,128)(2,1)S(1)} %collective-permute-done.4.refs_0_.refs_2_) | copy-start | bytes 4718596
  96.7 2.3 %collective-permute-start.5 = (f32[1,384,384]{2,1,0:T(8,128)}, f32[1,384,384]{2,1,0:T(8,128)}, u32[]{:S(2)}, u32[]{:S(2)}) collective-permute-start(f32[1,384,384]{2,1,0:T(8,128)} %shard_map.69.refs_4_), channel_id=1, source_target_pairs={{0,1},{1,0},{2,3},{3,2},{4,5},{5,4},{6,7},{7,6},{8,9},{9,8},{10,11... | collective-permute-start | bytes 1769480 | tf_op jit(solution)/shard_map/ppermute | solution.py:17
  99.1 1.3 copy-start.7
  100.3 1.3 copy-start.15
  104.6 11.1 %collective-permute-start.10 = (f32[8,384]{1,0:T(8,128)S(1)}, f32[8,384]{1,0:T(8,128)S(1)}, u32[]{:S(2)}, u32[]{:S(2)}) collective-permute-start(f32[8,384]{1,0:T(8,128)S(1)} %get-tuple-element.17.refs_0_), channel_id=1, source_target_pairs={{0,20},{2,22},{4,16},{6,18},{8,28},{10,30},{12,24},{14,26},{16,4},... | collective-permute-start | bytes 36872 | tf_op jit(solution)/shard_map/ppermute | solution.py:17
  104.7 11.0 %collective-permute-start.11 = (f32[8,384]{1,0:T(8,128)S(1)}, f32[8,384]{1,0:T(8,128)S(1)}, u32[]{:S(2)}, u32[]{:S(2)}) collective-permute-start(f32[8,384]{1,0:T(8,128)S(1)} %get-tuple-element.17.refs_0_), channel_id=1, source_target_pairs={{0,28},{2,30},{4,24},{6,26},{8,20},{10,22},{12,16},{14,18},{16,12}... | collective-permute-start | bytes 36872 | tf_op jit(solution)/shard_map/ppermute | solution.py:17
  104.8 10.9 %collective-permute-start.9 = (f32[8,384]{1,0:T(8,128)S(1)}, f32[8,384]{1,0:T(8,128)S(1)}, u32[]{:S(2)}, u32[]{:S(2)}) collective-permute-start(f32[8,384]{1,0:T(8,128)S(1)} %get-tuple-element.17.refs_0_), channel_id=1, source_target_pairs={{0,12},{2,14},{4,8},{6,10},{8,4},{10,6},{12,0},{14,2},{16,28},{18,... | collective-permute-start | bytes 36872 | tf_op jit(solution)/shard_map/ppermute | solution.py:17
  111.7 33.0 %collective-permute-start.15 = (bf16[176,2048]{1,0:T(8,128)(2,1)S(1)}, bf16[176,2048]{1,0:T(8,128)(2,1)S(1)}, u32[]{:S(2)}, u32[]{:S(2)}) collective-permute-start(bf16[176,2048]{1,0:T(8,128)(2,1)S(1)} %shard_map.78), channel_id=1, source_target_pairs={{0,16},{2,18},{4,20},{6,22},{8,24},{10,26},{12,28},{14,30},{16,0},... | collective-permute-start | bytes 2162696 | tf_op jit(solution)/shard_map/ppermute | solution.py:17
  111.8 33.0 %collective-permute-start.17 = (bf16[176,2048]{1,0:T(8,128)(2,1)S(1)}, bf16[176,2048]{1,0:T(8,128)(2,1)S(1)}, u32[]{:S(2)}, u32[]{:S(2)}) collective-permute-start(bf16[176,2048]{1,0:T(8,128)(2,1)S(1)} %shard_map.79), channel_id=1, source_target_pairs={{0,8},{2,10},{4,12},{6,14},{8,0},{10,2},{12,4},{14,6},{16,24},{18,... | collective-permute-start | bytes 2162696 | tf_op jit(solution)/shard_map/ppermute | solution.py:17
  115.7 4.2 %collective-permute-start.12 = (f32[4,8,384]{2,1,0:T(8,128)S(1)}, f32[4,8,384]{2,1,0:T(8,128)S(1)}, u32[]{:S(2)}, u32[]{:S(2)}) collective-permute-start(f32[4,8,384]{2,1,0:T(8,128)S(1)} %shard_map.73.refs_2_), channel_id=1, source_target_pairs={{0,4},{2,6},{4,0},{6,2},{8,12},{10,14},{12,8},{14,10},{16,20},{18,... | collective-permute-start | bytes 147464 | tf_op jit(solution)/shard_map/ppermute | solution.py:17
  118.8 10.3 %collective-permute-start.18 = (f32[208,384]{1,0:T(8,128)S(1)}, f32[208,384]{1,0:T(8,128)S(1)}, u32[]{:S(2)}, u32[]{:S(2)}) collective-permute-start(f32[208,384]{1,0:T(8,128)S(1)} %get-tuple-element.24.refs_2_), channel_id=1, source_target_pairs={{0,1},{1,0},{2,3},{3,2},{4,5},{5,4},{6,7},{7,6},{8,9},{9,8},{10,11... | collective-permute-start | bytes 958472 | tf_op jit(solution)/shard_map/ppermute | solution.py:17
  118.9 10.3 %collective-permute-start.19 = (f32[208,384]{1,0:T(8,128)S(1)}, f32[208,384]{1,0:T(8,128)S(1)}, u32[]{:S(2)}, u32[]{:S(2)}) collective-permute-start(f32[208,384]{1,0:T(8,128)S(1)} %get-tuple-element.25.refs_4_), channel_id=1, source_target_pairs={{0,1},{1,0},{2,3},{3,2},{4,5},{5,4},{6,7},{7,6},{8,9},{9,8},{10,11... | collective-permute-start | bytes 958472 | tf_op jit(solution)/shard_map/ppermute | solution.py:17
  119.9 3.7 %copy-start.9 = (bf16[384,2048]{1,0:T(8,128)(2,1)S(1)}, bf16[384,2048]{1,0:T(8,128)(2,1)}, u32[]{:S(2)}) copy-start(bf16[384,2048]{1,0:T(8,128)(2,1)} %copy-done.8) | copy-start | bytes 4718596
  119.9 3.7 %copy-start.11 = (bf16[384,2048]{1,0:T(8,128)(2,1)S(1)}, bf16[384,2048]{1,0:T(8,128)(2,1)}, u32[]{:S(2)}) copy-start(bf16[384,2048]{1,0:T(8,128)(2,1)} %copy-done.10) | copy-start | bytes 4718596
  119.9 3.7 %copy-start.13 = (bf16[384,2048]{1,0:T(8,128)(2,1)S(1)}, bf16[384,2048]{1,0:T(8,128)(2,1)}, u32[]{:S(2)}) copy-start(bf16[384,2048]{1,0:T(8,128)(2,1)} %copy-done.12) | copy-start | bytes 4718596
  122.1 5.8 %collective-permute-start.13 = (f32[1]{0:T(128)}, f32[1]{0:T(128)}, u32[]{:S(2)}, u32[]{:S(2)}) collective-permute-start(f32[1]{0:T(128)} %bitcast.5), channel_id=1, source_target_pairs={{0,2},{2,0},{4,6},{6,4},{8,10},{10,8},{12,14},{14,12},{16,18},{18,... | collective-permute-start | bytes 20 | tf_op jit(solution)/shard_map/ppermute | solution.py:17
  123.6 5.6 %copy-start.5 = (bf16[384,2048]{1,0:T(8,128)(2,1)S(1)}, bf16[384,2048]{1,0:T(8,128)(2,1)}, u32[]{:S(2)}) copy-start(bf16[384,2048]{1,0:T(8,128)(2,1)} %copy-done.4) | copy-start | bytes 4718596
  146.0 2.0 %collective-permute-start.20 = (f32[2,176,384]{2,1,0:T(8,128)S(1)}, f32[2,176,384]{2,1,0:T(8,128)S(1)}, u32[]{:S(2)}, u32[]{:S(2)}) collective-permute-start(f32[2,176,384]{2,1,0:T(8,128)S(1)} %shard_map.82.refs_0_), channel_id=1, source_target_pairs={{0,1},{1,0},{2,3},{3,2},{4,5},{5,4},{6,7},{7,6},{8,9},{9,8},{10,11... | collective-permute-start | bytes 1622024 | tf_op jit(solution)/shard_map/ppermute | solution.py:17

commit v4 on v1

--- a/solution.py
+++ b/solution.py
@@ -32,7 +32,7 @@
     return pl.pallas_call(
         kernel,
         out_shape=out_shape,
-        compiler_params=pltpu.CompilerParams(vmem_limit_bytes=20 * 1024 * 1024),
+        compiler_params=pltpu.CompilerParams(vmem_limit_bytes=12 * 1024 * 1024),
         cost_estimate=pl.CostEstimate(flops=flops, bytes_accessed=0, transcendentals=0),
         **kwargs,
     )(*operands)
@@ -111,6 +111,7 @@
         in_specs=[pl.BlockSpec(memory_space=pl.ANY)] * count,
         out_specs=pl.BlockSpec(memory_space=pl.ANY),
         input_output_aliases={0: 0},
+        compiler_params=pltpu.CompilerParams(vmem_limit_bytes=1024 * 1024),
         cost_estimate=pl.CostEstimate(flops=0, bytes_accessed=0, transcendentals=0),
     )(array, *earlier)
 
@@ -325,16 +326,19 @@
     active = pair_on[me]
     place = positive.reshape(rows, 1)
 
-    first = rows // 2
+    first = 13 * rows // 24
     upper = list(reversed(range(1, levels)))
     far_p = [None] * levels
     for k in reversed(range(levels)):
         far_p[k] = exchanged(passages, "dp", masks[k])
-    part = 5 * rows // 6
+    part = 3 * rows // 4
     far_upper = exchanged(queries[:part], "dp", masks[0])
     far_q = joined(far_upper, exchanged(queries[part:], "dp", masks[0]))
-    head = held_until(rows_after(queries, 0, first, []), [far_upper])
-    heads = [exchanged(head, "dp", masks[k]) for k in upper]
+    firsts = {upper[0]: first, upper[1]: 5 * rows // 8}
+    heads = []
+    for k in upper:
+        head = held_until(rows_after(queries, 0, firsts[k], []), [far_upper])
+        heads.append(exchanged(head, "dp", masks[k]))
 
     early = partial_tiles(queries, [passages, far_p[0]])
     early_other = exchanged(early, "sub", 1)
@@ -369,7 +373,9 @@
         packs[member] = exchanged(pack, "dp", offset)
     come = [packs[member | (member > 1)] for member in range(0, group, 2)]
     tails = [
-        exchanged(rows_after(queries, first, rows - first, [pack, piece]), "dp", masks[k])
+        exchanged(
+            rows_after(queries, firsts[k], rows - firsts[k], [pack, piece]), "dp", masks[k]
+        )
         for k, piece in zip(upper, heads)
     ]
     bundle = call(
@@ -392,7 +398,7 @@
         ),
         [active, tiles, row_lse, place, *packs],
         scalars=1,
-        flops=5405000000,
+        flops=4692000000,
     )
     total = total[0, :1]
     for bit in range(low):
@@ -414,16 +420,16 @@
         last=False,
     )
     ends = []
-    for tail in tails:
-        (part,) = partial_rows(passages, [tail], ends[-2:-1] or [token, passage_grad, loss])
+    for piece in tails[::-1]:
+        (part,) = partial_rows(passages, [piece], ends[-2:-1] or [token, passage_grad, loss])
         ends += [part, exchanged(part, "sub", 1)]
     passage_grad = passage_product(
         col_lse,
         far_lse,
         [passage_grad],
         ends,
-        [(k, first) for k in upper],
-        tails,
+        [(k, firsts[k]) for k in upper[::-1]],
+        tails[::-1],
         last=True,
     )
     return (loss, query_grad, passage_grad)

time: 152 us -> 153 us (level)
  starting transfers between devices: 22.6 us -> 27.7 us
  Pallas kernels: 34 us -> 29.6 us
    ppermute x22, starting transfers between devices: 22.6 us -> 27.7 us  [exchanged(): return lax.ppermute(block, axis, [(i, i ^ offset) for i in range(count)])]
    pallas_call x17 -> x18, Pallas kernels: 34 us -> 29.6 us  [call(): pl.pallas_call(kernel, out_shape=out_shape, compiler_params=pltpu.Compile...]
    unnamed x24 -> x34, local copies, waits for them, and re-layouts: 4.68 us -> 5.14 us
  transfers between devices with their start and end apart: 22 -> 22, of which waited for: 10 -> 9; matrix products, arithmetic and copies ran while one was open for 2% -> 1% of each run, Pallas kernels for 20% -> 17%
where the time goes in v4:
time: 153 us
  waiting for transfers between devices  85.1 us (56%)
  Pallas kernels  29.6 us (19%)
  starting transfers between devices  27.7 us (18%)
  local copies, waits for them, and re-layouts  7.4 us (5%)
  between operations  3.24 us (2%)
    ppermute x22, waiting for transfers between devices, exchanged(): return lax.ppermute(block, axis, [(i, i ^ offset) for i in range(count)])  85.1 us
    pallas_call x18, Pallas kernels, call(): pl.pallas_call(kernel, out_shape=out_shape, compiler_params=pltpu.Compile...  29.6 us
    ppermute x22, starting transfers between devices, exchanged(): return lax.ppermute(block, axis, [(i, i ^ offset) for i in range(count)])  27.7 us
    unnamed x34, local copies, waits for them, and re-layouts  5.14 us
  transfers between devices with their start and end apart: 22, of which 9 were waited for; matrix products, arithmetic and copies ran while one was open for 1% of the time, Pallas kernels for 17%

profile of v4, /device:TPU:0, one launch (start us, length us, event | category | flops | bytes accessed | tf_op | source)
XLA Modules:
  0.0 153.0 jit_solution(4602931801540773590)
XLA Ops:
  0.7 3.0 %collective-permute-start = (bf16[384,2048]{1,0:T(8,128)(2,1)}, bf16[384,2048]{1,0:T(8,128)(2,1)S(1)}, u32[]{:S(2)}, u32[]{:S(2)}) collective-permute-start(bf16[384,2048]{1,0:T(8,128)(2,1)} %right_ref.7), channel_id=1, source_target_pairs={{0,4},{2,6},{4,0},{6,2},{8,12},{10,14},{12,8},{14,10},{16,20},{18,... | collective-permute-start | bytes 4718600 | tf_op jit(solution)/shard_map/ppermute | solution.py:17
  3.7 2.6 %collective-permute-start.2 = (bf16[384,2048]{1,0:T(8,128)(2,1)}, bf16[384,2048]{1,0:T(8,128)(2,1)S(1)}, u32[]{:S(2)}, u32[]{:S(2)}) collective-permute-start(bf16[384,2048]{1,0:T(8,128)(2,1)} %right_ref.7), channel_id=1, source_target_pairs={{0,16},{2,18},{4,20},{6,22},{8,24},{10,26},{12,28},{14,30},{16,0},... | collective-permute-start | bytes 4718600 | tf_op jit(solution)/shard_map/ppermute | solution.py:17
  6.3 1.6 %collective-permute-start.4 = (bf16[384,2048]{1,0:T(8,128)(2,1)}, bf16[384,2048]{1,0:T(8,128)(2,1)S(1)}, u32[]{:S(2)}, u32[]{:S(2)}) collective-permute-start(bf16[384,2048]{1,0:T(8,128)(2,1)} %right_ref.7), channel_id=1, source_target_pairs={{0,8},{2,10},{4,12},{6,14},{8,0},{10,2},{12,4},{14,6},{16,24},{18,... | collective-permute-start | bytes 4718600 | tf_op jit(solution)/shard_map/ppermute | solution.py:17
  7.9 1.4 slice.21
  9.2 0.6 collective-permute-start.6
  9.8 29.3 %collective-permute-done.refs_1_ = bf16[384,2048]{1,0:T(8,128)(2,1)S(1)} collective-permute-done((bf16[384,2048]{1,0:T(8,128)(2,1)}, bf16[384,2048]{1,0:T(8,128)(2,1)S(1)}, u32[]{:S(2)}, u32[]{:S(2)}) %collective-permute-start) | collective-permute-done | bytes 1572896 | tf_op jit(solution)/shard_map/ppermute | solution.py:17
  39.1 1.4 copy-done.2
  40.5 1.8 %shard_map.67.refs_0_ = f32[2,384,384]{2,1,0:T(8,128)S(1)} custom-call(bf16[384,2048]{1,0:T(8,128)(2,1)S(1)} %copy-done.1, bf16[384,2048]{1,0:T(8,128)(2,1)S(1)} %copy-done.2, bf16[384,2048]{1,0:T(8,128)(2,1)S(1)} %collective-permute-done.refs_1_), custom_call_target="tpu_custom_call" | custom-call | tf_op jit(solution)/shard_map/pallas_call | solution.py:32
  42.4 1.1 copy-done.8
  43.5 2.1 %collective-permute-start.7 = (bf16[96,2048]{1,0:T(8,128)(2,1)S(1)}, bf16[96,2048]{1,0:T(8,128)(2,1)S(1)}, u32[]{:S(2)}, u32[]{:S(2)}) collective-permute-start(bf16[96,2048]{1,0:T(8,128)(2,1)S(1)} %slice.22), channel_id=1, source_target_pairs={{0,4},{2,6},{4,0},{6,2},{8,12},{10,14},{12,8},{14,10},{16,20},{18,... | collective-permute-start | bytes 1179656 | tf_op jit(solution)/shard_map/ppermute | solution.py:17
  45.6 1.0 shard_map.76.refs_0_
  46.7 17.7 %collective-permute-done.6.upper_ref.refs_1_ = bf16[288,2048]{1,0:T(8,128)(2,1)S(1)} collective-permute-done((bf16[288,2048]{1,0:T(8,128)(2,1)S(1)}, bf16[288,2048]{1,0:T(8,128)(2,1)S(1)}, u32[]{:S(2)}, u32[]{:S(2)}) %collective-permute-start.6) | collective-permute-done | bytes 1179680 | tf_op jit(solution)/shard_map/ppermute | solution.py:17
  64.4 2.1 %collective-permute-start.14 = (bf16[240,2048]{1,0:T(8,128)(2,1)}, bf16[240,2048]{1,0:T(8,128)(2,1)}, u32[]{:S(2)}, u32[]{:S(2)}) collective-permute-start(bf16[240,2048]{1,0:T(8,128)(2,1)} %shard_map.77), channel_id=1, source_target_pairs={{0,8},{2,10},{4,12},{6,14},{8,0},{10,2},{12,4},{14,6},{16,24},{18,... | collective-permute-start | bytes 2949128 | tf_op jit(solution)/shard_map/ppermute | solution.py:17
  66.5 1.0 shard_map.79.refs_0_
  67.6 4.4 %collective-permute-done.7.lower_ref = bf16[96,2048]{1,0:T(8,128)(2,1)S(1)} collective-permute-done((bf16[96,2048]{1,0:T(8,128)(2,1)S(1)}, bf16[96,2048]{1,0:T(8,128)(2,1)S(1)}, u32[]{:S(2)}, u32[]{:S(2)}) %collective-permute-start.7) | collective-permute-done | bytes 393248 | tf_op jit(solution)/shard_map/ppermute | solution.py:17
  72.0 2.8 %collective-permute-start.16 = (bf16[208,2048]{1,0:T(8,128)(2,1)}, bf16[208,2048]{1,0:T(8,128)(2,1)}, u32[]{:S(2)}, u32[]{:S(2)}) collective-permute-start(bf16[208,2048]{1,0:T(8,128)(2,1)} %shard_map.80), channel_id=1, source_target_pairs={{0,16},{2,18},{4,20},{6,22},{8,24},{10,26},{12,28},{14,30},{16,0},... | collective-permute-start | bytes 2555912 | tf_op jit(solution)/shard_map/ppermute | solution.py:17
  74.9 1.8 %shard_map.71.refs_0_ = f32[384,384]{1,0:T(8,128)} custom-call(bf16[384,2048]{1,0:T(8,128)(2,1)S(1)} %copy-done.3, bf16[384,2048]{1,0:T(8,128)(2,1)S(1)} %shard_map.70.refs_0_.refs_8_), custom_call_target="tpu_custom_call" | custom-call | tf_op jit(solution)/shard_map/pallas_call | solution.py:32
  76.8 1.8 %shard_map.68.refs_2_ = f32[1,384,384]{2,1,0:T(8,128)} custom-call(bf16[384,2048]{1,0:T(8,128)(2,1)S(1)} %copy-done.1, bf16[384,2048]{1,0:T(8,128)(2,1)S(1)} %collective-permute-done.2.refs_0_.refs_3_, f32[2,384,384]{2,1,0:T(8,128)S(1)} %collective-permute-done.1.refs_1_), custom_call_target="tpu_custom_call" | custom-call | tf_op jit(solution)/shard_map/pallas_call | solution.py:32
  78.7 0.5 collective-permute-start.3
  79.2 1.8 %shard_map.69.refs_4_ = f32[1,384,384]{2,1,0:T(8,128)} custom-call(bf16[384,2048]{1,0:T(8,128)(2,1)S(1)} %copy-done.1, bf16[384,2048]{1,0:T(8,128)(2,1)S(1)} %collective-permute-done.4.refs_0_.refs_2_, f32[2,384,384]{2,1,0:T(8,128)S(1)} %collective-permute-done.1.refs_1_), custom_call_target="tpu_custom_call" | custom-call | tf_op jit(solution)/shard_map/pallas_call | solution.py:32
  81.0 0.1 copy.9.refs_6_.pos_ref
  81.2 0.2 dynamic-slice_reduce_fusion.act_ref
  81.4 1.9 %collective-permute-done.5.refs_5_ = f32[1,384,384]{2,1,0:T(8,128)} collective-permute-done((f32[1,384,384]{2,1,0:T(8,128)}, f32[1,384,384]{2,1,0:T(8,128)}, u32[]{:S(2)}, u32[]{:S(2)}) %collective-permute-start.5) | collective-permute-done | bytes 589856 | tf_op jit(solution)/shard_map/ppermute | solution.py:17
  83.3 1.3 copy-done.7
  84.6 1.3 copy-done.15
  85.9 3.0 %shard_map.72 = (f32[4,384,384]{2,1,0:T(8,128)S(1)}, f32[384,1]{1,0:T(8,128)S(1)}, f32[8,384]{1,0:T(8,128)S(1)}) custom-call(s32[3]{0:T(128)S(1)} %dynamic-slice_reduce_fusion.act_ref, f32[2,384,384]{2,1,0:T(8,128)S(1)} %copy-done.15, f32[2,384,384]{2,1,0:T(8,128)S(1)} %copy-done.7, f32[1,384,384]{2,1,0:T(8,128)} %shard_map.68.refs_2_, ...), custom_call_target="tpu_custom_call" | custom-call | tf_op jit(solution)/shard_map/pallas_call | solution.py:32
  88.9 1.4 collective-permute-start.10
  90.2 3.5 %collective-permute-start.11 = (f32[8,384]{1,0:T(8,128)S(1)}, f32[8,384]{1,0:T(8,128)S(1)}, u32[]{:S(2)}, u32[]{:S(2)}) collective-permute-start(f32[8,384]{1,0:T(8,128)S(1)} %get-tuple-element.17.refs_0_), channel_id=1, source_target_pairs={{0,28},{2,30},{4,24},{6,26},{8,20},{10,22},{12,16},{14,18},{16,12}... | collective-permute-start | bytes 36872 | tf_op jit(solution)/shard_map/ppermute | solution.py:17
  93.8 0.5 collective-permute-start.9
  94.3 19.2 %collective-permute-done.16.refs_0_.refs_9_.refs_1_ = bf16[208,2048]{1,0:T(8,128)(2,1)} collective-permute-done((bf16[208,2048]{1,0:T(8,128)(2,1)}, bf16[208,2048]{1,0:T(8,128)(2,1)}, u32[]{:S(2)}, u32[]{:S(2)}) %collective-permute-start.16) | collective-permute-done | bytes 852000 | tf_op jit(solution)/shard_map/ppermute | solution.py:17
  113.5 3.5 %collective-permute-start.20 = (bf16[176,2048]{1,0:T(8,128)(2,1)S(1)}, bf16[176,2048]{1,0:T(8,128)(2,1)S(1)}, u32[]{:S(2)}, u32[]{:S(2)}) collective-permute-start(bf16[176,2048]{1,0:T(8,128)(2,1)S(1)} %shard_map.84), channel_id=1, source_target_pairs={{0,16},{2,18},{4,20},{6,22},{8,24},{10,26},{12,28},{14,30},{16,0},... | collective-permute-start | bytes 2162696 | tf_op jit(solution)/shard_map/ppermute | solution.py:17
  117.0 0.6 collective-permute-start.12
  117.6 0.2 collective-permute-start.15
  117.8 2.6 %shard_map.81 = (f32[208,384]{1,0:T(8,128)S(1)}, f32[240,384]{1,0:T(8,128)S(1)}) custom-call(bf16[384,2048]{1,0:T(8,128)(2,1)S(1)} %copy-done.3, bf16[208,2048]{1,0:T(8,128)(2,1)} %collective-permute-done.16.refs_0_.refs_9_.refs_1_, bf16[240,2048]{1,0:T(8,128)(2,1)} %collective-permute-done.14.refs_1_.refs_10_, f32[4,8,384]{2,1,0:T(8,128)S(1)} %shard_map.73.refs_2_), custom_call_target="tpu_custom_call" | custom-call | tf_op jit(solution)/shard_map/pallas_call | solution.py:32
  120.5 0.5 collective-permute-start.17
  121.0 0.1 collective-permute-done.12
  121.1 1.7 %shard_map.74 = (bf16[4,384,384]{2,1,0:T(8,128)(2,1)S(1)}, bf16[384,384]{1,0:T(8,128)(2,1)S(1)}, f32[8,384]{1,0:T(8,128)S(1)}, f32[384,8]{1,0:T(8,128)S(1)}, f32[8,128]{1,0:T(8,128)S(1)}) custom-call(s32[3]{0:T(128)S(1)} %dynamic-slice_reduce_fusion.act_ref, f32[4,384,384]{2,1,0:T(8,128)S(1)} %get-tuple-element.15.tile_ref, ...), custom_call_target="tpu_custom_call" | custom-call | flops 4691999744 | tf_op jit(solution)/shard_map/pallas_call | solution.py:32
  122.8 0.5 slice.27
  123.3 1.5 collective-permute-start.13
  124.8 4.3 %shard_map.75 = (f32[384,2048]{1,0:T(8,128)}, f32[8,128]{1,0:T(8,128)S(1)}) custom-call(bf16[4,384,384]{2,1,0:T(8,128)(2,1)S(1)} %get-tuple-element.19.grad_ref, bf16[384,2048]{1,0:T(8,128)(2,1)S(1)} %copy-done.3, bf16[384,2048]{1,0:T(8,128)(2,1)S(1)} %copy-done.9, bf16[384,2048]{1,0:T(8,128)(2,1)S(1)} %copy-done.13, bf16[384,2048]{1,0:T(8,128)(2,1)S(1)} %copy-done.11), custom_call_target="tpu_custom_call" | custom-call | tf_op jit(solution)/shard_map/pallas_call | solution.py:32
  130.4 4.9 %shard_map.82.refs_2_.refs_4_ = f32[384,2048]{1,0:T(8,128)S(1)} custom-call(f32[8,384]{1,0:T(8,128)S(1)} %get-tuple-element.21.col_ref, f32[384,8]{1,0:T(8,128)S(1)} %get-tuple-element.22.far_ref, f32[384,384]{1,0:T(8,128)} %shard_map.71.refs_0_, f32[384,384]{1,0:T(8,128)} %collective-permute-done.8.refs_7_.refs_1_, ...), custom_call_target="tpu_custom_call" | custom-call | tf_op jit(solution)/shard_map/pallas_call | solution.py:32
  135.3 8.1 %collective-permute-done.15.refs_0_.refs_5_ = bf16[144,2048]{1,0:T(8,128)(2,1)S(1)} collective-permute-done((bf16[144,2048]{1,0:T(8,128)(2,1)S(1)}, bf16[144,2048]{1,0:T(8,128)(2,1)S(1)}, u32[]{:S(2)}, u32[]{:S(2)}) %collective-permute-start.15) | collective-permute-done | bytes 589856 | tf_op jit(solution)/shard_map/ppermute | solution.py:17
  143.4 0.6 shard_map.83.refs_1_.refs_0_
  144.0 2.9 %collective-permute-done.20.refs_0_.refs_6_ = bf16[176,2048]{1,0:T(8,128)(2,1)S(1)} collective-permute-done((bf16[176,2048]{1,0:T(8,128)(2,1)S(1)}, bf16[176,2048]{1,0:T(8,128)(2,1)S(1)}, u32[]{:S(2)}, u32[]{:S(2)}) %collective-permute-start.20) | collective-permute-done | bytes 720928 | tf_op jit(solution)/shard_map/ppermute | solution.py:17
  146.9 0.7 shard_map.85.refs_2_
  147.7 0.5 collective-permute-start.19
  148.2 1.4 collective-permute-done.19.refs_1_
  149.5 2.4 %shard_map.86 = f32[384,2048]{1,0:T(8,128)} custom-call(f32[8,384]{1,0:T(8,128)S(1)} %get-tuple-element.21.col_ref, f32[384,8]{1,0:T(8,128)S(1)} %get-tuple-element.22.far_ref, f32[144,384]{1,0:T(8,128)S(1)} %shard_map.83.refs_1_.refs_0_, f32[144,384]{1,0:T(8,128)S(1)} %collective-permute-done.19.refs_1_, f32[176,384]{1,0:T(8,128)S(1)} %shard_map.85.refs_2_, ...), custom_call_target="tpu_custom_call" | custom-call | tf_op jit(solution)/shard_map/pallas_call | solution.py:32
  (56 shorter events, 0.6 us)
Async XLA Ops:
  0.6 80.5 %copy-start = (s32[16,3]{0,1:T(4,128)S(1)}, s32[16,3]{0,1:T(4,128)}, u32[]{:S(2)}) copy-start(s32[16,3]{0,1:T(4,128)} %param.7) | copy-start | bytes 580
  0.6 38.5 %copy-start.1 = (bf16[384,2048]{1,0:T(8,128)(2,1)S(1)}, bf16[384,2048]{1,0:T(8,128)(2,1)}, u32[]{:S(2)}) copy-start(bf16[384,2048]{1,0:T(8,128)(2,1)} %array_ref.7) | copy-start | bytes 4718596
  0.7 38.5 %collective-permute-start = (bf16[384,2048]{1,0:T(8,128)(2,1)}, bf16[384,2048]{1,0:T(8,128)(2,1)S(1)}, u32[]{:S(2)}, u32[]{:S(2)}) collective-permute-start(bf16[384,2048]{1,0:T(8,128)(2,1)} %right_ref.7), channel_id=1, source_target_pairs={{0,4},{2,6},{4,0},{6,2},{8,12},{10,14},{12,8},{14,10},{16,20},{18,... | collective-permute-start | bytes 4718600 | tf_op jit(solution)/shard_map/ppermute | solution.py:17
  3.7 73.1 %collective-permute-start.2 = (bf16[384,2048]{1,0:T(8,128)(2,1)}, bf16[384,2048]{1,0:T(8,128)(2,1)S(1)}, u32[]{:S(2)}, u32[]{:S(2)}) collective-permute-start(bf16[384,2048]{1,0:T(8,128)(2,1)} %right_ref.7), channel_id=1, source_target_pairs={{0,16},{2,18},{4,20},{6,22},{8,24},{10,26},{12,28},{14,30},{16,0},... | collective-permute-start | bytes 4718600 | tf_op jit(solution)/shard_map/ppermute | solution.py:17
  6.3 72.9 %collective-permute-start.4 = (bf16[384,2048]{1,0:T(8,128)(2,1)}, bf16[384,2048]{1,0:T(8,128)(2,1)S(1)}, u32[]{:S(2)}, u32[]{:S(2)}) collective-permute-start(bf16[384,2048]{1,0:T(8,128)(2,1)} %right_ref.7), channel_id=1, source_target_pairs={{0,8},{2,10},{4,12},{6,14},{8,0},{10,2},{12,4},{14,6},{16,24},{18,... | collective-permute-start | bytes 4718600 | tf_op jit(solution)/shard_map/ppermute | solution.py:17
  9.2 55.2 %collective-permute-start.6 = (bf16[288,2048]{1,0:T(8,128)(2,1)S(1)}, bf16[288,2048]{1,0:T(8,128)(2,1)S(1)}, u32[]{:S(2)}, u32[]{:S(2)}) collective-permute-start(bf16[288,2048]{1,0:T(8,128)(2,1)S(1)} %slice.21), channel_id=1, source_target_pairs={{0,4},{2,6},{4,0},{6,2},{8,12},{10,14},{12,8},{14,10},{16,20},{18,... | collective-permute-start | bytes 3538952 | tf_op jit(solution)/shard_map/ppermute | solution.py:17
  39.1 1.4 copy-start.2
  42.3 1.1 copy-start.8
  43.5 3.2 %copy-start.14 = (f32[2,384,384]{2,1,0:T(8,128)}, f32[2,384,384]{2,1,0:T(8,128)S(1)}, u32[]{:S(2)}) copy-start(f32[2,384,384]{2,1,0:T(8,128)S(1)} %shard_map.67.refs_0_) | copy-start | bytes 3538948
  43.5 33.3 %collective-permute-start.1 = (f32[2,384,384]{2,1,0:T(8,128)S(1)}, f32[2,384,384]{2,1,0:T(8,128)S(1)}, u32[]{:S(2)}, u32[]{:S(2)}) collective-permute-start(f32[2,384,384]{2,1,0:T(8,128)S(1)} %shard_map.67.refs_0_), channel_id=1, source_target_pairs={{0,1},{1,0},{2,3},{3,2},{4,5},{5,4},{6,7},{7,6},{8,9},{9,8},{10,11... | collective-permute-start | bytes 3538952 | tf_op jit(solution)/shard_map/ppermute | solution.py:17
  43.5 28.5 %collective-permute-start.7 = (bf16[96,2048]{1,0:T(8,128)(2,1)S(1)}, bf16[96,2048]{1,0:T(8,128)(2,1)S(1)}, u32[]{:S(2)}, u32[]{:S(2)}) collective-permute-start(bf16[96,2048]{1,0:T(8,128)(2,1)S(1)} %slice.22), channel_id=1, source_target_pairs={{0,4},{2,6},{4,0},{6,2},{8,12},{10,14},{12,8},{14,10},{16,20},{18,... | collective-permute-start | bytes 1179656 | tf_op jit(solution)/shard_map/ppermute | solution.py:17
  64.4 53.1 %collective-permute-start.14 = (bf16[240,2048]{1,0:T(8,128)(2,1)}, bf16[240,2048]{1,0:T(8,128)(2,1)}, u32[]{:S(2)}, u32[]{:S(2)}) collective-permute-start(bf16[240,2048]{1,0:T(8,128)(2,1)} %shard_map.77), channel_id=1, source_target_pairs={{0,8},{2,10},{4,12},{6,14},{8,0},{10,2},{12,4},{14,6},{16,24},{18,... | collective-permute-start | bytes 2949128 | tf_op jit(solution)/shard_map/ppermute | solution.py:17
  67.5 7.4 %copy-start.3 = (bf16[384,2048]{1,0:T(8,128)(2,1)S(1)}, bf16[384,2048]{1,0:T(8,128)(2,1)}, u32[]{:S(2)}) copy-start(bf16[384,2048]{1,0:T(8,128)(2,1)} %right_ref.7) | copy-start | bytes 4718596
  72.0 41.4 %collective-permute-start.16 = (bf16[208,2048]{1,0:T(8,128)(2,1)}, bf16[208,2048]{1,0:T(8,128)(2,1)}, u32[]{:S(2)}, u32[]{:S(2)}) collective-permute-start(bf16[208,2048]{1,0:T(8,128)(2,1)} %shard_map.80), channel_id=1, source_target_pairs={{0,16},{2,18},{4,20},{6,22},{8,24},{10,26},{12,28},{14,30},{16,0},... | collective-permute-start | bytes 2555912 | tf_op jit(solution)/shard_map/ppermute | solution.py:17
  74.9 1.8 %copy-start.4 = (bf16[384,2048]{1,0:T(8,128)(2,1)}, bf16[384,2048]{1,0:T(8,128)(2,1)S(1)}, u32[]{:S(2)}) copy-start(bf16[384,2048]{1,0:T(8,128)(2,1)S(1)} %shard_map.70.refs_0_.refs_8_) | copy-start | bytes 4718596
  76.8 1.9 %copy-start.10 = (bf16[384,2048]{1,0:T(8,128)(2,1)}, bf16[384,2048]{1,0:T(8,128)(2,1)S(1)}, u32[]{:S(2)}) copy-start(bf16[384,2048]{1,0:T(8,128)(2,1)S(1)} %collective-permute-done.2.refs_0_.refs_3_) | copy-start | bytes 4718596
  76.8 4.6 %collective-permute-start.8 = (f32[384,384]{1,0:T(8,128)}, f32[384,384]{1,0:T(8,128)}, u32[]{:S(2)}, u32[]{:S(2)}) collective-permute-start(f32[384,384]{1,0:T(8,128)} %shard_map.71.refs_0_), channel_id=1, source_target_pairs={{0,1},{1,0},{2,3},{3,2},{4,5},{5,4},{6,7},{7,6},{8,9},{9,8},{10,11... | collective-permute-start | bytes 1769480 | tf_op jit(solution)/shard_map/ppermute | solution.py:17
  76.8 2.3 %copy-start.6 = (f32[2,384,384]{2,1,0:T(8,128)}, f32[2,384,384]{2,1,0:T(8,128)S(1)}, u32[]{:S(2)}) copy-start(f32[2,384,384]{2,1,0:T(8,128)S(1)} %collective-permute-done.1.refs_1_) | copy-start | bytes 3538948
  78.7 2.3 %copy-start.16 = (s32[1,384]{1,0:T(1,128)S(1)}, s32[1,384]{1,0:T(1,128)}, u32[]{:S(2)}) copy-start(s32[1,384]{1,0:T(1,128)} %param.6) | copy-start | bytes 4612
  78.7 2.7 %collective-permute-start.3 = (f32[1,384,384]{2,1,0:T(8,128)}, f32[1,384,384]{2,1,0:T(8,128)}, u32[]{:S(2)}, u32[]{:S(2)}) collective-permute-start(f32[1,384,384]{2,1,0:T(8,128)} %shard_map.68.refs_2_), channel_id=1, source_target_pairs={{0,1},{1,0},{2,3},{3,2},{4,5},{5,4},{6,7},{7,6},{8,9},{9,8},{10,11... | collective-permute-start | bytes 1769480 | tf_op jit(solution)/shard_map/ppermute | solution.py:17
  79.2 1.8 %copy-start.12 = (bf16[384,2048]{1,0:T(8,128)(2,1)}, bf16[384,2048]{1,0:T(8,128)(2,1)S(1)}, u32[]{:S(2)}) copy-start(bf16[384,2048]{1,0:T(8,128)(2,1)S(1)} %collective-permute-done.4.refs_0_.refs_2_) | copy-start | bytes 4718596
  81.0 2.3 %collective-permute-start.5 = (f32[1,384,384]{2,1,0:T(8,128)}, f32[1,384,384]{2,1,0:T(8,128)}, u32[]{:S(2)}, u32[]{:S(2)}) collective-permute-start(f32[1,384,384]{2,1,0:T(8,128)} %shard_map.69.refs_4_), channel_id=1, source_target_pairs={{0,1},{1,0},{2,3},{3,2},{4,5},{5,4},{6,7},{7,6},{8,9},{9,8},{10,11... | collective-permute-start | bytes 1769480 | tf_op jit(solution)/shard_map/ppermute | solution.py:17
  83.3 1.3 copy-start.7
  84.6 1.3 copy-start.15
  88.9 28.1 %collective-permute-start.10 = (f32[8,384]{1,0:T(8,128)S(1)}, f32[8,384]{1,0:T(8,128)S(1)}, u32[]{:S(2)}, u32[]{:S(2)}) collective-permute-start(f32[8,384]{1,0:T(8,128)S(1)} %get-tuple-element.17.refs_0_), channel_id=1, source_target_pairs={{0,20},{2,22},{4,16},{6,18},{8,28},{10,30},{12,24},{14,26},{16,4},... | collective-permute-start | bytes 36872 | tf_op jit(solution)/shard_map/ppermute | solution.py:17
  90.2 26.7 %collective-permute-start.11 = (f32[8,384]{1,0:T(8,128)S(1)}, f32[8,384]{1,0:T(8,128)S(1)}, u32[]{:S(2)}, u32[]{:S(2)}) collective-permute-start(f32[8,384]{1,0:T(8,128)S(1)} %get-tuple-element.17.refs_0_), channel_id=1, source_target_pairs={{0,28},{2,30},{4,24},{6,26},{8,20},{10,22},{12,16},{14,18},{16,12}... | collective-permute-start | bytes 36872 | tf_op jit(solution)/shard_map/ppermute | solution.py:17
  93.8 23.2 %collective-permute-start.9 = (f32[8,384]{1,0:T(8,128)S(1)}, f32[8,384]{1,0:T(8,128)S(1)}, u32[]{:S(2)}, u32[]{:S(2)}) collective-permute-start(f32[8,384]{1,0:T(8,128)S(1)} %get-tuple-element.17.refs_0_), channel_id=1, source_target_pairs={{0,12},{2,14},{4,8},{6,10},{8,4},{10,6},{12,0},{14,2},{16,28},{18,... | collective-permute-start | bytes 36872 | tf_op jit(solution)/shard_map/ppermute | solution.py:17
  113.5 33.4 %collective-permute-start.20 = (bf16[176,2048]{1,0:T(8,128)(2,1)S(1)}, bf16[176,2048]{1,0:T(8,128)(2,1)S(1)}, u32[]{:S(2)}, u32[]{:S(2)}) collective-permute-start(bf16[176,2048]{1,0:T(8,128)(2,1)S(1)} %shard_map.84), channel_id=1, source_target_pairs={{0,16},{2,18},{4,20},{6,22},{8,24},{10,26},{12,28},{14,30},{16,0},... | collective-permute-start | bytes 2162696 | tf_op jit(solution)/shard_map/ppermute | solution.py:17
  117.0 4.2 %collective-permute-start.12 = (f32[4,8,384]{2,1,0:T(8,128)S(1)}, f32[4,8,384]{2,1,0:T(8,128)S(1)}, u32[]{:S(2)}, u32[]{:S(2)}) collective-permute-start(f32[4,8,384]{2,1,0:T(8,128)S(1)} %shard_map.73.refs_2_), channel_id=1, source_target_pairs={{0,4},{2,6},{4,0},{6,2},{8,12},{10,14},{12,8},{14,10},{16,20},{18,... | collective-permute-start | bytes 147464 | tf_op jit(solution)/shard_map/ppermute | solution.py:17
  117.6 25.8 %collective-permute-start.15 = (bf16[144,2048]{1,0:T(8,128)(2,1)S(1)}, bf16[144,2048]{1,0:T(8,128)(2,1)S(1)}, u32[]{:S(2)}, u32[]{:S(2)}) collective-permute-start(bf16[144,2048]{1,0:T(8,128)(2,1)S(1)} %shard_map.78), channel_id=1, source_target_pairs={{0,8},{2,10},{4,12},{6,14},{8,0},{10,2},{12,4},{14,6},{16,24},{18,... | collective-permute-start | bytes 1769480 | tf_op jit(solution)/shard_map/ppermute | solution.py:17
  120.4 10.0 %collective-permute-start.18 = (f32[240,384]{1,0:T(8,128)S(1)}, f32[240,384]{1,0:T(8,128)S(1)}, u32[]{:S(2)}, u32[]{:S(2)}) collective-permute-start(f32[240,384]{1,0:T(8,128)S(1)} %get-tuple-element.25.refs_4_), channel_id=1, source_target_pairs={{0,1},{1,0},{2,3},{3,2},{4,5},{5,4},{6,7},{7,6},{8,9},{9,8},{10,11... | collective-permute-start | bytes 1105928 | tf_op jit(solution)/shard_map/ppermute | solution.py:17
  120.5 9.9 %collective-permute-start.17 = (f32[208,384]{1,0:T(8,128)S(1)}, f32[208,384]{1,0:T(8,128)S(1)}, u32[]{:S(2)}, u32[]{:S(2)}) collective-permute-start(f32[208,384]{1,0:T(8,128)S(1)} %get-tuple-element.24.refs_2_), channel_id=1, source_target_pairs={{0,1},{1,0},{2,3},{3,2},{4,5},{5,4},{6,7},{7,6},{8,9},{9,8},{10,11... | collective-permute-start | bytes 958472 | tf_op jit(solution)/shard_map/ppermute | solution.py:17
  121.1 3.7 %copy-start.9 = (bf16[384,2048]{1,0:T(8,128)(2,1)S(1)}, bf16[384,2048]{1,0:T(8,128)(2,1)}, u32[]{:S(2)}) copy-start(bf16[384,2048]{1,0:T(8,128)(2,1)} %copy-done.8) | copy-start | bytes 4718596
  121.1 3.7 %copy-start.11 = (bf16[384,2048]{1,0:T(8,128)(2,1)S(1)}, bf16[384,2048]{1,0:T(8,128)(2,1)}, u32[]{:S(2)}) copy-start(bf16[384,2048]{1,0:T(8,128)(2,1)} %copy-done.10) | copy-start | bytes 4718596
  121.1 3.7 %copy-start.13 = (bf16[384,2048]{1,0:T(8,128)(2,1)S(1)}, bf16[384,2048]{1,0:T(8,128)(2,1)}, u32[]{:S(2)}) copy-start(bf16[384,2048]{1,0:T(8,128)(2,1)} %copy-done.12) | copy-start | bytes 4718596
  123.3 5.8 %collective-permute-start.13 = (f32[1]{0:T(128)}, f32[1]{0:T(128)}, u32[]{:S(2)}, u32[]{:S(2)}) collective-permute-start(f32[1]{0:T(128)} %bitcast.5), channel_id=1, source_target_pairs={{0,2},{2,0},{4,6},{6,4},{8,10},{10,8},{12,14},{14,12},{16,18},{18,... | collective-permute-start | bytes 20 | tf_op jit(solution)/shard_map/ppermute | solution.py:17
  124.8 5.6 %copy-start.5 = (bf16[384,2048]{1,0:T(8,128)(2,1)S(1)}, bf16[384,2048]{1,0:T(8,128)(2,1)}, u32[]{:S(2)}) copy-start(bf16[384,2048]{1,0:T(8,128)(2,1)} %copy-done.4) | copy-start | bytes 4718596
  147.6 1.9 %collective-permute-start.21 = (f32[176,384]{1,0:T(8,128)S(1)}, f32[176,384]{1,0:T(8,128)S(1)}, u32[]{:S(2)}, u32[]{:S(2)}) collective-permute-start(f32[176,384]{1,0:T(8,128)S(1)} %shard_map.85.refs_2_), channel_id=1, source_target_pairs={{0,1},{1,0},{2,3},{3,2},{4,5},{5,4},{6,7},{7,6},{8,9},{9,8},{10,11... | collective-permute-start | bytes 811016 | tf_op jit(solution)/shard_map/ppermute | solution.py:17
  147.7 1.9 %collective-permute-start.19 = (f32[144,384]{1,0:T(8,128)S(1)}, f32[144,384]{1,0:T(8,128)S(1)}, u32[]{:S(2)}, u32[]{:S(2)}) collective-permute-start(f32[144,384]{1,0:T(8,128)S(1)} %shard_map.83.refs_1_.refs_0_), channel_id=1, source_target_pairs={{0,1},{1,0},{2,3},{3,2},{4,5},{5,4},{6,7},{7,6},{8,9},{9,8},{10,11... | collective-permute-start | bytes 663560 | tf_op jit(solution)/shard_map/ppermute | solution.py:17

commit v5 on v3

--- a/solution.py
+++ b/solution.py
@@ -354,7 +354,7 @@
     far_p = [None] * levels
     for k in reversed(range(levels)):
         far_p[k] = exchanged(passages, "dp", masks[k])
-    part = 5 * rows // 6
+    part = 2 * rows // 3
     far_upper = exchanged(queries[:part], "dp", masks[0])
     far_q = joined(far_upper, exchanged(queries[part:], "dp", masks[0]))
     head = held_until(rows_after(queries, 0, first, []), [far_upper])

time: 152 us -> 152 us (level)
  transfers between devices with their start and end apart: 21 -> 21, of which waited for: 10 -> 10; matrix products, arithmetic and copies ran while one was open for 2% -> 1% of each run, Pallas kernels for 16% -> 16%
where the time goes in v5:
time: 152 us; the launch traced here: 151 us
  waiting for transfers between devices  90.2 us (59%)
  Pallas kernels  28.4 us (19%)
  starting transfers between devices  22.2 us (15%)
  local copies, waits for them, and re-layouts  7.34 us (5%)
  between operations  3.33 us (2%)
    ppermute x21, waiting for transfers between devices, exchanged(): return lax.ppermute(block, axis, [(i, i ^ offset) for i in range(count)])  90.2 us
    pallas_call x16, Pallas kernels, call(): pl.pallas_call(kernel, out_shape=out_shape, compiler_params=pltpu.Compile...  28.4 us
    ppermute x21, starting transfers between devices, exchanged(): return lax.ppermute(block, axis, [(i, i ^ offset) for i in range(count)])  22.2 us
    unnamed x34, local copies, waits for them, and re-layouts  5.14 us
  transfers between devices with their start and end apart: 21, of which 10 were waited for; matrix products, arithmetic and copies ran while one was open for 1% of the time, Pallas kernels for 16%

profile of v5, /device:TPU:0, one launch (start us, length us, event | category | flops | bytes accessed | tf_op | source)
XLA Modules:
  0.0 151.4 jit_solution(14903163312855586104)
XLA Ops:
  0.7 3.0 %collective-permute-start = (bf16[384,2048]{1,0:T(8,128)(2,1)}, bf16[384,2048]{1,0:T(8,128)(2,1)S(1)}, u32[]{:S(2)}, u32[]{:S(2)}) collective-permute-start(bf16[384,2048]{1,0:T(8,128)(2,1)} %right_ref.5), channel_id=1, source_target_pairs={{0,4},{2,6},{4,0},{6,2},{8,12},{10,14},{12,8},{14,10},{16,20},{18,... | collective-permute-start | bytes 4718600 | tf_op jit(solution)/shard_map/ppermute | solution.py:17
  3.7 2.6 %collective-permute-start.2 = (bf16[384,2048]{1,0:T(8,128)(2,1)}, bf16[384,2048]{1,0:T(8,128)(2,1)S(1)}, u32[]{:S(2)}, u32[]{:S(2)}) collective-permute-start(bf16[384,2048]{1,0:T(8,128)(2,1)} %right_ref.5), channel_id=1, source_target_pairs={{0,16},{2,18},{4,20},{6,22},{8,24},{10,26},{12,28},{14,30},{16,0},... | collective-permute-start | bytes 4718600 | tf_op jit(solution)/shard_map/ppermute | solution.py:17
  6.3 1.6 %collective-permute-start.4 = (bf16[384,2048]{1,0:T(8,128)(2,1)}, bf16[384,2048]{1,0:T(8,128)(2,1)S(1)}, u32[]{:S(2)}, u32[]{:S(2)}) collective-permute-start(bf16[384,2048]{1,0:T(8,128)(2,1)} %right_ref.5), channel_id=1, source_target_pairs={{0,8},{2,10},{4,12},{6,14},{8,0},{10,2},{12,4},{14,6},{16,24},{18,... | collective-permute-start | bytes 4718600 | tf_op jit(solution)/shard_map/ppermute | solution.py:17
  7.9 1.3 slice.21
  9.2 0.6 collective-permute-start.6
  9.8 29.4 %collective-permute-done.refs_1_ = bf16[384,2048]{1,0:T(8,128)(2,1)S(1)} collective-permute-done((bf16[384,2048]{1,0:T(8,128)(2,1)}, bf16[384,2048]{1,0:T(8,128)(2,1)S(1)}, u32[]{:S(2)}, u32[]{:S(2)}) %collective-permute-start) | collective-permute-done | bytes 1572896 | tf_op jit(solution)/shard_map/ppermute | solution.py:17
  39.1 1.4 copy-done.2
  40.5 1.8 %shard_map.67.refs_0_ = f32[2,384,384]{2,1,0:T(8,128)S(1)} custom-call(bf16[384,2048]{1,0:T(8,128)(2,1)S(1)} %copy-done.1, bf16[384,2048]{1,0:T(8,128)(2,1)S(1)} %copy-done.2, bf16[384,2048]{1,0:T(8,128)(2,1)S(1)} %collective-permute-done.refs_1_), custom_call_target="tpu_custom_call" | custom-call | tf_op jit(solution)/shard_map/pallas_call | solution.py:32
  42.4 1.1 copy-done.8
  43.5 2.1 %collective-permute-start.7 = (bf16[128,2048]{1,0:T(8,128)(2,1)S(1)}, bf16[128,2048]{1,0:T(8,128)(2,1)S(1)}, u32[]{:S(2)}, u32[]{:S(2)}) collective-permute-start(bf16[128,2048]{1,0:T(8,128)(2,1)S(1)} %slice.22), channel_id=1, source_target_pairs={{0,4},{2,6},{4,0},{6,2},{8,12},{10,14},{12,8},{14,10},{16,20},{18,... | collective-permute-start | bytes 1572872 | tf_op jit(solution)/shard_map/ppermute | solution.py:17
  45.7 1.0 shard_map.76.refs_0_
  46.7 14.9 %collective-permute-done.6.upper_ref.refs_1_ = bf16[256,2048]{1,0:T(8,128)(2,1)S(1)} collective-permute-done((bf16[256,2048]{1,0:T(8,128)(2,1)S(1)}, bf16[256,2048]{1,0:T(8,128)(2,1)S(1)}, u32[]{:S(2)}, u32[]{:S(2)}) %collective-permute-start.6) | collective-permute-done | bytes 1048608 | tf_op jit(solution)/shard_map/ppermute | solution.py:17
  61.6 3.1 %collective-permute-start.14 = (bf16[208,2048]{1,0:T(8,128)(2,1)}, bf16[208,2048]{1,0:T(8,128)(2,1)}, u32[]{:S(2)}, u32[]{:S(2)}) collective-permute-start(bf16[208,2048]{1,0:T(8,128)(2,1)} %shard_map.77), channel_id=1, source_target_pairs={{0,16},{2,18},{4,20},{6,22},{8,24},{10,26},{12,28},{14,30},{16,0},... | collective-permute-start | bytes 2555912 | tf_op jit(solution)/shard_map/ppermute | solution.py:17
  64.7 7.3 %collective-permute-done.7.lower_ref = bf16[128,2048]{1,0:T(8,128)(2,1)S(1)} collective-permute-done((bf16[128,2048]{1,0:T(8,128)(2,1)S(1)}, bf16[128,2048]{1,0:T(8,128)(2,1)S(1)}, u32[]{:S(2)}, u32[]{:S(2)}) %collective-permute-start.7) | collective-permute-done | bytes 524320 | tf_op jit(solution)/shard_map/ppermute | solution.py:17
  72.0 1.8 %collective-permute-start.16 = (bf16[208,2048]{1,0:T(8,128)(2,1)}, bf16[208,2048]{1,0:T(8,128)(2,1)}, u32[]{:S(2)}, u32[]{:S(2)}) collective-permute-start(bf16[208,2048]{1,0:T(8,128)(2,1)} %shard_map.77), channel_id=1, source_target_pairs={{0,8},{2,10},{4,12},{6,14},{8,0},{10,2},{12,4},{14,6},{16,24},{18,... | collective-permute-start | bytes 2555912 | tf_op jit(solution)/shard_map/ppermute | solution.py:17
  73.8 0.1 shard_map.70.refs_0_.refs_8_
  73.9 1.9 %shard_map.71.refs_0_ = f32[384,384]{1,0:T(8,128)} custom-call(bf16[384,2048]{1,0:T(8,128)(2,1)S(1)} %copy-done.3, bf16[384,2048]{1,0:T(8,128)(2,1)S(1)} %shard_map.70.refs_0_.refs_8_), custom_call_target="tpu_custom_call" | custom-call | tf_op jit(solution)/shard_map/pallas_call | solution.py:32
  75.8 16.7 %collective-permute-done.2.refs_0_.refs_3_ = bf16[384,2048]{1,0:T(8,128)(2,1)S(1)} collective-permute-done((bf16[384,2048]{1,0:T(8,128)(2,1)}, bf16[384,2048]{1,0:T(8,128)(2,1)S(1)}, u32[]{:S(2)}, u32[]{:S(2)}) %collective-permute-start.2) | collective-permute-done | bytes 1572896 | tf_op jit(solution)/shard_map/ppermute | solution.py:17
  92.6 1.8 %shard_map.68.refs_2_ = f32[1,384,384]{2,1,0:T(8,128)} custom-call(bf16[384,2048]{1,0:T(8,128)(2,1)S(1)} %copy-done.1, bf16[384,2048]{1,0:T(8,128)(2,1)S(1)} %collective-permute-done.2.refs_0_.refs_3_, f32[2,384,384]{2,1,0:T(8,128)S(1)} %collective-permute-done.1.refs_1_), custom_call_target="tpu_custom_call" | custom-call | tf_op jit(solution)/shard_map/pallas_call | solution.py:32
  94.4 0.5 collective-permute-start.3
  94.9 1.8 %shard_map.69.refs_4_ = f32[1,384,384]{2,1,0:T(8,128)} custom-call(bf16[384,2048]{1,0:T(8,128)(2,1)S(1)} %copy-done.1, bf16[384,2048]{1,0:T(8,128)(2,1)S(1)} %collective-permute-done.4.refs_0_.refs_2_, f32[2,384,384]{2,1,0:T(8,128)S(1)} %collective-permute-done.1.refs_1_), custom_call_target="tpu_custom_call" | custom-call | tf_op jit(solution)/shard_map/pallas_call | solution.py:32
  96.7 0.1 copy.8.refs_6_.pos_ref
  96.9 0.2 dynamic-slice_reduce_fusion.act_ref
  97.1 2.0 %collective-permute-done.5.refs_5_ = f32[1,384,384]{2,1,0:T(8,128)} collective-permute-done((f32[1,384,384]{2,1,0:T(8,128)}, f32[1,384,384]{2,1,0:T(8,128)}, u32[]{:S(2)}, u32[]{:S(2)}) %collective-permute-start.5) | collective-permute-done | bytes 589856 | tf_op jit(solution)/shard_map/ppermute | solution.py:17
  99.1 1.3 copy-done.7
  100.3 1.3 copy-done.15
  101.6 3.0 %shard_map.72 = (f32[4,384,384]{2,1,0:T(8,128)S(1)}, f32[384,1]{1,0:T(8,128)S(1)}, f32[8,384]{1,0:T(8,128)S(1)}) custom-call(s32[3]{0:T(128)S(1)} %dynamic-slice_reduce_fusion.act_ref, f32[2,384,384]{2,1,0:T(8,128)S(1)} %copy-done.15, f32[2,384,384]{2,1,0:T(8,128)S(1)} %copy-done.7, f32[1,384,384]{2,1,0:T(8,128)} %shard_map.68.refs_2_, ...), custom_call_target="tpu_custom_call" | custom-call | tf_op jit(solution)/shard_map/pallas_call | solution.py:32
  104.6 0.1 collective-permute-start.10
  104.8 0.1 collective-permute-start.9
  104.8 6.8 %collective-permute-done.14.refs_1_.refs_0_.refs_9_ = bf16[208,2048]{1,0:T(8,128)(2,1)} collective-permute-done((bf16[208,2048]{1,0:T(8,128)(2,1)}, bf16[208,2048]{1,0:T(8,128)(2,1)}, u32[]{:S(2)}, u32[]{:S(2)}) %collective-permute-start.14) | collective-permute-done | bytes 852000 | tf_op jit(solution)/shard_map/ppermute | solution.py:17
  111.7 0.1 collective-permute-start.15
  111.8 3.9 %collective-permute-start.17 = (bf16[176,2048]{1,0:T(8,128)(2,1)S(1)}, bf16[176,2048]{1,0:T(8,128)(2,1)S(1)}, u32[]{:S(2)}, u32[]{:S(2)}) collective-permute-start(bf16[176,2048]{1,0:T(8,128)(2,1)S(1)} %shard_map.79), channel_id=1, source_target_pairs={{0,8},{2,10},{4,12},{6,14},{8,0},{10,2},{12,4},{14,6},{16,24},{18,... | collective-permute-start | bytes 2162696 | tf_op jit(solution)/shard_map/ppermute | solution.py:17
  115.7 0.6 collective-permute-start.12
  116.3 2.6 %shard_map.80 = (f32[208,384]{1,0:T(8,128)S(1)}, f32[208,384]{1,0:T(8,128)S(1)}) custom-call(bf16[384,2048]{1,0:T(8,128)(2,1)S(1)} %copy-done.3, bf16[208,2048]{1,0:T(8,128)(2,1)} %collective-permute-done.14.refs_1_.refs_0_.refs_9_, bf16[208,2048]{1,0:T(8,128)(2,1)} %collective-permute-done.16.refs_1_.refs_10_, f32[4,8,384]{2,1,0:T(8,128)S(1)} %shard_map.73.refs_2_), custom_call_target="tpu_custom_call" | custom-call | tf_op jit(solution)/shard_map/pallas_call | solution.py:32
  118.8 0.1 collective-permute-start.18
  118.9 0.5 collective-permute-start.19
  119.4 0.4 collective-permute-done.12
  119.9 1.7 %shard_map.74 = (bf16[4,384,384]{2,1,0:T(8,128)(2,1)S(1)}, bf16[384,384]{1,0:T(8,128)(2,1)S(1)}, f32[8,384]{1,0:T(8,128)S(1)}, f32[384,8]{1,0:T(8,128)S(1)}, f32[8,128]{1,0:T(8,128)S(1)}) custom-call(s32[3]{0:T(128)S(1)} %dynamic-slice_reduce_fusion.act_ref, f32[4,384,384]{2,1,0:T(8,128)S(1)} %get-tuple-element.15.tile_ref, ...), custom_call_target="tpu_custom_call" | custom-call | flops 4714999808 | tf_op jit(solution)/shard_map/pallas_call | solution.py:32
  121.5 0.5 slice.27
  122.1 1.5 collective-permute-start.13
  123.6 4.3 %shard_map.75 = (f32[384,2048]{1,0:T(8,128)}, f32[8,128]{1,0:T(8,128)S(1)}) custom-call(bf16[4,384,384]{2,1,0:T(8,128)(2,1)S(1)} %get-tuple-element.19.grad_ref, bf16[384,2048]{1,0:T(8,128)(2,1)S(1)} %copy-done.3, bf16[384,2048]{1,0:T(8,128)(2,1)S(1)} %copy-done.9, bf16[384,2048]{1,0:T(8,128)(2,1)S(1)} %copy-done.13, bf16[384,2048]{1,0:T(8,128)(2,1)S(1)} %copy-done.11), custom_call_target="tpu_custom_call" | custom-call | tf_op jit(solution)/shard_map/pallas_call | solution.py:32
  129.2 4.8 %shard_map.81.refs_3_.refs_2_ = f32[384,2048]{1,0:T(8,128)S(1)} custom-call(f32[8,384]{1,0:T(8,128)S(1)} %get-tuple-element.21.col_ref, f32[384,8]{1,0:T(8,128)S(1)} %get-tuple-element.22.far_ref, f32[384,384]{1,0:T(8,128)} %shard_map.71.refs_0_, f32[384,384]{1,0:T(8,128)} %collective-permute-done.8.refs_7_.refs_1_, ...), custom_call_target="tpu_custom_call" | custom-call | tf_op jit(solution)/shard_map/pallas_call | solution.py:32
  134.1 10.6 %collective-permute-done.15.refs_0_.refs_3_ = bf16[176,2048]{1,0:T(8,128)(2,1)S(1)} collective-permute-done((bf16[176,2048]{1,0:T(8,128)(2,1)S(1)}, bf16[176,2048]{1,0:T(8,128)(2,1)S(1)}, u32[]{:S(2)}, u32[]{:S(2)}) %collective-permute-start.15) | collective-permute-done | bytes 720928 | tf_op jit(solution)/shard_map/ppermute | solution.py:17
  144.6 0.2 collective-permute-done.17.refs_1_.refs_4_
  144.8 1.1 shard_map.82.refs_0_
  146.0 0.1 collective-permute-start.20
  146.0 1.9 %collective-permute-done.20.refs_1_ = f32[2,176,384]{2,1,0:T(8,128)S(1)} collective-permute-done((f32[2,176,384]{2,1,0:T(8,128)S(1)}, f32[2,176,384]{2,1,0:T(8,128)S(1)}, u32[]{:S(2)}, u32[]{:S(2)}) %collective-permute-start.20) | collective-permute-done | bytes 540704 | tf_op jit(solution)/shard_map/ppermute | solution.py:17
  148.0 2.3 %shard_map.83 = f32[384,2048]{1,0:T(8,128)} custom-call(f32[8,384]{1,0:T(8,128)S(1)} %get-tuple-element.21.col_ref, f32[384,8]{1,0:T(8,128)S(1)} %get-tuple-element.22.far_ref, f32[2,176,384]{2,1,0:T(8,128)S(1)} %shard_map.82.refs_0_, f32[2,176,384]{2,1,0:T(8,128)S(1)} %collective-permute-done.20.refs_1_, f32[384,2048]{1,0:T(8,128)S(1)} %shard_map.81.refs_3_.refs_2_, ...), custom_call_target="tpu_custom_call" | custom-call | tf_op jit(solution)/shard_map/pallas_call | solution.py:32
  (51 shorter events, 0.3 us)
Async XLA Ops:
  0.6 96.3 %copy-start = (s32[16,3]{0,1:T(4,128)S(1)}, s32[16,3]{0,1:T(4,128)}, u32[]{:S(2)}) copy-start(s32[16,3]{0,1:T(4,128)} %param.7) | copy-start | bytes 580
  0.6 38.5 %copy-start.1 = (bf16[384,2048]{1,0:T(8,128)(2,1)S(1)}, bf16[384,2048]{1,0:T(8,128)(2,1)}, u32[]{:S(2)}) copy-start(bf16[384,2048]{1,0:T(8,128)(2,1)} %refs_7_.1) | copy-start | bytes 4718596
  0.7 38.5 %collective-permute-start = (bf16[384,2048]{1,0:T(8,128)(2,1)}, bf16[384,2048]{1,0:T(8,128)(2,1)S(1)}, u32[]{:S(2)}, u32[]{:S(2)}) collective-permute-start(bf16[384,2048]{1,0:T(8,128)(2,1)} %right_ref.5), channel_id=1, source_target_pairs={{0,4},{2,6},{4,0},{6,2},{8,12},{10,14},{12,8},{14,10},{16,20},{18,... | collective-permute-start | bytes 4718600 | tf_op jit(solution)/shard_map/ppermute | solution.py:17
  3.7 88.9 %collective-permute-start.2 = (bf16[384,2048]{1,0:T(8,128)(2,1)}, bf16[384,2048]{1,0:T(8,128)(2,1)S(1)}, u32[]{:S(2)}, u32[]{:S(2)}) collective-permute-start(bf16[384,2048]{1,0:T(8,128)(2,1)} %right_ref.5), channel_id=1, source_target_pairs={{0,16},{2,18},{4,20},{6,22},{8,24},{10,26},{12,28},{14,30},{16,0},... | collective-permute-start | bytes 4718600 | tf_op jit(solution)/shard_map/ppermute | solution.py:17
  6.3 88.6 %collective-permute-start.4 = (bf16[384,2048]{1,0:T(8,128)(2,1)}, bf16[384,2048]{1,0:T(8,128)(2,1)S(1)}, u32[]{:S(2)}, u32[]{:S(2)}) collective-permute-start(bf16[384,2048]{1,0:T(8,128)(2,1)} %right_ref.5), channel_id=1, source_target_pairs={{0,8},{2,10},{4,12},{6,14},{8,0},{10,2},{12,4},{14,6},{16,24},{18,... | collective-permute-start | bytes 4718600 | tf_op jit(solution)/shard_map/ppermute | solution.py:17
  9.2 52.4 %collective-permute-start.6 = (bf16[256,2048]{1,0:T(8,128)(2,1)S(1)}, bf16[256,2048]{1,0:T(8,128)(2,1)S(1)}, u32[]{:S(2)}, u32[]{:S(2)}) collective-permute-start(bf16[256,2048]{1,0:T(8,128)(2,1)S(1)} %slice.21), channel_id=1, source_target_pairs={{0,4},{2,6},{4,0},{6,2},{8,12},{10,14},{12,8},{14,10},{16,20},{18,... | collective-permute-start | bytes 3145736 | tf_op jit(solution)/shard_map/ppermute | solution.py:17
  39.1 1.4 copy-start.2
  42.3 1.1 copy-start.8
  43.5 3.2 %copy-start.14 = (f32[2,384,384]{2,1,0:T(8,128)}, f32[2,384,384]{2,1,0:T(8,128)S(1)}, u32[]{:S(2)}) copy-start(f32[2,384,384]{2,1,0:T(8,128)S(1)} %shard_map.67.refs_0_) | copy-start | bytes 3538948
  43.5 49.1 %collective-permute-start.1 = (f32[2,384,384]{2,1,0:T(8,128)S(1)}, f32[2,384,384]{2,1,0:T(8,128)S(1)}, u32[]{:S(2)}, u32[]{:S(2)}) collective-permute-start(f32[2,384,384]{2,1,0:T(8,128)S(1)} %shard_map.67.refs_0_), channel_id=1, source_target_pairs={{0,1},{1,0},{2,3},{3,2},{4,5},{5,4},{6,7},{7,6},{8,9},{9,8},{10,11... | collective-permute-start | bytes 3538952 | tf_op jit(solution)/shard_map/ppermute | solution.py:17
  43.5 28.5 %collective-permute-start.7 = (bf16[128,2048]{1,0:T(8,128)(2,1)S(1)}, bf16[128,2048]{1,0:T(8,128)(2,1)S(1)}, u32[]{:S(2)}, u32[]{:S(2)}) collective-permute-start(bf16[128,2048]{1,0:T(8,128)(2,1)S(1)} %slice.22), channel_id=1, source_target_pairs={{0,4},{2,6},{4,0},{6,2},{8,12},{10,14},{12,8},{14,10},{16,20},{18,... | collective-permute-start | bytes 1572872 | tf_op jit(solution)/shard_map/ppermute | solution.py:17
  61.6 12.3 %copy-start.3 = (bf16[384,2048]{1,0:T(8,128)(2,1)S(1)}, bf16[384,2048]{1,0:T(8,128)(2,1)}, u32[]{:S(2)}) copy-start(bf16[384,2048]{1,0:T(8,128)(2,1)} %right_ref.5) | copy-start | bytes 4718596
  61.6 50.0 %collective-permute-start.14 = (bf16[208,2048]{1,0:T(8,128)(2,1)}, bf16[208,2048]{1,0:T(8,128)(2,1)}, u32[]{:S(2)}, u32[]{:S(2)}) collective-permute-start(bf16[208,2048]{1,0:T(8,128)(2,1)} %shard_map.77), channel_id=1, source_target_pairs={{0,16},{2,18},{4,20},{6,22},{8,24},{10,26},{12,28},{14,30},{16,0},... | collective-permute-start | bytes 2555912 | tf_op jit(solution)/shard_map/ppermute | solution.py:17
  72.0 39.7 %collective-permute-start.16 = (bf16[208,2048]{1,0:T(8,128)(2,1)}, bf16[208,2048]{1,0:T(8,128)(2,1)}, u32[]{:S(2)}, u32[]{:S(2)}) collective-permute-start(bf16[208,2048]{1,0:T(8,128)(2,1)} %shard_map.77), channel_id=1, source_target_pairs={{0,8},{2,10},{4,12},{6,14},{8,0},{10,2},{12,4},{14,6},{16,24},{18,... | collective-permute-start | bytes 2555912 | tf_op jit(solution)/shard_map/ppermute | solution.py:17
  73.9 1.9 %copy-start.4 = (bf16[384,2048]{1,0:T(8,128)(2,1)}, bf16[384,2048]{1,0:T(8,128)(2,1)S(1)}, u32[]{:S(2)}) copy-start(bf16[384,2048]{1,0:T(8,128)(2,1)S(1)} %shard_map.70.refs_0_.refs_8_) | copy-start | bytes 4718596
  92.5 1.8 %copy-start.10 = (bf16[384,2048]{1,0:T(8,128)(2,1)}, bf16[384,2048]{1,0:T(8,128)(2,1)S(1)}, u32[]{:S(2)}) copy-start(bf16[384,2048]{1,0:T(8,128)(2,1)S(1)} %collective-permute-done.2.refs_0_.refs_3_) | copy-start | bytes 4718596
  92.5 4.5 %collective-permute-start.8 = (f32[384,384]{1,0:T(8,128)}, f32[384,384]{1,0:T(8,128)}, u32[]{:S(2)}, u32[]{:S(2)}) collective-permute-start(f32[384,384]{1,0:T(8,128)} %shard_map.71.refs_0_), channel_id=1, source_target_pairs={{0,1},{1,0},{2,3},{3,2},{4,5},{5,4},{6,7},{7,6},{8,9},{9,8},{10,11... | collective-permute-start | bytes 1769480 | tf_op jit(solution)/shard_map/ppermute | solution.py:17
  92.5 2.3 %copy-start.6 = (f32[2,384,384]{2,1,0:T(8,128)}, f32[2,384,384]{2,1,0:T(8,128)S(1)}, u32[]{:S(2)}) copy-start(f32[2,384,384]{2,1,0:T(8,128)S(1)} %collective-permute-done.1.refs_1_) | copy-start | bytes 3538948
  94.4 2.4 %copy-start.16 = (s32[1,384]{1,0:T(1,128)S(1)}, s32[1,384]{1,0:T(1,128)}, u32[]{:S(2)}) copy-start(s32[1,384]{1,0:T(1,128)} %param.6) | copy-start | bytes 4612
  94.4 2.7 %collective-permute-start.3 = (f32[1,384,384]{2,1,0:T(8,128)}, f32[1,384,384]{2,1,0:T(8,128)}, u32[]{:S(2)}, u32[]{:S(2)}) collective-permute-start(f32[1,384,384]{2,1,0:T(8,128)} %shard_map.68.refs_2_), channel_id=1, source_target_pairs={{0,1},{1,0},{2,3},{3,2},{4,5},{5,4},{6,7},{7,6},{8,9},{9,8},{10,11... | collective-permute-start | bytes 1769480 | tf_op jit(solution)/shard_map/ppermute | solution.py:17
  94.9 1.8 %copy-start.12 = (bf16[384,2048]{1,0:T(8,128)(2,1)}, bf16[384,2048]{1,0:T(8,128)(2,1)S(1)}, u32[]{:S(2)}) copy-start(bf16[384,2048]{1,0:T(8,128)(2,1)S(1)} %collective-permute-done.4.refs_0_.refs_2_) | copy-start | bytes 4718596
  96.7 2.3 %collective-permute-start.5 = (f32[1,384,384]{2,1,0:T(8,128)}, f32[1,384,384]{2,1,0:T(8,128)}, u32[]{:S(2)}, u32[]{:S(2)}) collective-permute-start(f32[1,384,384]{2,1,0:T(8,128)} %shard_map.69.refs_4_), channel_id=1, source_target_pairs={{0,1},{1,0},{2,3},{3,2},{4,5},{5,4},{6,7},{7,6},{8,9},{9,8},{10,11... | collective-permute-start | bytes 1769480 | tf_op jit(solution)/shard_map/ppermute | solution.py:17
  99.1 1.3 copy-start.7
  100.3 1.3 copy-start.15
  104.6 11.1 %collective-permute-start.10 = (f32[8,384]{1,0:T(8,128)S(1)}, f32[8,384]{1,0:T(8,128)S(1)}, u32[]{:S(2)}, u32[]{:S(2)}) collective-permute-start(f32[8,384]{1,0:T(8,128)S(1)} %get-tuple-element.17.refs_0_), channel_id=1, source_target_pairs={{0,20},{2,22},{4,16},{6,18},{8,28},{10,30},{12,24},{14,26},{16,4},... | collective-permute-start | bytes 36872 | tf_op jit(solution)/shard_map/ppermute | solution.py:17
  104.7 11.0 %collective-permute-start.11 = (f32[8,384]{1,0:T(8,128)S(1)}, f32[8,384]{1,0:T(8,128)S(1)}, u32[]{:S(2)}, u32[]{:S(2)}) collective-permute-start(f32[8,384]{1,0:T(8,128)S(1)} %get-tuple-element.17.refs_0_), channel_id=1, source_target_pairs={{0,28},{2,30},{4,24},{6,26},{8,20},{10,22},{12,16},{14,18},{16,12}... | collective-permute-start | bytes 36872 | tf_op jit(solution)/shard_map/ppermute | solution.py:17
  104.8 10.9 %collective-permute-start.9 = (f32[8,384]{1,0:T(8,128)S(1)}, f32[8,384]{1,0:T(8,128)S(1)}, u32[]{:S(2)}, u32[]{:S(2)}) collective-permute-start(f32[8,384]{1,0:T(8,128)S(1)} %get-tuple-element.17.refs_0_), channel_id=1, source_target_pairs={{0,12},{2,14},{4,8},{6,10},{8,4},{10,6},{12,0},{14,2},{16,28},{18,... | collective-permute-start | bytes 36872 | tf_op jit(solution)/shard_map/ppermute | solution.py:17
  111.7 33.0 %collective-permute-start.15 = (bf16[176,2048]{1,0:T(8,128)(2,1)S(1)}, bf16[176,2048]{1,0:T(8,128)(2,1)S(1)}, u32[]{:S(2)}, u32[]{:S(2)}) collective-permute-start(bf16[176,2048]{1,0:T(8,128)(2,1)S(1)} %shard_map.78), channel_id=1, source_target_pairs={{0,16},{2,18},{4,20},{6,22},{8,24},{10,26},{12,28},{14,30},{16,0},... | collective-permute-start | bytes 2162696 | tf_op jit(solution)/shard_map/ppermute | solution.py:17
  111.8 33.0 %collective-permute-start.17 = (bf16[176,2048]{1,0:T(8,128)(2,1)S(1)}, bf16[176,2048]{1,0:T(8,128)(2,1)S(1)}, u32[]{:S(2)}, u32[]{:S(2)}) collective-permute-start(bf16[176,2048]{1,0:T(8,128)(2,1)S(1)} %shard_map.79), channel_id=1, source_target_pairs={{0,8},{2,10},{4,12},{6,14},{8,0},{10,2},{12,4},{14,6},{16,24},{18,... | collective-permute-start | bytes 2162696 | tf_op jit(solution)/shard_map/ppermute | solution.py:17
  115.7 4.2 %collective-permute-start.12 = (f32[4,8,384]{2,1,0:T(8,128)S(1)}, f32[4,8,384]{2,1,0:T(8,128)S(1)}, u32[]{:S(2)}, u32[]{:S(2)}) collective-permute-start(f32[4,8,384]{2,1,0:T(8,128)S(1)} %shard_map.73.refs_2_), channel_id=1, source_target_pairs={{0,4},{2,6},{4,0},{6,2},{8,12},{10,14},{12,8},{14,10},{16,20},{18,... | collective-permute-start | bytes 147464 | tf_op jit(solution)/shard_map/ppermute | solution.py:17
  118.8 10.3 %collective-permute-start.18 = (f32[208,384]{1,0:T(8,128)S(1)}, f32[208,384]{1,0:T(8,128)S(1)}, u32[]{:S(2)}, u32[]{:S(2)}) collective-permute-start(f32[208,384]{1,0:T(8,128)S(1)} %get-tuple-element.24.refs_2_), channel_id=1, source_target_pairs={{0,1},{1,0},{2,3},{3,2},{4,5},{5,4},{6,7},{7,6},{8,9},{9,8},{10,11... | collective-permute-start | bytes 958472 | tf_op jit(solution)/shard_map/ppermute | solution.py:17
  118.9 10.3 %collective-permute-start.19 = (f32[208,384]{1,0:T(8,128)S(1)}, f32[208,384]{1,0:T(8,128)S(1)}, u32[]{:S(2)}, u32[]{:S(2)}) collective-permute-start(f32[208,384]{1,0:T(8,128)S(1)} %get-tuple-element.25.refs_4_), channel_id=1, source_target_pairs={{0,1},{1,0},{2,3},{3,2},{4,5},{5,4},{6,7},{7,6},{8,9},{9,8},{10,11... | collective-permute-start | bytes 958472 | tf_op jit(solution)/shard_map/ppermute | solution.py:17
  119.9 3.7 %copy-start.9 = (bf16[384,2048]{1,0:T(8,128)(2,1)S(1)}, bf16[384,2048]{1,0:T(8,128)(2,1)}, u32[]{:S(2)}) copy-start(bf16[384,2048]{1,0:T(8,128)(2,1)} %copy-done.8) | copy-start | bytes 4718596
  119.9 3.7 %copy-start.11 = (bf16[384,2048]{1,0:T(8,128)(2,1)S(1)}, bf16[384,2048]{1,0:T(8,128)(2,1)}, u32[]{:S(2)}) copy-start(bf16[384,2048]{1,0:T(8,128)(2,1)} %copy-done.10) | copy-start | bytes 4718596
  119.9 3.7 %copy-start.13 = (bf16[384,2048]{1,0:T(8,128)(2,1)S(1)}, bf16[384,2048]{1,0:T(8,128)(2,1)}, u32[]{:S(2)}) copy-start(bf16[384,2048]{1,0:T(8,128)(2,1)} %copy-done.12) | copy-start | bytes 4718596
  122.1 5.8 %collective-permute-start.13 = (f32[1]{0:T(128)}, f32[1]{0:T(128)}, u32[]{:S(2)}, u32[]{:S(2)}) collective-permute-start(f32[1]{0:T(128)} %bitcast.5), channel_id=1, source_target_pairs={{0,2},{2,0},{4,6},{6,4},{8,10},{10,8},{12,14},{14,12},{16,18},{18,... | collective-permute-start | bytes 20 | tf_op jit(solution)/shard_map/ppermute | solution.py:17
  123.6 5.6 %copy-start.5 = (bf16[384,2048]{1,0:T(8,128)(2,1)S(1)}, bf16[384,2048]{1,0:T(8,128)(2,1)}, u32[]{:S(2)}) copy-start(bf16[384,2048]{1,0:T(8,128)(2,1)} %copy-done.4) | copy-start | bytes 4718596
  146.0 2.0 %collective-permute-start.20 = (f32[2,176,384]{2,1,0:T(8,128)S(1)}, f32[2,176,384]{2,1,0:T(8,128)S(1)}, u32[]{:S(2)}, u32[]{:S(2)}) collective-permute-start(f32[2,176,384]{2,1,0:T(8,128)S(1)} %shard_map.82.refs_0_), channel_id=1, source_target_pairs={{0,1},{1,0},{2,3},{3,2},{4,5},{5,4},{6,7},{7,6},{8,9},{9,8},{10,11... | collective-permute-start | bytes 1622024 | tf_op jit(solution)/shard_map/ppermute | solution.py:17

commit v6 on v3

--- a/solution.py
+++ b/solution.py
@@ -244,7 +244,7 @@
     return jnp.dot(left, right, preferred_element_type=jnp.float32)
 
 
-STEP = 512
+STEP = 256
 
 
 def column_blocks(width):

time: 152 us -> 152 us (level)
  transfers between devices with their start and end apart: 21 -> 21, of which waited for: 10 -> 10; matrix products, arithmetic and copies ran while one was open for 2% -> 2% of each run, Pallas kernels for 16% -> 17%
where the time goes in v6:
time: 152 us; the launch traced here: 151 us
  waiting for transfers between devices  90 us (59%)
  Pallas kernels  28.5 us (19%)
  starting transfers between devices  22.2 us (15%)
  local copies, waits for them, and re-layouts  7.45 us (5%)
  between operations  3.33 us (2%)
    ppermute x21, waiting for transfers between devices, exchanged(): return lax.ppermute(block, axis, [(i, i ^ offset) for i in range(count)])  90 us
    pallas_call x16, Pallas kernels, call(): pl.pallas_call(kernel, out_shape=out_shape, compiler_params=pltpu.Compile...  28.5 us
    ppermute x21, starting transfers between devices, exchanged(): return lax.ppermute(block, axis, [(i, i ^ offset) for i in range(count)])  22.2 us
    unnamed x34, local copies, waits for them, and re-layouts  5.14 us
  transfers between devices with their start and end apart: 21, of which 10 were waited for; matrix products, arithmetic and copies ran while one was open for 2% of the time, Pallas kernels for 17%

profile of v6, /device:TPU:0, one launch (start us, length us, event | category | flops | bytes accessed | tf_op | source)
XLA Modules:
  0.0 151.5 jit_solution(7217553699837473246)
XLA Ops:
  0.7 3.0 %collective-permute-start = (bf16[384,2048]{1,0:T(8,128)(2,1)}, bf16[384,2048]{1,0:T(8,128)(2,1)S(1)}, u32[]{:S(2)}, u32[]{:S(2)}) collective-permute-start(bf16[384,2048]{1,0:T(8,128)(2,1)} %right_ref.5), channel_id=1, source_target_pairs={{0,4},{2,6},{4,0},{6,2},{8,12},{10,14},{12,8},{14,10},{16,20},{18,... | collective-permute-start | bytes 4718600 | tf_op jit(solution)/shard_map/ppermute | solution.py:17
  3.7 2.6 %collective-permute-start.2 = (bf16[384,2048]{1,0:T(8,128)(2,1)}, bf16[384,2048]{1,0:T(8,128)(2,1)S(1)}, u32[]{:S(2)}, u32[]{:S(2)}) collective-permute-start(bf16[384,2048]{1,0:T(8,128)(2,1)} %right_ref.5), channel_id=1, source_target_pairs={{0,16},{2,18},{4,20},{6,22},{8,24},{10,26},{12,28},{14,30},{16,0},... | collective-permute-start | bytes 4718600 | tf_op jit(solution)/shard_map/ppermute | solution.py:17
  6.3 1.6 %collective-permute-start.4 = (bf16[384,2048]{1,0:T(8,128)(2,1)}, bf16[384,2048]{1,0:T(8,128)(2,1)S(1)}, u32[]{:S(2)}, u32[]{:S(2)}) collective-permute-start(bf16[384,2048]{1,0:T(8,128)(2,1)} %right_ref.5), channel_id=1, source_target_pairs={{0,8},{2,10},{4,12},{6,14},{8,0},{10,2},{12,4},{14,6},{16,24},{18,... | collective-permute-start | bytes 4718600 | tf_op jit(solution)/shard_map/ppermute | solution.py:17
  7.9 1.4 slice.21
  9.3 0.6 collective-permute-start.6
  9.9 29.2 %collective-permute-done.refs_1_ = bf16[384,2048]{1,0:T(8,128)(2,1)S(1)} collective-permute-done((bf16[384,2048]{1,0:T(8,128)(2,1)}, bf16[384,2048]{1,0:T(8,128)(2,1)S(1)}, u32[]{:S(2)}, u32[]{:S(2)}) %collective-permute-start) | collective-permute-done | bytes 1572896 | tf_op jit(solution)/shard_map/ppermute | solution.py:17
  39.1 1.4 copy-done.2
  40.5 1.8 %shard_map.67.refs_0_ = f32[2,384,384]{2,1,0:T(8,128)S(1)} custom-call(bf16[384,2048]{1,0:T(8,128)(2,1)S(1)} %copy-done.1, bf16[384,2048]{1,0:T(8,128)(2,1)S(1)} %copy-done.2, bf16[384,2048]{1,0:T(8,128)(2,1)S(1)} %collective-permute-done.refs_1_), custom_call_target="tpu_custom_call" | custom-call | tf_op jit(solution)/shard_map/pallas_call | solution.py:32
  42.4 1.1 copy-done.8
  43.5 2.1 %collective-permute-start.7 = (bf16[64,2048]{1,0:T(8,128)(2,1)S(1)}, bf16[64,2048]{1,0:T(8,128)(2,1)S(1)}, u32[]{:S(2)}, u32[]{:S(2)}) collective-permute-start(bf16[64,2048]{1,0:T(8,128)(2,1)S(1)} %slice.22), channel_id=1, source_target_pairs={{0,4},{2,6},{4,0},{6,2},{8,12},{10,14},{12,8},{14,10},{16,20},{18,... | collective-permute-start | bytes 786440 | tf_op jit(solution)/shard_map/ppermute | solution.py:17
  45.6 1.0 shard_map.76.refs_0_
  46.7 20.5 %collective-permute-done.6.upper_ref.refs_1_ = bf16[320,2048]{1,0:T(8,128)(2,1)S(1)} collective-permute-done((bf16[320,2048]{1,0:T(8,128)(2,1)S(1)}, bf16[320,2048]{1,0:T(8,128)(2,1)S(1)}, u32[]{:S(2)}, u32[]{:S(2)}) %collective-permute-start.6) | collective-permute-done | bytes 1310752 | tf_op jit(solution)/shard_map/ppermute | solution.py:17
  67.2 3.1 %collective-permute-start.14 = (bf16[208,2048]{1,0:T(8,128)(2,1)}, bf16[208,2048]{1,0:T(8,128)(2,1)}, u32[]{:S(2)}, u32[]{:S(2)}) collective-permute-start(bf16[208,2048]{1,0:T(8,128)(2,1)} %shard_map.77), channel_id=1, source_target_pairs={{0,16},{2,18},{4,20},{6,22},{8,24},{10,26},{12,28},{14,30},{16,0},... | collective-permute-start | bytes 2555912 | tf_op jit(solution)/shard_map/ppermute | solution.py:17
  70.3 1.7 %collective-permute-done.7.lower_ref = bf16[64,2048]{1,0:T(8,128)(2,1)S(1)} collective-permute-done((bf16[64,2048]{1,0:T(8,128)(2,1)S(1)}, bf16[64,2048]{1,0:T(8,128)(2,1)S(1)}, u32[]{:S(2)}, u32[]{:S(2)}) %collective-permute-start.7) | collective-permute-done | bytes 262176 | tf_op jit(solution)/shard_map/ppermute | solution.py:17
  72.0 1.8 %collective-permute-start.16 = (bf16[208,2048]{1,0:T(8,128)(2,1)}, bf16[208,2048]{1,0:T(8,128)(2,1)}, u32[]{:S(2)}, u32[]{:S(2)}) collective-permute-start(bf16[208,2048]{1,0:T(8,128)(2,1)} %shard_map.77), channel_id=1, source_target_pairs={{0,8},{2,10},{4,12},{6,14},{8,0},{10,2},{12,4},{14,6},{16,24},{18,... | collective-permute-start | bytes 2555912 | tf_op jit(solution)/shard_map/ppermute | solution.py:17
  73.8 0.1 shard_map.70.refs_0_.refs_8_
  73.9 1.9 %shard_map.71.refs_0_ = f32[384,384]{1,0:T(8,128)} custom-call(bf16[384,2048]{1,0:T(8,128)(2,1)S(1)} %copy-done.3, bf16[384,2048]{1,0:T(8,128)(2,1)S(1)} %shard_map.70.refs_0_.refs_8_), custom_call_target="tpu_custom_call" | custom-call | tf_op jit(solution)/shard_map/pallas_call | solution.py:32
  75.8 16.7 %collective-permute-done.2.refs_0_.refs_3_ = bf16[384,2048]{1,0:T(8,128)(2,1)S(1)} collective-permute-done((bf16[384,2048]{1,0:T(8,128)(2,1)}, bf16[384,2048]{1,0:T(8,128)(2,1)S(1)}, u32[]{:S(2)}, u32[]{:S(2)}) %collective-permute-start.2) | collective-permute-done | bytes 1572896 | tf_op jit(solution)/shard_map/ppermute | solution.py:17
  92.6 1.8 %shard_map.68.refs_2_ = f32[1,384,384]{2,1,0:T(8,128)} custom-call(bf16[384,2048]{1,0:T(8,128)(2,1)S(1)} %copy-done.1, bf16[384,2048]{1,0:T(8,128)(2,1)S(1)} %collective-permute-done.2.refs_0_.refs_3_, f32[2,384,384]{2,1,0:T(8,128)S(1)} %collective-permute-done.1.refs_1_), custom_call_target="tpu_custom_call" | custom-call | tf_op jit(solution)/shard_map/pallas_call | solution.py:32
  94.4 0.5 collective-permute-start.3
  94.9 1.8 %shard_map.69.refs_4_ = f32[1,384,384]{2,1,0:T(8,128)} custom-call(bf16[384,2048]{1,0:T(8,128)(2,1)S(1)} %copy-done.1, bf16[384,2048]{1,0:T(8,128)(2,1)S(1)} %collective-permute-done.4.refs_0_.refs_2_, f32[2,384,384]{2,1,0:T(8,128)S(1)} %collective-permute-done.1.refs_1_), custom_call_target="tpu_custom_call" | custom-call | tf_op jit(solution)/shard_map/pallas_call | solution.py:32
  96.7 0.1 copy.8.refs_6_.pos_ref
  96.9 0.2 dynamic-slice_reduce_fusion.act_ref
  97.1 2.0 %collective-permute-done.5.refs_5_ = f32[1,384,384]{2,1,0:T(8,128)} collective-permute-done((f32[1,384,384]{2,1,0:T(8,128)}, f32[1,384,384]{2,1,0:T(8,128)}, u32[]{:S(2)}, u32[]{:S(2)}) %collective-permute-start.5) | collective-permute-done | bytes 589856 | tf_op jit(solution)/shard_map/ppermute | solution.py:17
  99.1 1.3 copy-done.7
  100.3 1.3 copy-done.15
  101.6 3.0 %shard_map.72 = (f32[4,384,384]{2,1,0:T(8,128)S(1)}, f32[384,1]{1,0:T(8,128)S(1)}, f32[8,384]{1,0:T(8,128)S(1)}) custom-call(s32[3]{0:T(128)S(1)} %dynamic-slice_reduce_fusion.act_ref, f32[2,384,384]{2,1,0:T(8,128)S(1)} %copy-done.15, f32[2,384,384]{2,1,0:T(8,128)S(1)} %copy-done.7, f32[1,384,384]{2,1,0:T(8,128)} %shard_map.68.refs_2_, ...), custom_call_target="tpu_custom_call" | custom-call | tf_op jit(solution)/shard_map/pallas_call | solution.py:32
  104.6 0.1 collective-permute-start.10
  104.8 0.1 collective-permute-start.9
  104.8 6.8 %collective-permute-done.14.refs_1_.refs_0_.refs_9_ = bf16[208,2048]{1,0:T(8,128)(2,1)} collective-permute-done((bf16[208,2048]{1,0:T(8,128)(2,1)}, bf16[208,2048]{1,0:T(8,128)(2,1)}, u32[]{:S(2)}, u32[]{:S(2)}) %collective-permute-start.14) | collective-permute-done | bytes 852000 | tf_op jit(solution)/shard_map/ppermute | solution.py:17
  111.7 0.1 collective-permute-start.15
  111.8 3.9 %collective-permute-start.17 = (bf16[176,2048]{1,0:T(8,128)(2,1)S(1)}, bf16[176,2048]{1,0:T(8,128)(2,1)S(1)}, u32[]{:S(2)}, u32[]{:S(2)}) collective-permute-start(bf16[176,2048]{1,0:T(8,128)(2,1)S(1)} %shard_map.79), channel_id=1, source_target_pairs={{0,8},{2,10},{4,12},{6,14},{8,0},{10,2},{12,4},{14,6},{16,24},{18,... | collective-permute-start | bytes 2162696 | tf_op jit(solution)/shard_map/ppermute | solution.py:17
  115.7 0.6 collective-permute-start.12
  116.3 2.6 %shard_map.80 = (f32[208,384]{1,0:T(8,128)S(1)}, f32[208,384]{1,0:T(8,128)S(1)}) custom-call(bf16[384,2048]{1,0:T(8,128)(2,1)S(1)} %copy-done.3, bf16[208,2048]{1,0:T(8,128)(2,1)} %collective-permute-done.14.refs_1_.refs_0_.refs_9_, bf16[208,2048]{1,0:T(8,128)(2,1)} %collective-permute-done.16.refs_1_.refs_10_, f32[4,8,384]{2,1,0:T(8,128)S(1)} %shard_map.73.refs_2_), custom_call_target="tpu_custom_call" | custom-call | tf_op jit(solution)/shard_map/pallas_call | solution.py:32
  118.8 0.1 collective-permute-start.18
  118.9 0.5 collective-permute-start.19
  119.4 0.4 collective-permute-done.12
  119.9 1.7 %shard_map.74 = (bf16[4,384,384]{2,1,0:T(8,128)(2,1)S(1)}, bf16[384,384]{1,0:T(8,128)(2,1)S(1)}, f32[8,384]{1,0:T(8,128)S(1)}, f32[384,8]{1,0:T(8,128)S(1)}, f32[8,128]{1,0:T(8,128)S(1)}) custom-call(s32[3]{0:T(128)S(1)} %dynamic-slice_reduce_fusion.act_ref, f32[4,384,384]{2,1,0:T(8,128)S(1)} %get-tuple-element.15.tile_ref, ...), custom_call_target="tpu_custom_call" | custom-call | flops 4714999808 | tf_op jit(solution)/shard_map/pallas_call | solution.py:32
  121.5 0.5 slice.27
  122.1 1.5 collective-permute-start.13
  123.6 4.4 %shard_map.75 = (f32[384,2048]{1,0:T(8,128)}, f32[8,128]{1,0:T(8,128)S(1)}) custom-call(bf16[4,384,384]{2,1,0:T(8,128)(2,1)S(1)} %get-tuple-element.19.grad_ref, bf16[384,2048]{1,0:T(8,128)(2,1)S(1)} %copy-done.3, bf16[384,2048]{1,0:T(8,128)(2,1)S(1)} %copy-done.9, bf16[384,2048]{1,0:T(8,128)(2,1)S(1)} %copy-done.13, bf16[384,2048]{1,0:T(8,128)(2,1)S(1)} %copy-done.11), custom_call_target="tpu_custom_call" | custom-call | tf_op jit(solution)/shard_map/pallas_call | solution.py:32
  129.3 4.8 %shard_map.81.refs_3_.refs_2_ = f32[384,2048]{1,0:T(8,128)S(1)} custom-call(f32[8,384]{1,0:T(8,128)S(1)} %get-tuple-element.21.col_ref, f32[384,8]{1,0:T(8,128)S(1)} %get-tuple-element.22.far_ref, f32[384,384]{1,0:T(8,128)} %shard_map.71.refs_0_, f32[384,384]{1,0:T(8,128)} %collective-permute-done.8.refs_7_.refs_1_, ...), custom_call_target="tpu_custom_call" | custom-call | tf_op jit(solution)/shard_map/pallas_call | solution.py:32
  134.1 10.5 %collective-permute-done.15.refs_0_.refs_3_ = bf16[176,2048]{1,0:T(8,128)(2,1)S(1)} collective-permute-done((bf16[176,2048]{1,0:T(8,128)(2,1)S(1)}, bf16[176,2048]{1,0:T(8,128)(2,1)S(1)}, u32[]{:S(2)}, u32[]{:S(2)}) %collective-permute-start.15) | collective-permute-done | bytes 720928 | tf_op jit(solution)/shard_map/ppermute | solution.py:17
  144.6 0.2 collective-permute-done.17.refs_1_.refs_4_
  144.8 1.1 shard_map.82.refs_0_
  146.0 0.1 collective-permute-start.20
  146.0 1.9 %collective-permute-done.20.refs_1_ = f32[2,176,384]{2,1,0:T(8,128)S(1)} collective-permute-done((f32[2,176,384]{2,1,0:T(8,128)S(1)}, f32[2,176,384]{2,1,0:T(8,128)S(1)}, u32[]{:S(2)}, u32[]{:S(2)}) %collective-permute-start.20) | collective-permute-done | bytes 540704 | tf_op jit(solution)/shard_map/ppermute | solution.py:17
  148.0 2.4 %shard_map.83 = f32[384,2048]{1,0:T(8,128)} custom-call(f32[8,384]{1,0:T(8,128)S(1)} %get-tuple-element.21.col_ref, f32[384,8]{1,0:T(8,128)S(1)} %get-tuple-element.22.far_ref, f32[2,176,384]{2,1,0:T(8,128)S(1)} %shard_map.82.refs_0_, f32[2,176,384]{2,1,0:T(8,128)S(1)} %collective-permute-done.20.refs_1_, f32[384,2048]{1,0:T(8,128)S(1)} %shard_map.81.refs_3_.refs_2_, ...), custom_call_target="tpu_custom_call" | custom-call | tf_op jit(solution)/shard_map/pallas_call | solution.py:32
  (51 shorter events, 0.3 us)
Async XLA Ops:
  0.6 96.3 %copy-start = (s32[16,3]{0,1:T(4,128)S(1)}, s32[16,3]{0,1:T(4,128)}, u32[]{:S(2)}) copy-start(s32[16,3]{0,1:T(4,128)} %param.7) | copy-start | bytes 580
  0.6 38.5 %copy-start.1 = (bf16[384,2048]{1,0:T(8,128)(2,1)S(1)}, bf16[384,2048]{1,0:T(8,128)(2,1)}, u32[]{:S(2)}) copy-start(bf16[384,2048]{1,0:T(8,128)(2,1)} %refs_7_.1) | copy-start | bytes 4718596
  0.7 38.5 %collective-permute-start = (bf16[384,2048]{1,0:T(8,128)(2,1)}, bf16[384,2048]{1,0:T(8,128)(2,1)S(1)}, u32[]{:S(2)}, u32[]{:S(2)}) collective-permute-start(bf16[384,2048]{1,0:T(8,128)(2,1)} %right_ref.5), channel_id=1, source_target_pairs={{0,4},{2,6},{4,0},{6,2},{8,12},{10,14},{12,8},{14,10},{16,20},{18,... | collective-permute-start | bytes 4718600 | tf_op jit(solution)/shard_map/ppermute | solution.py:17
  3.7 88.9 %collective-permute-start.2 = (bf16[384,2048]{1,0:T(8,128)(2,1)}, bf16[384,2048]{1,0:T(8,128)(2,1)S(1)}, u32[]{:S(2)}, u32[]{:S(2)}) collective-permute-start(bf16[384,2048]{1,0:T(8,128)(2,1)} %right_ref.5), channel_id=1, source_target_pairs={{0,16},{2,18},{4,20},{6,22},{8,24},{10,26},{12,28},{14,30},{16,0},... | collective-permute-start | bytes 4718600 | tf_op jit(solution)/shard_map/ppermute | solution.py:17
  6.3 88.6 %collective-permute-start.4 = (bf16[384,2048]{1,0:T(8,128)(2,1)}, bf16[384,2048]{1,0:T(8,128)(2,1)S(1)}, u32[]{:S(2)}, u32[]{:S(2)}) collective-permute-start(bf16[384,2048]{1,0:T(8,128)(2,1)} %right_ref.5), channel_id=1, source_target_pairs={{0,8},{2,10},{4,12},{6,14},{8,0},{10,2},{12,4},{14,6},{16,24},{18,... | collective-permute-start | bytes 4718600 | tf_op jit(solution)/shard_map/ppermute | solution.py:17
  9.3 57.9 %collective-permute-start.6 = (bf16[320,2048]{1,0:T(8,128)(2,1)S(1)}, bf16[320,2048]{1,0:T(8,128)(2,1)S(1)}, u32[]{:S(2)}, u32[]{:S(2)}) collective-permute-start(bf16[320,2048]{1,0:T(8,128)(2,1)S(1)} %slice.21), channel_id=1, source_target_pairs={{0,4},{2,6},{4,0},{6,2},{8,12},{10,14},{12,8},{14,10},{16,20},{18,... | collective-permute-start | bytes 3932168 | tf_op jit(solution)/shard_map/ppermute | solution.py:17
  39.1 1.4 copy-start.2
  42.3 1.1 copy-start.8
  43.5 23.7 %copy-start.14 = (f32[2,384,384]{2,1,0:T(8,128)}, f32[2,384,384]{2,1,0:T(8,128)S(1)}, u32[]{:S(2)}) copy-start(f32[2,384,384]{2,1,0:T(8,128)S(1)} %shard_map.67.refs_0_) | copy-start | bytes 3538948
  43.5 49.1 %collective-permute-start.1 = (f32[2,384,384]{2,1,0:T(8,128)S(1)}, f32[2,384,384]{2,1,0:T(8,128)S(1)}, u32[]{:S(2)}, u32[]{:S(2)}) collective-permute-start(f32[2,384,384]{2,1,0:T(8,128)S(1)} %shard_map.67.refs_0_), channel_id=1, source_target_pairs={{0,1},{1,0},{2,3},{3,2},{4,5},{5,4},{6,7},{7,6},{8,9},{9,8},{10,11... | collective-permute-start | bytes 3538952 | tf_op jit(solution)/shard_map/ppermute | solution.py:17
  43.5 28.5 %collective-permute-start.7 = (bf16[64,2048]{1,0:T(8,128)(2,1)S(1)}, bf16[64,2048]{1,0:T(8,128)(2,1)S(1)}, u32[]{:S(2)}, u32[]{:S(2)}) collective-permute-start(bf16[64,2048]{1,0:T(8,128)(2,1)S(1)} %slice.22), channel_id=1, source_target_pairs={{0,4},{2,6},{4,0},{6,2},{8,12},{10,14},{12,8},{14,10},{16,20},{18,... | collective-permute-start | bytes 786440 | tf_op jit(solution)/shard_map/ppermute | solution.py:17
  67.2 6.7 %copy-start.3 = (bf16[384,2048]{1,0:T(8,128)(2,1)S(1)}, bf16[384,2048]{1,0:T(8,128)(2,1)}, u32[]{:S(2)}) copy-start(bf16[384,2048]{1,0:T(8,128)(2,1)} %right_ref.5) | copy-start | bytes 4718596
  67.2 44.4 %collective-permute-start.14 = (bf16[208,2048]{1,0:T(8,128)(2,1)}, bf16[208,2048]{1,0:T(8,128)(2,1)}, u32[]{:S(2)}, u32[]{:S(2)}) collective-permute-start(bf16[208,2048]{1,0:T(8,128)(2,1)} %shard_map.77), channel_id=1, source_target_pairs={{0,16},{2,18},{4,20},{6,22},{8,24},{10,26},{12,28},{14,30},{16,0},... | collective-permute-start | bytes 2555912 | tf_op jit(solution)/shard_map/ppermute | solution.py:17
  72.0 39.7 %collective-permute-start.16 = (bf16[208,2048]{1,0:T(8,128)(2,1)}, bf16[208,2048]{1,0:T(8,128)(2,1)}, u32[]{:S(2)}, u32[]{:S(2)}) collective-permute-start(bf16[208,2048]{1,0:T(8,128)(2,1)} %shard_map.77), channel_id=1, source_target_pairs={{0,8},{2,10},{4,12},{6,14},{8,0},{10,2},{12,4},{14,6},{16,24},{18,... | collective-permute-start | bytes 2555912 | tf_op jit(solution)/shard_map/ppermute | solution.py:17
  73.9 1.9 %copy-start.4 = (bf16[384,2048]{1,0:T(8,128)(2,1)}, bf16[384,2048]{1,0:T(8,128)(2,1)S(1)}, u32[]{:S(2)}) copy-start(bf16[384,2048]{1,0:T(8,128)(2,1)S(1)} %shard_map.70.refs_0_.refs_8_) | copy-start | bytes 4718596
  92.5 1.8 %copy-start.10 = (bf16[384,2048]{1,0:T(8,128)(2,1)}, bf16[384,2048]{1,0:T(8,128)(2,1)S(1)}, u32[]{:S(2)}) copy-start(bf16[384,2048]{1,0:T(8,128)(2,1)S(1)} %collective-permute-done.2.refs_0_.refs_3_) | copy-start | bytes 4718596
  92.5 4.5 %collective-permute-start.8 = (f32[384,384]{1,0:T(8,128)}, f32[384,384]{1,0:T(8,128)}, u32[]{:S(2)}, u32[]{:S(2)}) collective-permute-start(f32[384,384]{1,0:T(8,128)} %shard_map.71.refs_0_), channel_id=1, source_target_pairs={{0,1},{1,0},{2,3},{3,2},{4,5},{5,4},{6,7},{7,6},{8,9},{9,8},{10,11... | collective-permute-start | bytes 1769480 | tf_op jit(solution)/shard_map/ppermute | solution.py:17
  92.5 2.3 %copy-start.6 = (f32[2,384,384]{2,1,0:T(8,128)}, f32[2,384,384]{2,1,0:T(8,128)S(1)}, u32[]{:S(2)}) copy-start(f32[2,384,384]{2,1,0:T(8,128)S(1)} %collective-permute-done.1.refs_1_) | copy-start | bytes 3538948
  94.4 2.4 %copy-start.16 = (s32[1,384]{1,0:T(1,128)S(1)}, s32[1,384]{1,0:T(1,128)}, u32[]{:S(2)}) copy-start(s32[1,384]{1,0:T(1,128)} %param.6) | copy-start | bytes 4612
  94.4 2.7 %collective-permute-start.3 = (f32[1,384,384]{2,1,0:T(8,128)}, f32[1,384,384]{2,1,0:T(8,128)}, u32[]{:S(2)}, u32[]{:S(2)}) collective-permute-start(f32[1,384,384]{2,1,0:T(8,128)} %shard_map.68.refs_2_), channel_id=1, source_target_pairs={{0,1},{1,0},{2,3},{3,2},{4,5},{5,4},{6,7},{7,6},{8,9},{9,8},{10,11... | collective-permute-start | bytes 1769480 | tf_op jit(solution)/shard_map/ppermute | solution.py:17
  94.9 1.8 %copy-start.12 = (bf16[384,2048]{1,0:T(8,128)(2,1)}, bf16[384,2048]{1,0:T(8,128)(2,1)S(1)}, u32[]{:S(2)}) copy-start(bf16[384,2048]{1,0:T(8,128)(2,1)S(1)} %collective-permute-done.4.refs_0_.refs_2_) | copy-start | bytes 4718596
  96.7 2.3 %collective-permute-start.5 = (f32[1,384,384]{2,1,0:T(8,128)}, f32[1,384,384]{2,1,0:T(8,128)}, u32[]{:S(2)}, u32[]{:S(2)}) collective-permute-start(f32[1,384,384]{2,1,0:T(8,128)} %shard_map.69.refs_4_), channel_id=1, source_target_pairs={{0,1},{1,0},{2,3},{3,2},{4,5},{5,4},{6,7},{7,6},{8,9},{9,8},{10,11... | collective-permute-start | bytes 1769480 | tf_op jit(solution)/shard_map/ppermute | solution.py:17
  99.1 1.3 copy-start.7
  100.3 1.3 copy-start.15
  104.6 11.1 %collective-permute-start.10 = (f32[8,384]{1,0:T(8,128)S(1)}, f32[8,384]{1,0:T(8,128)S(1)}, u32[]{:S(2)}, u32[]{:S(2)}) collective-permute-start(f32[8,384]{1,0:T(8,128)S(1)} %get-tuple-element.17.refs_0_), channel_id=1, source_target_pairs={{0,20},{2,22},{4,16},{6,18},{8,28},{10,30},{12,24},{14,26},{16,4},... | collective-permute-start | bytes 36872 | tf_op jit(solution)/shard_map/ppermute | solution.py:17
  104.7 11.0 %collective-permute-start.11 = (f32[8,384]{1,0:T(8,128)S(1)}, f32[8,384]{1,0:T(8,128)S(1)}, u32[]{:S(2)}, u32[]{:S(2)}) collective-permute-start(f32[8,384]{1,0:T(8,128)S(1)} %get-tuple-element.17.refs_0_), channel_id=1, source_target_pairs={{0,28},{2,30},{4,24},{6,26},{8,20},{10,22},{12,16},{14,18},{16,12}... | collective-permute-start | bytes 36872 | tf_op jit(solution)/shard_map/ppermute | solution.py:17
  104.8 10.9 %collective-permute-start.9 = (f32[8,384]{1,0:T(8,128)S(1)}, f32[8,384]{1,0:T(8,128)S(1)}, u32[]{:S(2)}, u32[]{:S(2)}) collective-permute-start(f32[8,384]{1,0:T(8,128)S(1)} %get-tuple-element.17.refs_0_), channel_id=1, source_target_pairs={{0,12},{2,14},{4,8},{6,10},{8,4},{10,6},{12,0},{14,2},{16,28},{18,... | collective-permute-start | bytes 36872 | tf_op jit(solution)/shard_map/ppermute | solution.py:17
  111.7 33.0 %collective-permute-start.15 = (bf16[176,2048]{1,0:T(8,128)(2,1)S(1)}, bf16[176,2048]{1,0:T(8,128)(2,1)S(1)}, u32[]{:S(2)}, u32[]{:S(2)}) collective-permute-start(bf16[176,2048]{1,0:T(8,128)(2,1)S(1)} %shard_map.78), channel_id=1, source_target_pairs={{0,16},{2,18},{4,20},{6,22},{8,24},{10,26},{12,28},{14,30},{16,0},... | collective-permute-start | bytes 2162696 | tf_op jit(solution)/shard_map/ppermute | solution.py:17
  111.8 33.0 %collective-permute-start.17 = (bf16[176,2048]{1,0:T(8,128)(2,1)S(1)}, bf16[176,2048]{1,0:T(8,128)(2,1)S(1)}, u32[]{:S(2)}, u32[]{:S(2)}) collective-permute-start(bf16[176,2048]{1,0:T(8,128)(2,1)S(1)} %shard_map.79), channel_id=1, source_target_pairs={{0,8},{2,10},{4,12},{6,14},{8,0},{10,2},{12,4},{14,6},{16,24},{18,... | collective-permute-start | bytes 2162696 | tf_op jit(solution)/shard_map/ppermute | solution.py:17
  115.7 4.2 %collective-permute-start.12 = (f32[4,8,384]{2,1,0:T(8,128)S(1)}, f32[4,8,384]{2,1,0:T(8,128)S(1)}, u32[]{:S(2)}, u32[]{:S(2)}) collective-permute-start(f32[4,8,384]{2,1,0:T(8,128)S(1)} %shard_map.73.refs_2_), channel_id=1, source_target_pairs={{0,4},{2,6},{4,0},{6,2},{8,12},{10,14},{12,8},{14,10},{16,20},{18,... | collective-permute-start | bytes 147464 | tf_op jit(solution)/shard_map/ppermute | solution.py:17
  118.8 10.4 %collective-permute-start.18 = (f32[208,384]{1,0:T(8,128)S(1)}, f32[208,384]{1,0:T(8,128)S(1)}, u32[]{:S(2)}, u32[]{:S(2)}) collective-permute-start(f32[208,384]{1,0:T(8,128)S(1)} %get-tuple-element.24.refs_2_), channel_id=1, source_target_pairs={{0,1},{1,0},{2,3},{3,2},{4,5},{5,4},{6,7},{7,6},{8,9},{9,8},{10,11... | collective-permute-start | bytes 958472 | tf_op jit(solution)/shard_map/ppermute | solution.py:17
  118.9 10.3 %collective-permute-start.19 = (f32[208,384]{1,0:T(8,128)S(1)}, f32[208,384]{1,0:T(8,128)S(1)}, u32[]{:S(2)}, u32[]{:S(2)}) collective-permute-start(f32[208,384]{1,0:T(8,128)S(1)} %get-tuple-element.25.refs_4_), channel_id=1, source_target_pairs={{0,1},{1,0},{2,3},{3,2},{4,5},{5,4},{6,7},{7,6},{8,9},{9,8},{10,11... | collective-permute-start | bytes 958472 | tf_op jit(solution)/shard_map/ppermute | solution.py:17
  119.9 3.7 %copy-start.9 = (bf16[384,2048]{1,0:T(8,128)(2,1)S(1)}, bf16[384,2048]{1,0:T(8,128)(2,1)}, u32[]{:S(2)}) copy-start(bf16[384,2048]{1,0:T(8,128)(2,1)} %copy-done.8) | copy-start | bytes 4718596
  119.9 3.7 %copy-start.11 = (bf16[384,2048]{1,0:T(8,128)(2,1)S(1)}, bf16[384,2048]{1,0:T(8,128)(2,1)}, u32[]{:S(2)}) copy-start(bf16[384,2048]{1,0:T(8,128)(2,1)} %copy-done.10) | copy-start | bytes 4718596
  119.9 3.7 %copy-start.13 = (bf16[384,2048]{1,0:T(8,128)(2,1)S(1)}, bf16[384,2048]{1,0:T(8,128)(2,1)}, u32[]{:S(2)}) copy-start(bf16[384,2048]{1,0:T(8,128)(2,1)} %copy-done.12) | copy-start | bytes 4718596
  122.1 5.9 %collective-permute-start.13 = (f32[1]{0:T(128)}, f32[1]{0:T(128)}, u32[]{:S(2)}, u32[]{:S(2)}) collective-permute-start(f32[1]{0:T(128)} %bitcast.5), channel_id=1, source_target_pairs={{0,2},{2,0},{4,6},{6,4},{8,10},{10,8},{12,14},{14,12},{16,18},{18,... | collective-permute-start | bytes 20 | tf_op jit(solution)/shard_map/ppermute | solution.py:17
  123.6 5.7 %copy-start.5 = (bf16[384,2048]{1,0:T(8,128)(2,1)S(1)}, bf16[384,2048]{1,0:T(8,128)(2,1)}, u32[]{:S(2)}) copy-start(bf16[384,2048]{1,0:T(8,128)(2,1)} %copy-done.4) | copy-start | bytes 4718596
  146.0 2.0 %collective-permute-start.20 = (f32[2,176,384]{2,1,0:T(8,128)S(1)}, f32[2,176,384]{2,1,0:T(8,128)S(1)}, u32[]{:S(2)}, u32[]{:S(2)}) collective-permute-start(f32[2,176,384]{2,1,0:T(8,128)S(1)} %shard_map.82.refs_0_), channel_id=1, source_target_pairs={{0,1},{1,0},{2,3},{3,2},{4,5},{5,4},{6,7},{7,6},{8,9},{9,8},{10,11... | collective-permute-start | bytes 1622024 | tf_op jit(solution)/shard_map/ppermute | solution.py:17

commit v7 on v3

--- a/solution.py
+++ b/solution.py
@@ -349,7 +349,7 @@
     active = pair_on[me]
     place = positive.reshape(rows, 1)
 
-    first = 13 * rows // 24
+    first = rows // 2
     upper = list(reversed(range(1, levels)))
     far_p = [None] * levels
     for k in reversed(range(levels)):
@@ -416,7 +416,7 @@
         ),
         [active, tiles, row_lse, place, *packs],
         scalars=1,
-        flops=4715000000,
+        flops=5405000000,
     )
     total = total[0, :1]
     for bit in range(low):

time: 152 us -> 152 us (level)
  no operation moved by 1% of the time
where the time goes in v7:
time: 152 us
  waiting for transfers between devices  90.5 us (60%)
  Pallas kernels  28.1 us (18%)
  starting transfers between devices  22.2 us (15%)
  local copies, waits for them, and re-layouts  7.45 us (5%)
  between operations  3.3 us (2%)
    ppermute x21, waiting for transfers between devices, exchanged(): return lax.ppermute(block, axis, [(i, i ^ offset) for i in range(count)])  90.5 us
    pallas_call x16, Pallas kernels, call(): pl.pallas_call(kernel, out_shape=out_shape, compiler_params=pltpu.Compile...  28.1 us
    ppermute x21, starting transfers between devices, exchanged(): return lax.ppermute(block, axis, [(i, i ^ offset) for i in range(count)])  22.2 us
    unnamed x34, local copies, waits for them, and re-layouts  5.14 us
  transfers between devices with their start and end apart: 21, of which 10 were waited for; matrix products, arithmetic and copies ran while one was open for 2% of the time, Pallas kernels for 16%

profile of v7, /device:TPU:0, one launch (start us, length us, event | category | flops | bytes accessed | tf_op | source)
XLA Modules:
  0.0 151.5 jit_solution(9388198032083502931)
XLA Ops:
  0.7 3.0 %collective-permute-start = (bf16[384,2048]{1,0:T(8,128)(2,1)}, bf16[384,2048]{1,0:T(8,128)(2,1)S(1)}, u32[]{:S(2)}, u32[]{:S(2)}) collective-permute-start(bf16[384,2048]{1,0:T(8,128)(2,1)} %right_ref.5), channel_id=1, source_target_pairs={{0,4},{2,6},{4,0},{6,2},{8,12},{10,14},{12,8},{14,10},{16,20},{18,... | collective-permute-start | bytes 4718600 | tf_op jit(solution)/shard_map/ppermute | solution.py:17
  3.7 2.6 %collective-permute-start.2 = (bf16[384,2048]{1,0:T(8,128)(2,1)}, bf16[384,2048]{1,0:T(8,128)(2,1)S(1)}, u32[]{:S(2)}, u32[]{:S(2)}) collective-permute-start(bf16[384,2048]{1,0:T(8,128)(2,1)} %right_ref.5), channel_id=1, source_target_pairs={{0,16},{2,18},{4,20},{6,22},{8,24},{10,26},{12,28},{14,30},{16,0},... | collective-permute-start | bytes 4718600 | tf_op jit(solution)/shard_map/ppermute | solution.py:17
  6.3 1.6 %collective-permute-start.4 = (bf16[384,2048]{1,0:T(8,128)(2,1)}, bf16[384,2048]{1,0:T(8,128)(2,1)S(1)}, u32[]{:S(2)}, u32[]{:S(2)}) collective-permute-start(bf16[384,2048]{1,0:T(8,128)(2,1)} %right_ref.5), channel_id=1, source_target_pairs={{0,8},{2,10},{4,12},{6,14},{8,0},{10,2},{12,4},{14,6},{16,24},{18,... | collective-permute-start | bytes 4718600 | tf_op jit(solution)/shard_map/ppermute | solution.py:17
  7.9 1.4 slice.21
  9.3 0.6 collective-permute-start.6
  9.9 29.2 %collective-permute-done.refs_1_ = bf16[384,2048]{1,0:T(8,128)(2,1)S(1)} collective-permute-done((bf16[384,2048]{1,0:T(8,128)(2,1)}, bf16[384,2048]{1,0:T(8,128)(2,1)S(1)}, u32[]{:S(2)}, u32[]{:S(2)}) %collective-permute-start) | collective-permute-done | bytes 1572896 | tf_op jit(solution)/shard_map/ppermute | solution.py:17
  39.1 1.4 copy-done.2
  40.5 1.8 %shard_map.67.refs_0_ = f32[2,384,384]{2,1,0:T(8,128)S(1)} custom-call(bf16[384,2048]{1,0:T(8,128)(2,1)S(1)} %copy-done.1, bf16[384,2048]{1,0:T(8,128)(2,1)S(1)} %copy-done.2, bf16[384,2048]{1,0:T(8,128)(2,1)S(1)} %collective-permute-done.refs_1_), custom_call_target="tpu_custom_call" | custom-call | tf_op jit(solution)/shard_map/pallas_call | solution.py:32
  42.4 1.1 copy-done.8
  43.5 2.1 %collective-permute-start.7 = (bf16[64,2048]{1,0:T(8,128)(2,1)S(1)}, bf16[64,2048]{1,0:T(8,128)(2,1)S(1)}, u32[]{:S(2)}, u32[]{:S(2)}) collective-permute-start(bf16[64,2048]{1,0:T(8,128)(2,1)S(1)} %slice.22), channel_id=1, source_target_pairs={{0,4},{2,6},{4,0},{6,2},{8,12},{10,14},{12,8},{14,10},{16,20},{18,... | collective-permute-start | bytes 786440 | tf_op jit(solution)/shard_map/ppermute | solution.py:17
  45.6 1.0 shard_map.76.refs_0_
  46.6 20.6 %collective-permute-done.6.upper_ref.refs_1_ = bf16[320,2048]{1,0:T(8,128)(2,1)S(1)} collective-permute-done((bf16[320,2048]{1,0:T(8,128)(2,1)S(1)}, bf16[320,2048]{1,0:T(8,128)(2,1)S(1)}, u32[]{:S(2)}, u32[]{:S(2)}) %collective-permute-start.6) | collective-permute-done | bytes 1310752 | tf_op jit(solution)/shard_map/ppermute | solution.py:17
  67.2 3.1 %collective-permute-start.14 = (bf16[192,2048]{1,0:T(8,128)(2,1)}, bf16[192,2048]{1,0:T(8,128)(2,1)}, u32[]{:S(2)}, u32[]{:S(2)}) collective-permute-start(bf16[192,2048]{1,0:T(8,128)(2,1)} %shard_map.77), channel_id=1, source_target_pairs={{0,16},{2,18},{4,20},{6,22},{8,24},{10,26},{12,28},{14,30},{16,0},... | collective-permute-start | bytes 2359304 | tf_op jit(solution)/shard_map/ppermute | solution.py:17
  70.3 1.7 %collective-permute-done.7.lower_ref = bf16[64,2048]{1,0:T(8,128)(2,1)S(1)} collective-permute-done((bf16[64,2048]{1,0:T(8,128)(2,1)S(1)}, bf16[64,2048]{1,0:T(8,128)(2,1)S(1)}, u32[]{:S(2)}, u32[]{:S(2)}) %collective-permute-start.7) | collective-permute-done | bytes 262176 | tf_op jit(solution)/shard_map/ppermute | solution.py:17
  72.0 1.8 %collective-permute-start.16 = (bf16[192,2048]{1,0:T(8,128)(2,1)}, bf16[192,2048]{1,0:T(8,128)(2,1)}, u32[]{:S(2)}, u32[]{:S(2)}) collective-permute-start(bf16[192,2048]{1,0:T(8,128)(2,1)} %shard_map.77), channel_id=1, source_target_pairs={{0,8},{2,10},{4,12},{6,14},{8,0},{10,2},{12,4},{14,6},{16,24},{18,... | collective-permute-start | bytes 2359304 | tf_op jit(solution)/shard_map/ppermute | solution.py:17
  73.8 0.1 shard_map.70.refs_0_.refs_8_
  73.9 1.8 %shard_map.71.refs_0_ = f32[384,384]{1,0:T(8,128)} custom-call(bf16[384,2048]{1,0:T(8,128)(2,1)S(1)} %copy-done.3, bf16[384,2048]{1,0:T(8,128)(2,1)S(1)} %shard_map.70.refs_0_.refs_8_), custom_call_target="tpu_custom_call" | custom-call | tf_op jit(solution)/shard_map/pallas_call | solution.py:32
  75.8 15.4 %collective-permute-done.2.refs_0_.refs_3_ = bf16[384,2048]{1,0:T(8,128)(2,1)S(1)} collective-permute-done((bf16[384,2048]{1,0:T(8,128)(2,1)}, bf16[384,2048]{1,0:T(8,128)(2,1)S(1)}, u32[]{:S(2)}, u32[]{:S(2)}) %collective-permute-start.2) | collective-permute-done | bytes 1572896 | tf_op jit(solution)/shard_map/ppermute | solution.py:17
  91.2 1.8 %shard_map.68.refs_2_ = f32[1,384,384]{2,1,0:T(8,128)} custom-call(bf16[384,2048]{1,0:T(8,128)(2,1)S(1)} %copy-done.1, bf16[384,2048]{1,0:T(8,128)(2,1)S(1)} %collective-permute-done.2.refs_0_.refs_3_, f32[2,384,384]{2,1,0:T(8,128)S(1)} %collective-permute-done.1.refs_1_), custom_call_target="tpu_custom_call" | custom-call | tf_op jit(solution)/shard_map/pallas_call | solution.py:32
  93.0 0.5 collective-permute-start.3
  93.5 1.8 %shard_map.69.refs_4_ = f32[1,384,384]{2,1,0:T(8,128)} custom-call(bf16[384,2048]{1,0:T(8,128)(2,1)S(1)} %copy-done.1, bf16[384,2048]{1,0:T(8,128)(2,1)S(1)} %collective-permute-done.4.refs_0_.refs_2_, f32[2,384,384]{2,1,0:T(8,128)S(1)} %collective-permute-done.1.refs_1_), custom_call_target="tpu_custom_call" | custom-call | tf_op jit(solution)/shard_map/pallas_call | solution.py:32
  95.3 0.1 copy.8.refs_6_.pos_ref
  95.5 0.2 dynamic-slice_reduce_fusion.act_ref
  95.7 2.0 %collective-permute-done.5.refs_5_ = f32[1,384,384]{2,1,0:T(8,128)} collective-permute-done((f32[1,384,384]{2,1,0:T(8,128)}, f32[1,384,384]{2,1,0:T(8,128)}, u32[]{:S(2)}, u32[]{:S(2)}) %collective-permute-start.5) | collective-permute-done | bytes 589856 | tf_op jit(solution)/shard_map/ppermute | solution.py:17
  97.7 1.3 copy-done.7
  98.9 1.3 copy-done.15
  100.2 3.0 %shard_map.72 = (f32[4,384,384]{2,1,0:T(8,128)S(1)}, f32[384,1]{1,0:T(8,128)S(1)}, f32[8,384]{1,0:T(8,128)S(1)}) custom-call(s32[3]{0:T(128)S(1)} %dynamic-slice_reduce_fusion.act_ref, f32[2,384,384]{2,1,0:T(8,128)S(1)} %copy-done.15, f32[2,384,384]{2,1,0:T(8,128)S(1)} %copy-done.7, f32[1,384,384]{2,1,0:T(8,128)} %shard_map.68.refs_2_, ...), custom_call_target="tpu_custom_call" | custom-call | tf_op jit(solution)/shard_map/pallas_call | solution.py:32
  103.2 0.1 collective-permute-start.10
  103.4 0.1 collective-permute-start.9
  103.4 5.4 %collective-permute-done.14.refs_1_.refs_0_.refs_9_ = bf16[192,2048]{1,0:T(8,128)(2,1)} collective-permute-done((bf16[192,2048]{1,0:T(8,128)(2,1)}, bf16[192,2048]{1,0:T(8,128)(2,1)}, u32[]{:S(2)}, u32[]{:S(2)}) %collective-permute-start.14) | collective-permute-done | bytes 786464 | tf_op jit(solution)/shard_map/ppermute | solution.py:17
  108.9 0.1 collective-permute-start.15
  109.0 3.9 %collective-permute-start.17 = (bf16[192,2048]{1,0:T(8,128)(2,1)S(1)}, bf16[192,2048]{1,0:T(8,128)(2,1)S(1)}, u32[]{:S(2)}, u32[]{:S(2)}) collective-permute-start(bf16[192,2048]{1,0:T(8,128)(2,1)S(1)} %shard_map.79), channel_id=1, source_target_pairs={{0,8},{2,10},{4,12},{6,14},{8,0},{10,2},{12,4},{14,6},{16,24},{18,... | collective-permute-start | bytes 2359304 | tf_op jit(solution)/shard_map/ppermute | solution.py:17
  112.9 0.6 collective-permute-start.12
  113.5 2.5 %shard_map.80 = (f32[192,384]{1,0:T(8,128)S(1)}, f32[192,384]{1,0:T(8,128)S(1)}) custom-call(bf16[384,2048]{1,0:T(8,128)(2,1)S(1)} %copy-done.3, bf16[192,2048]{1,0:T(8,128)(2,1)} %collective-permute-done.14.refs_1_.refs_0_.refs_9_, bf16[192,2048]{1,0:T(8,128)(2,1)} %collective-permute-done.16.refs_1_.refs_10_, f32[4,8,384]{2,1,0:T(8,128)S(1)} %shard_map.73.refs_2_), custom_call_target="tpu_custom_call" | custom-call | tf_op jit(solution)/shard_map/pallas_call | solution.py:32
  116.0 0.1 collective-permute-start.18
  116.1 0.5 collective-permute-start.19
  116.6 0.5 collective-permute-done.12
  117.1 1.7 %shard_map.74 = (bf16[4,384,384]{2,1,0:T(8,128)(2,1)S(1)}, bf16[384,384]{1,0:T(8,128)(2,1)S(1)}, f32[8,384]{1,0:T(8,128)S(1)}, f32[384,8]{1,0:T(8,128)S(1)}, f32[8,128]{1,0:T(8,128)S(1)}) custom-call(s32[3]{0:T(128)S(1)} %dynamic-slice_reduce_fusion.act_ref, f32[4,384,384]{2,1,0:T(8,128)S(1)} %get-tuple-element.15.tile_ref, ...), custom_call_target="tpu_custom_call" | custom-call | flops 5405000192 | tf_op jit(solution)/shard_map/pallas_call | solution.py:32
  118.7 0.5 slice.27
  119.3 1.5 collective-permute-start.13
  120.8 4.3 %shard_map.75 = (f32[384,2048]{1,0:T(8,128)}, f32[8,128]{1,0:T(8,128)S(1)}) custom-call(bf16[4,384,384]{2,1,0:T(8,128)(2,1)S(1)} %get-tuple-element.19.grad_ref, bf16[384,2048]{1,0:T(8,128)(2,1)S(1)} %copy-done.3, bf16[384,2048]{1,0:T(8,128)(2,1)S(1)} %copy-done.9, bf16[384,2048]{1,0:T(8,128)(2,1)S(1)} %copy-done.13, bf16[384,2048]{1,0:T(8,128)(2,1)S(1)} %copy-done.11), custom_call_target="tpu_custom_call" | custom-call | tf_op jit(solution)/shard_map/pallas_call | solution.py:32
  126.4 4.6 %shard_map.81.refs_3_.refs_2_ = f32[384,2048]{1,0:T(8,128)S(1)} custom-call(f32[8,384]{1,0:T(8,128)S(1)} %get-tuple-element.21.col_ref, f32[384,8]{1,0:T(8,128)S(1)} %get-tuple-element.22.far_ref, f32[384,384]{1,0:T(8,128)} %shard_map.71.refs_0_, f32[384,384]{1,0:T(8,128)} %collective-permute-done.8.refs_7_.refs_1_, ...), custom_call_target="tpu_custom_call" | custom-call | tf_op jit(solution)/shard_map/pallas_call | solution.py:32
  131.0 13.7 %collective-permute-done.15.refs_0_.refs_3_ = bf16[192,2048]{1,0:T(8,128)(2,1)S(1)} collective-permute-done((bf16[192,2048]{1,0:T(8,128)(2,1)S(1)}, bf16[192,2048]{1,0:T(8,128)(2,1)S(1)}, u32[]{:S(2)}, u32[]{:S(2)}) %collective-permute-start.15) | collective-permute-done | bytes 786464 | tf_op jit(solution)/shard_map/ppermute | solution.py:17
  144.7 0.2 collective-permute-done.17.refs_1_.refs_4_
  144.9 1.1 shard_map.82.refs_0_
  146.0 0.1 collective-permute-start.20
  146.1 2.0 %collective-permute-done.20.refs_1_ = f32[2,192,384]{2,1,0:T(8,128)S(1)} collective-permute-done((f32[2,192,384]{2,1,0:T(8,128)S(1)}, f32[2,192,384]{2,1,0:T(8,128)S(1)}, u32[]{:S(2)}, u32[]{:S(2)}) %collective-permute-start.20) | collective-permute-done | bytes 589856 | tf_op jit(solution)/shard_map/ppermute | solution.py:17
  148.1 2.3 %shard_map.83 = f32[384,2048]{1,0:T(8,128)} custom-call(f32[8,384]{1,0:T(8,128)S(1)} %get-tuple-element.21.col_ref, f32[384,8]{1,0:T(8,128)S(1)} %get-tuple-element.22.far_ref, f32[2,192,384]{2,1,0:T(8,128)S(1)} %shard_map.82.refs_0_, f32[2,192,384]{2,1,0:T(8,128)S(1)} %collective-permute-done.20.refs_1_, f32[384,2048]{1,0:T(8,128)S(1)} %shard_map.81.refs_3_.refs_2_, ...), custom_call_target="tpu_custom_call" | custom-call | tf_op jit(solution)/shard_map/pallas_call | solution.py:32
  (51 shorter events, 0.3 us)
Async XLA Ops:
  0.6 94.9 %copy-start = (s32[16,3]{0,1:T(4,128)S(1)}, s32[16,3]{0,1:T(4,128)}, u32[]{:S(2)}) copy-start(s32[16,3]{0,1:T(4,128)} %param.7) | copy-start | bytes 580
  0.6 38.5 %copy-start.1 = (bf16[384,2048]{1,0:T(8,128)(2,1)S(1)}, bf16[384,2048]{1,0:T(8,128)(2,1)}, u32[]{:S(2)}) copy-start(bf16[384,2048]{1,0:T(8,128)(2,1)} %refs_7_.1) | copy-start | bytes 4718596
  0.7 38.5 %collective-permute-start = (bf16[384,2048]{1,0:T(8,128)(2,1)}, bf16[384,2048]{1,0:T(8,128)(2,1)S(1)}, u32[]{:S(2)}, u32[]{:S(2)}) collective-permute-start(bf16[384,2048]{1,0:T(8,128)(2,1)} %right_ref.5), channel_id=1, source_target_pairs={{0,4},{2,6},{4,0},{6,2},{8,12},{10,14},{12,8},{14,10},{16,20},{18,... | collective-permute-start | bytes 4718600 | tf_op jit(solution)/shard_map/ppermute | solution.py:17
  3.7 87.4 %collective-permute-start.2 = (bf16[384,2048]{1,0:T(8,128)(2,1)}, bf16[384,2048]{1,0:T(8,128)(2,1)S(1)}, u32[]{:S(2)}, u32[]{:S(2)}) collective-permute-start(bf16[384,2048]{1,0:T(8,128)(2,1)} %right_ref.5), channel_id=1, source_target_pairs={{0,16},{2,18},{4,20},{6,22},{8,24},{10,26},{12,28},{14,30},{16,0},... | collective-permute-start | bytes 4718600 | tf_op jit(solution)/shard_map/ppermute | solution.py:17
  6.3 87.2 %collective-permute-start.4 = (bf16[384,2048]{1,0:T(8,128)(2,1)}, bf16[384,2048]{1,0:T(8,128)(2,1)S(1)}, u32[]{:S(2)}, u32[]{:S(2)}) collective-permute-start(bf16[384,2048]{1,0:T(8,128)(2,1)} %right_ref.5), channel_id=1, source_target_pairs={{0,8},{2,10},{4,12},{6,14},{8,0},{10,2},{12,4},{14,6},{16,24},{18,... | collective-permute-start | bytes 4718600 | tf_op jit(solution)/shard_map/ppermute | solution.py:17
  9.3 57.9 %collective-permute-start.6 = (bf16[320,2048]{1,0:T(8,128)(2,1)S(1)}, bf16[320,2048]{1,0:T(8,128)(2,1)S(1)}, u32[]{:S(2)}, u32[]{:S(2)}) collective-permute-start(bf16[320,2048]{1,0:T(8,128)(2,1)S(1)} %slice.21), channel_id=1, source_target_pairs={{0,4},{2,6},{4,0},{6,2},{8,12},{10,14},{12,8},{14,10},{16,20},{18,... | collective-permute-start | bytes 3932168 | tf_op jit(solution)/shard_map/ppermute | solution.py:17
  39.1 1.4 copy-start.2
  42.3 1.1 copy-start.8
  43.5 23.7 %copy-start.14 = (f32[2,384,384]{2,1,0:T(8,128)}, f32[2,384,384]{2,1,0:T(8,128)S(1)}, u32[]{:S(2)}) copy-start(f32[2,384,384]{2,1,0:T(8,128)S(1)} %shard_map.67.refs_0_) | copy-start | bytes 3538948
  43.5 47.7 %collective-permute-start.1 = (f32[2,384,384]{2,1,0:T(8,128)S(1)}, f32[2,384,384]{2,1,0:T(8,128)S(1)}, u32[]{:S(2)}, u32[]{:S(2)}) collective-permute-start(f32[2,384,384]{2,1,0:T(8,128)S(1)} %shard_map.67.refs_0_), channel_id=1, source_target_pairs={{0,1},{1,0},{2,3},{3,2},{4,5},{5,4},{6,7},{7,6},{8,9},{9,8},{10,11... | collective-permute-start | bytes 3538952 | tf_op jit(solution)/shard_map/ppermute | solution.py:17
  43.5 28.5 %collective-permute-start.7 = (bf16[64,2048]{1,0:T(8,128)(2,1)S(1)}, bf16[64,2048]{1,0:T(8,128)(2,1)S(1)}, u32[]{:S(2)}, u32[]{:S(2)}) collective-permute-start(bf16[64,2048]{1,0:T(8,128)(2,1)S(1)} %slice.22), channel_id=1, source_target_pairs={{0,4},{2,6},{4,0},{6,2},{8,12},{10,14},{12,8},{14,10},{16,20},{18,... | collective-permute-start | bytes 786440 | tf_op jit(solution)/shard_map/ppermute | solution.py:17
  67.2 6.7 %copy-start.3 = (bf16[384,2048]{1,0:T(8,128)(2,1)S(1)}, bf16[384,2048]{1,0:T(8,128)(2,1)}, u32[]{:S(2)}) copy-start(bf16[384,2048]{1,0:T(8,128)(2,1)} %right_ref.5) | copy-start | bytes 4718596
  67.2 41.6 %collective-permute-start.14 = (bf16[192,2048]{1,0:T(8,128)(2,1)}, bf16[192,2048]{1,0:T(8,128)(2,1)}, u32[]{:S(2)}, u32[]{:S(2)}) collective-permute-start(bf16[192,2048]{1,0:T(8,128)(2,1)} %shard_map.77), channel_id=1, source_target_pairs={{0,16},{2,18},{4,20},{6,22},{8,24},{10,26},{12,28},{14,30},{16,0},... | collective-permute-start | bytes 2359304 | tf_op jit(solution)/shard_map/ppermute | solution.py:17
  72.0 36.9 %collective-permute-start.16 = (bf16[192,2048]{1,0:T(8,128)(2,1)}, bf16[192,2048]{1,0:T(8,128)(2,1)}, u32[]{:S(2)}, u32[]{:S(2)}) collective-permute-start(bf16[192,2048]{1,0:T(8,128)(2,1)} %shard_map.77), channel_id=1, source_target_pairs={{0,8},{2,10},{4,12},{6,14},{8,0},{10,2},{12,4},{14,6},{16,24},{18,... | collective-permute-start | bytes 2359304 | tf_op jit(solution)/shard_map/ppermute | solution.py:17
  73.9 1.9 %copy-start.4 = (bf16[384,2048]{1,0:T(8,128)(2,1)}, bf16[384,2048]{1,0:T(8,128)(2,1)S(1)}, u32[]{:S(2)}) copy-start(bf16[384,2048]{1,0:T(8,128)(2,1)S(1)} %shard_map.70.refs_0_.refs_8_) | copy-start | bytes 4718596
  91.1 1.8 %copy-start.10 = (bf16[384,2048]{1,0:T(8,128)(2,1)}, bf16[384,2048]{1,0:T(8,128)(2,1)S(1)}, u32[]{:S(2)}) copy-start(bf16[384,2048]{1,0:T(8,128)(2,1)S(1)} %collective-permute-done.2.refs_0_.refs_3_) | copy-start | bytes 4718596
  91.1 4.6 %collective-permute-start.8 = (f32[384,384]{1,0:T(8,128)}, f32[384,384]{1,0:T(8,128)}, u32[]{:S(2)}, u32[]{:S(2)}) collective-permute-start(f32[384,384]{1,0:T(8,128)} %shard_map.71.refs_0_), channel_id=1, source_target_pairs={{0,1},{1,0},{2,3},{3,2},{4,5},{5,4},{6,7},{7,6},{8,9},{9,8},{10,11... | collective-permute-start | bytes 1769480 | tf_op jit(solution)/shard_map/ppermute | solution.py:17
  91.1 2.3 %copy-start.6 = (f32[2,384,384]{2,1,0:T(8,128)}, f32[2,384,384]{2,1,0:T(8,128)S(1)}, u32[]{:S(2)}) copy-start(f32[2,384,384]{2,1,0:T(8,128)S(1)} %collective-permute-done.1.refs_1_) | copy-start | bytes 3538948
  93.0 2.4 %copy-start.16 = (s32[1,384]{1,0:T(1,128)S(1)}, s32[1,384]{1,0:T(1,128)}, u32[]{:S(2)}) copy-start(s32[1,384]{1,0:T(1,128)} %param.6) | copy-start | bytes 4612
  93.0 2.7 %collective-permute-start.3 = (f32[1,384,384]{2,1,0:T(8,128)}, f32[1,384,384]{2,1,0:T(8,128)}, u32[]{:S(2)}, u32[]{:S(2)}) collective-permute-start(f32[1,384,384]{2,1,0:T(8,128)} %shard_map.68.refs_2_), channel_id=1, source_target_pairs={{0,1},{1,0},{2,3},{3,2},{4,5},{5,4},{6,7},{7,6},{8,9},{9,8},{10,11... | collective-permute-start | bytes 1769480 | tf_op jit(solution)/shard_map/ppermute | solution.py:17
  93.5 1.8 %copy-start.12 = (bf16[384,2048]{1,0:T(8,128)(2,1)}, bf16[384,2048]{1,0:T(8,128)(2,1)S(1)}, u32[]{:S(2)}) copy-start(bf16[384,2048]{1,0:T(8,128)(2,1)S(1)} %collective-permute-done.4.refs_0_.refs_2_) | copy-start | bytes 4718596
  95.3 2.3 %collective-permute-start.5 = (f32[1,384,384]{2,1,0:T(8,128)}, f32[1,384,384]{2,1,0:T(8,128)}, u32[]{:S(2)}, u32[]{:S(2)}) collective-permute-start(f32[1,384,384]{2,1,0:T(8,128)} %shard_map.69.refs_4_), channel_id=1, source_target_pairs={{0,1},{1,0},{2,3},{3,2},{4,5},{5,4},{6,7},{7,6},{8,9},{9,8},{10,11... | collective-permute-start | bytes 1769480 | tf_op jit(solution)/shard_map/ppermute | solution.py:17
  97.7 1.3 copy-start.7
  98.9 1.3 copy-start.15
  103.2 9.7 %collective-permute-start.10 = (f32[8,384]{1,0:T(8,128)S(1)}, f32[8,384]{1,0:T(8,128)S(1)}, u32[]{:S(2)}, u32[]{:S(2)}) collective-permute-start(f32[8,384]{1,0:T(8,128)S(1)} %get-tuple-element.17.refs_0_), channel_id=1, source_target_pairs={{0,20},{2,22},{4,16},{6,18},{8,28},{10,30},{12,24},{14,26},{16,4},... | collective-permute-start | bytes 36872 | tf_op jit(solution)/shard_map/ppermute | solution.py:17
  103.3 9.6 %collective-permute-start.11 = (f32[8,384]{1,0:T(8,128)S(1)}, f32[8,384]{1,0:T(8,128)S(1)}, u32[]{:S(2)}, u32[]{:S(2)}) collective-permute-start(f32[8,384]{1,0:T(8,128)S(1)} %get-tuple-element.17.refs_0_), channel_id=1, source_target_pairs={{0,28},{2,30},{4,24},{6,26},{8,20},{10,22},{12,16},{14,18},{16,12}... | collective-permute-start | bytes 36872 | tf_op jit(solution)/shard_map/ppermute | solution.py:17
  103.4 9.5 %collective-permute-start.9 = (f32[8,384]{1,0:T(8,128)S(1)}, f32[8,384]{1,0:T(8,128)S(1)}, u32[]{:S(2)}, u32[]{:S(2)}) collective-permute-start(f32[8,384]{1,0:T(8,128)S(1)} %get-tuple-element.17.refs_0_), channel_id=1, source_target_pairs={{0,12},{2,14},{4,8},{6,10},{8,4},{10,6},{12,0},{14,2},{16,28},{18,... | collective-permute-start | bytes 36872 | tf_op jit(solution)/shard_map/ppermute | solution.py:17
  108.9 35.8 %collective-permute-start.15 = (bf16[192,2048]{1,0:T(8,128)(2,1)S(1)}, bf16[192,2048]{1,0:T(8,128)(2,1)S(1)}, u32[]{:S(2)}, u32[]{:S(2)}) collective-permute-start(bf16[192,2048]{1,0:T(8,128)(2,1)S(1)} %shard_map.78), channel_id=1, source_target_pairs={{0,16},{2,18},{4,20},{6,22},{8,24},{10,26},{12,28},{14,30},{16,0},... | collective-permute-start | bytes 2359304 | tf_op jit(solution)/shard_map/ppermute | solution.py:17
  109.0 35.8 %collective-permute-start.17 = (bf16[192,2048]{1,0:T(8,128)(2,1)S(1)}, bf16[192,2048]{1,0:T(8,128)(2,1)S(1)}, u32[]{:S(2)}, u32[]{:S(2)}) collective-permute-start(bf16[192,2048]{1,0:T(8,128)(2,1)S(1)} %shard_map.79), channel_id=1, source_target_pairs={{0,8},{2,10},{4,12},{6,14},{8,0},{10,2},{12,4},{14,6},{16,24},{18,... | collective-permute-start | bytes 2359304 | tf_op jit(solution)/shard_map/ppermute | solution.py:17
  112.9 4.2 %collective-permute-start.12 = (f32[4,8,384]{2,1,0:T(8,128)S(1)}, f32[4,8,384]{2,1,0:T(8,128)S(1)}, u32[]{:S(2)}, u32[]{:S(2)}) collective-permute-start(f32[4,8,384]{2,1,0:T(8,128)S(1)} %shard_map.73.refs_2_), channel_id=1, source_target_pairs={{0,4},{2,6},{4,0},{6,2},{8,12},{10,14},{12,8},{14,10},{16,20},{18,... | collective-permute-start | bytes 147464 | tf_op jit(solution)/shard_map/ppermute | solution.py:17
  116.0 10.4 %collective-permute-start.18 = (f32[192,384]{1,0:T(8,128)S(1)}, f32[192,384]{1,0:T(8,128)S(1)}, u32[]{:S(2)}, u32[]{:S(2)}) collective-permute-start(f32[192,384]{1,0:T(8,128)S(1)} %get-tuple-element.24.refs_2_), channel_id=1, source_target_pairs={{0,1},{1,0},{2,3},{3,2},{4,5},{5,4},{6,7},{7,6},{8,9},{9,8},{10,11... | collective-permute-start | bytes 884744 | tf_op jit(solution)/shard_map/ppermute | solution.py:17
  116.1 10.3 %collective-permute-start.19 = (f32[192,384]{1,0:T(8,128)S(1)}, f32[192,384]{1,0:T(8,128)S(1)}, u32[]{:S(2)}, u32[]{:S(2)}) collective-permute-start(f32[192,384]{1,0:T(8,128)S(1)} %get-tuple-element.25.refs_4_), channel_id=1, source_target_pairs={{0,1},{1,0},{2,3},{3,2},{4,5},{5,4},{6,7},{7,6},{8,9},{9,8},{10,11... | collective-permute-start | bytes 884744 | tf_op jit(solution)/shard_map/ppermute | solution.py:17
  117.1 3.7 %copy-start.9 = (bf16[384,2048]{1,0:T(8,128)(2,1)S(1)}, bf16[384,2048]{1,0:T(8,128)(2,1)}, u32[]{:S(2)}) copy-start(bf16[384,2048]{1,0:T(8,128)(2,1)} %copy-done.8) | copy-start | bytes 4718596
  117.1 3.7 %copy-start.11 = (bf16[384,2048]{1,0:T(8,128)(2,1)S(1)}, bf16[384,2048]{1,0:T(8,128)(2,1)}, u32[]{:S(2)}) copy-start(bf16[384,2048]{1,0:T(8,128)(2,1)} %copy-done.10) | copy-start | bytes 4718596
  117.1 3.7 %copy-start.13 = (bf16[384,2048]{1,0:T(8,128)(2,1)S(1)}, bf16[384,2048]{1,0:T(8,128)(2,1)}, u32[]{:S(2)}) copy-start(bf16[384,2048]{1,0:T(8,128)(2,1)} %copy-done.12) | copy-start | bytes 4718596
  119.3 5.8 %collective-permute-start.13 = (f32[1]{0:T(128)}, f32[1]{0:T(128)}, u32[]{:S(2)}, u32[]{:S(2)}) collective-permute-start(f32[1]{0:T(128)} %bitcast.5), channel_id=1, source_target_pairs={{0,2},{2,0},{4,6},{6,4},{8,10},{10,8},{12,14},{14,12},{16,18},{18,... | collective-permute-start | bytes 20 | tf_op jit(solution)/shard_map/ppermute | solution.py:17
  120.8 5.6 %copy-start.5 = (bf16[384,2048]{1,0:T(8,128)(2,1)S(1)}, bf16[384,2048]{1,0:T(8,128)(2,1)}, u32[]{:S(2)}) copy-start(bf16[384,2048]{1,0:T(8,128)(2,1)} %copy-done.4) | copy-start | bytes 4718596
  146.0 2.1 %collective-permute-start.20 = (f32[2,192,384]{2,1,0:T(8,128)S(1)}, f32[2,192,384]{2,1,0:T(8,128)S(1)}, u32[]{:S(2)}, u32[]{:S(2)}) collective-permute-start(f32[2,192,384]{2,1,0:T(8,128)S(1)} %shard_map.82.refs_0_), channel_id=1, source_target_pairs={{0,1},{1,0},{2,3},{3,2},{4,5},{5,4},{6,7},{7,6},{8,9},{9,8},{10,11... | collective-permute-start | bytes 1769480 | tf_op jit(solution)/shard_map/ppermute | solution.py:17

commit v8 on v3

--- a/solution.py
+++ b/solution.py
@@ -32,7 +32,7 @@
     return pl.pallas_call(
         kernel,
         out_shape=out_shape,
-        compiler_params=pltpu.CompilerParams(vmem_limit_bytes=12 * 1024 * 1024),
+        compiler_params=pltpu.CompilerParams(vmem_limit_bytes=8 * 1024 * 1024),
         cost_estimate=pl.CostEstimate(flops=flops, bytes_accessed=0, transcendentals=0),
         **kwargs,
     )(*operands)

time: 152 us -> 152 us (level)
  no operation moved by 1% of the time
where the time goes in v8:
time: 152 us; the launch traced here: 151 us
  waiting for transfers between devices  91.1 us (60%)
  Pallas kernels  28.4 us (19%)
  starting transfers between devices  22.2 us (15%)
  local copies, waits for them, and re-layouts  6.32 us (4%)
  between operations  3.35 us (2%)
    ppermute x21, waiting for transfers between devices, exchanged(): return lax.ppermute(block, axis, [(i, i ^ offset) for i in range(count)])  91.1 us
    pallas_call x16, Pallas kernels, call(): pl.pallas_call(kernel, out_shape=out_shape, compiler_params=pltpu.Compile...  28.4 us
    ppermute x21, starting transfers between devices, exchanged(): return lax.ppermute(block, axis, [(i, i ^ offset) for i in range(count)])  22.2 us
    unnamed x34, local copies, waits for them, and re-layouts  4.01 us
  transfers between devices with their start and end apart: 21, of which 10 were waited for; matrix products, arithmetic and copies ran while one was open for 2% of the time, Pallas kernels for 16%

profile of v8, /device:TPU:0, one launch (start us, length us, event | category | flops | bytes accessed | tf_op | source)
XLA Modules:
  0.0 151.4 jit_solution(5969220290314266502)
XLA Ops:
  0.7 3.0 %collective-permute-start = (bf16[384,2048]{1,0:T(8,128)(2,1)}, bf16[384,2048]{1,0:T(8,128)(2,1)S(1)}, u32[]{:S(2)}, u32[]{:S(2)}) collective-permute-start(bf16[384,2048]{1,0:T(8,128)(2,1)} %right_ref.5), channel_id=1, source_target_pairs={{0,4},{2,6},{4,0},{6,2},{8,12},{10,14},{12,8},{14,10},{16,20},{18,... | collective-permute-start | bytes 4718600 | tf_op jit(solution)/shard_map/ppermute | solution.py:17
  3.7 2.6 %collective-permute-start.2 = (bf16[384,2048]{1,0:T(8,128)(2,1)}, bf16[384,2048]{1,0:T(8,128)(2,1)S(1)}, u32[]{:S(2)}, u32[]{:S(2)}) collective-permute-start(bf16[384,2048]{1,0:T(8,128)(2,1)} %right_ref.5), channel_id=1, source_target_pairs={{0,16},{2,18},{4,20},{6,22},{8,24},{10,26},{12,28},{14,30},{16,0},... | collective-permute-start | bytes 4718600 | tf_op jit(solution)/shard_map/ppermute | solution.py:17
  6.3 1.6 %collective-permute-start.4 = (bf16[384,2048]{1,0:T(8,128)(2,1)}, bf16[384,2048]{1,0:T(8,128)(2,1)S(1)}, u32[]{:S(2)}, u32[]{:S(2)}) collective-permute-start(bf16[384,2048]{1,0:T(8,128)(2,1)} %right_ref.5), channel_id=1, source_target_pairs={{0,8},{2,10},{4,12},{6,14},{8,0},{10,2},{12,4},{14,6},{16,24},{18,... | collective-permute-start | bytes 4718600 | tf_op jit(solution)/shard_map/ppermute | solution.py:17
  7.9 1.4 slice.21
  9.3 0.6 collective-permute-start.6
  9.9 29.2 %collective-permute-done.refs_1_ = bf16[384,2048]{1,0:T(8,128)(2,1)S(1)} collective-permute-done((bf16[384,2048]{1,0:T(8,128)(2,1)}, bf16[384,2048]{1,0:T(8,128)(2,1)S(1)}, u32[]{:S(2)}, u32[]{:S(2)}) %collective-permute-start) | collective-permute-done | bytes 1572896 | tf_op jit(solution)/shard_map/ppermute | solution.py:17
  39.1 1.4 copy-done.2
  40.5 1.8 %shard_map.67.refs_0_ = f32[2,384,384]{2,1,0:T(8,128)S(1)} custom-call(bf16[384,2048]{1,0:T(8,128)(2,1)S(1)} %copy-done.1, bf16[384,2048]{1,0:T(8,128)(2,1)S(1)} %copy-done.2, bf16[384,2048]{1,0:T(8,128)(2,1)S(1)} %collective-permute-done.refs_1_), custom_call_target="tpu_custom_call" | custom-call | tf_op jit(solution)/shard_map/pallas_call | solution.py:32
  42.4 0.1 collective-permute-start.1
  42.5 2.1 %collective-permute-start.7 = (bf16[64,2048]{1,0:T(8,128)(2,1)S(1)}, bf16[64,2048]{1,0:T(8,128)(2,1)S(1)}, u32[]{:S(2)}, u32[]{:S(2)}) collective-permute-start(bf16[64,2048]{1,0:T(8,128)(2,1)S(1)} %slice.22), channel_id=1, source_target_pairs={{0,4},{2,6},{4,0},{6,2},{8,12},{10,14},{12,8},{14,10},{16,20},{18,... | collective-permute-start | bytes 786440 | tf_op jit(solution)/shard_map/ppermute | solution.py:17
  44.6 1.0 shard_map.76.refs_0_
  45.6 21.6 %collective-permute-done.6.upper_ref.refs_1_ = bf16[320,2048]{1,0:T(8,128)(2,1)S(1)} collective-permute-done((bf16[320,2048]{1,0:T(8,128)(2,1)S(1)}, bf16[320,2048]{1,0:T(8,128)(2,1)S(1)}, u32[]{:S(2)}, u32[]{:S(2)}) %collective-permute-start.6) | collective-permute-done | bytes 1310752 | tf_op jit(solution)/shard_map/ppermute | solution.py:17
  67.2 3.1 %collective-permute-start.14 = (bf16[208,2048]{1,0:T(8,128)(2,1)}, bf16[208,2048]{1,0:T(8,128)(2,1)}, u32[]{:S(2)}, u32[]{:S(2)}) collective-permute-start(bf16[208,2048]{1,0:T(8,128)(2,1)} %shard_map.77), channel_id=1, source_target_pairs={{0,16},{2,18},{4,20},{6,22},{8,24},{10,26},{12,28},{14,30},{16,0},... | collective-permute-start | bytes 2555912 | tf_op jit(solution)/shard_map/ppermute | solution.py:17
  70.3 1.7 %collective-permute-done.7.lower_ref = bf16[64,2048]{1,0:T(8,128)(2,1)S(1)} collective-permute-done((bf16[64,2048]{1,0:T(8,128)(2,1)S(1)}, bf16[64,2048]{1,0:T(8,128)(2,1)S(1)}, u32[]{:S(2)}, u32[]{:S(2)}) %collective-permute-start.7) | collective-permute-done | bytes 262176 | tf_op jit(solution)/shard_map/ppermute | solution.py:17
  72.0 1.8 %collective-permute-start.16 = (bf16[208,2048]{1,0:T(8,128)(2,1)}, bf16[208,2048]{1,0:T(8,128)(2,1)}, u32[]{:S(2)}, u32[]{:S(2)}) collective-permute-start(bf16[208,2048]{1,0:T(8,128)(2,1)} %shard_map.77), channel_id=1, source_target_pairs={{0,8},{2,10},{4,12},{6,14},{8,0},{10,2},{12,4},{14,6},{16,24},{18,... | collective-permute-start | bytes 2555912 | tf_op jit(solution)/shard_map/ppermute | solution.py:17
  73.8 0.1 shard_map.70.refs_0_.refs_8_
  73.9 1.9 %shard_map.71.refs_0_ = f32[384,384]{1,0:T(8,128)} custom-call(bf16[384,2048]{1,0:T(8,128)(2,1)S(1)} %copy-done.3, bf16[384,2048]{1,0:T(8,128)(2,1)S(1)} %shard_map.70.refs_0_.refs_8_), custom_call_target="tpu_custom_call" | custom-call | tf_op jit(solution)/shard_map/pallas_call | solution.py:32
  75.8 16.7 %collective-permute-done.2.refs_0_.refs_3_ = bf16[384,2048]{1,0:T(8,128)(2,1)S(1)} collective-permute-done((bf16[384,2048]{1,0:T(8,128)(2,1)}, bf16[384,2048]{1,0:T(8,128)(2,1)S(1)}, u32[]{:S(2)}, u32[]{:S(2)}) %collective-permute-start.2) | collective-permute-done | bytes 1572896 | tf_op jit(solution)/shard_map/ppermute | solution.py:17
  92.6 1.8 %shard_map.68.refs_2_ = f32[1,384,384]{2,1,0:T(8,128)} custom-call(bf16[384,2048]{1,0:T(8,128)(2,1)S(1)} %copy-done.1, bf16[384,2048]{1,0:T(8,128)(2,1)S(1)} %collective-permute-done.2.refs_0_.refs_3_, f32[2,384,384]{2,1,0:T(8,128)S(1)} %collective-permute-done.1.refs_1_), custom_call_target="tpu_custom_call" | custom-call | tf_op jit(solution)/shard_map/pallas_call | solution.py:32
  94.4 0.5 collective-permute-start.3
  94.9 1.8 %shard_map.69.refs_4_ = f32[1,384,384]{2,1,0:T(8,128)} custom-call(bf16[384,2048]{1,0:T(8,128)(2,1)S(1)} %copy-done.1, bf16[384,2048]{1,0:T(8,128)(2,1)S(1)} %collective-permute-done.4.refs_0_.refs_2_, f32[2,384,384]{2,1,0:T(8,128)S(1)} %collective-permute-done.1.refs_1_), custom_call_target="tpu_custom_call" | custom-call | tf_op jit(solution)/shard_map/pallas_call | solution.py:32
  96.7 0.1 copy.8.refs_6_.pos_ref
  96.9 0.2 dynamic-slice_reduce_fusion.act_ref
  97.1 2.0 %collective-permute-done.5.refs_5_ = f32[1,384,384]{2,1,0:T(8,128)} collective-permute-done((f32[1,384,384]{2,1,0:T(8,128)}, f32[1,384,384]{2,1,0:T(8,128)}, u32[]{:S(2)}, u32[]{:S(2)}) %collective-permute-start.5) | collective-permute-done | bytes 589856 | tf_op jit(solution)/shard_map/ppermute | solution.py:17
  99.1 1.3 copy-done.7
  100.3 1.3 copy-done.15
  101.6 3.0 %shard_map.72 = (f32[4,384,384]{2,1,0:T(8,128)S(1)}, f32[384,1]{1,0:T(8,128)S(1)}, f32[8,384]{1,0:T(8,128)S(1)}) custom-call(s32[3]{0:T(128)S(1)} %dynamic-slice_reduce_fusion.act_ref, f32[2,384,384]{2,1,0:T(8,128)S(1)} %copy-done.15, f32[2,384,384]{2,1,0:T(8,128)S(1)} %copy-done.7, f32[1,384,384]{2,1,0:T(8,128)} %shard_map.68.refs_2_, ...), custom_call_target="tpu_custom_call" | custom-call | tf_op jit(solution)/shard_map/pallas_call | solution.py:32
  104.6 0.1 collective-permute-start.10
  104.7 0.1 collective-permute-start.9
  104.8 6.8 %collective-permute-done.14.refs_1_.refs_0_.refs_9_ = bf16[208,2048]{1,0:T(8,128)(2,1)} collective-permute-done((bf16[208,2048]{1,0:T(8,128)(2,1)}, bf16[208,2048]{1,0:T(8,128)(2,1)}, u32[]{:S(2)}, u32[]{:S(2)}) %collective-permute-start.14) | collective-permute-done | bytes 852000 | tf_op jit(solution)/shard_map/ppermute | solution.py:17
  111.7 0.1 collective-permute-start.15
  111.8 3.9 %collective-permute-start.17 = (bf16[176,2048]{1,0:T(8,128)(2,1)S(1)}, bf16[176,2048]{1,0:T(8,128)(2,1)S(1)}, u32[]{:S(2)}, u32[]{:S(2)}) collective-permute-start(bf16[176,2048]{1,0:T(8,128)(2,1)S(1)} %shard_map.79), channel_id=1, source_target_pairs={{0,8},{2,10},{4,12},{6,14},{8,0},{10,2},{12,4},{14,6},{16,24},{18,... | collective-permute-start | bytes 2162696 | tf_op jit(solution)/shard_map/ppermute | solution.py:17
  115.7 0.6 collective-permute-start.12
  116.3 2.6 %shard_map.80 = (f32[208,384]{1,0:T(8,128)S(1)}, f32[208,384]{1,0:T(8,128)S(1)}) custom-call(bf16[384,2048]{1,0:T(8,128)(2,1)S(1)} %copy-done.3, bf16[208,2048]{1,0:T(8,128)(2,1)} %collective-permute-done.14.refs_1_.refs_0_.refs_9_, bf16[208,2048]{1,0:T(8,128)(2,1)} %collective-permute-done.16.refs_1_.refs_10_, f32[4,8,384]{2,1,0:T(8,128)S(1)} %shard_map.73.refs_2_), custom_call_target="tpu_custom_call" | custom-call | tf_op jit(solution)/shard_map/pallas_call | solution.py:32
  118.8 0.1 collective-permute-start.18
  118.9 0.5 collective-permute-start.19
  119.4 0.4 collective-permute-done.12
  119.9 1.7 %shard_map.74 = (bf16[4,384,384]{2,1,0:T(8,128)(2,1)S(1)}, bf16[384,384]{1,0:T(8,128)(2,1)S(1)}, f32[8,384]{1,0:T(8,128)S(1)}, f32[384,8]{1,0:T(8,128)S(1)}, f32[8,128]{1,0:T(8,128)S(1)}) custom-call(s32[3]{0:T(128)S(1)} %dynamic-slice_reduce_fusion.act_ref, f32[4,384,384]{2,1,0:T(8,128)S(1)} %get-tuple-element.15.tile_ref, ...), custom_call_target="tpu_custom_call" | custom-call | flops 4714999808 | tf_op jit(solution)/shard_map/pallas_call | solution.py:32
  121.5 0.5 slice.27
  122.1 1.5 collective-permute-start.13
  123.6 4.3 %shard_map.75 = (f32[384,2048]{1,0:T(8,128)}, f32[8,128]{1,0:T(8,128)S(1)}) custom-call(bf16[4,384,384]{2,1,0:T(8,128)(2,1)S(1)} %get-tuple-element.19.grad_ref, bf16[384,2048]{1,0:T(8,128)(2,1)S(1)} %copy-done.3, bf16[384,2048]{1,0:T(8,128)(2,1)S(1)} %copy-done.9, bf16[384,2048]{1,0:T(8,128)(2,1)S(1)} %copy-done.13, bf16[384,2048]{1,0:T(8,128)(2,1)S(1)} %copy-done.11), custom_call_target="tpu_custom_call" | custom-call | tf_op jit(solution)/shard_map/pallas_call | solution.py:32
  129.2 4.9 %shard_map.81.refs_3_.refs_2_ = f32[384,2048]{1,0:T(8,128)S(1)} custom-call(f32[8,384]{1,0:T(8,128)S(1)} %get-tuple-element.21.col_ref, f32[384,8]{1,0:T(8,128)S(1)} %get-tuple-element.22.far_ref, f32[384,384]{1,0:T(8,128)} %shard_map.71.refs_0_, f32[384,384]{1,0:T(8,128)} %collective-permute-done.8.refs_7_.refs_1_, ...), custom_call_target="tpu_custom_call" | custom-call | tf_op jit(solution)/shard_map/pallas_call | solution.py:32
  134.1 10.6 %collective-permute-done.15.refs_0_.refs_3_ = bf16[176,2048]{1,0:T(8,128)(2,1)S(1)} collective-permute-done((bf16[176,2048]{1,0:T(8,128)(2,1)S(1)}, bf16[176,2048]{1,0:T(8,128)(2,1)S(1)}, u32[]{:S(2)}, u32[]{:S(2)}) %collective-permute-start.15) | collective-permute-done | bytes 720928 | tf_op jit(solution)/shard_map/ppermute | solution.py:17
  144.6 0.2 collective-permute-done.17.refs_1_.refs_4_
  144.8 1.1 shard_map.82.refs_0_
  146.0 0.1 collective-permute-start.20
  146.0 1.9 %collective-permute-done.20.refs_1_ = f32[2,176,384]{2,1,0:T(8,128)S(1)} collective-permute-done((f32[2,176,384]{2,1,0:T(8,128)S(1)}, f32[2,176,384]{2,1,0:T(8,128)S(1)}, u32[]{:S(2)}, u32[]{:S(2)}) %collective-permute-start.20) | collective-permute-done | bytes 540704 | tf_op jit(solution)/shard_map/ppermute | solution.py:17
  148.0 2.3 %shard_map.83 = f32[384,2048]{1,0:T(8,128)} custom-call(f32[8,384]{1,0:T(8,128)S(1)} %get-tuple-element.21.col_ref, f32[384,8]{1,0:T(8,128)S(1)} %get-tuple-element.22.far_ref, f32[2,176,384]{2,1,0:T(8,128)S(1)} %shard_map.82.refs_0_, f32[2,176,384]{2,1,0:T(8,128)S(1)} %collective-permute-done.20.refs_1_, f32[384,2048]{1,0:T(8,128)S(1)} %shard_map.81.refs_3_.refs_2_, ...), custom_call_target="tpu_custom_call" | custom-call | tf_op jit(solution)/shard_map/pallas_call | solution.py:32
  (51 shorter events, 0.3 us)
Async XLA Ops:
  0.6 96.2 %copy-start = (s32[16,3]{0,1:T(4,128)S(1)}, s32[16,3]{0,1:T(4,128)}, u32[]{:S(2)}) copy-start(s32[16,3]{0,1:T(4,128)} %param.7) | copy-start | bytes 580
  0.6 38.5 %copy-start.1 = (bf16[384,2048]{1,0:T(8,128)(2,1)S(1)}, bf16[384,2048]{1,0:T(8,128)(2,1)}, u32[]{:S(2)}) copy-start(bf16[384,2048]{1,0:T(8,128)(2,1)} %refs_7_.1) | copy-start | bytes 4718596
  0.7 38.5 %collective-permute-start = (bf16[384,2048]{1,0:T(8,128)(2,1)}, bf16[384,2048]{1,0:T(8,128)(2,1)S(1)}, u32[]{:S(2)}, u32[]{:S(2)}) collective-permute-start(bf16[384,2048]{1,0:T(8,128)(2,1)} %right_ref.5), channel_id=1, source_target_pairs={{0,4},{2,6},{4,0},{6,2},{8,12},{10,14},{12,8},{14,10},{16,20},{18,... | collective-permute-start | bytes 4718600 | tf_op jit(solution)/shard_map/ppermute | solution.py:17
  3.7 88.9 %collective-permute-start.2 = (bf16[384,2048]{1,0:T(8,128)(2,1)}, bf16[384,2048]{1,0:T(8,128)(2,1)S(1)}, u32[]{:S(2)}, u32[]{:S(2)}) collective-permute-start(bf16[384,2048]{1,0:T(8,128)(2,1)} %right_ref.5), channel_id=1, source_target_pairs={{0,16},{2,18},{4,20},{6,22},{8,24},{10,26},{12,28},{14,30},{16,0},... | collective-permute-start | bytes 4718600 | tf_op jit(solution)/shard_map/ppermute | solution.py:17
  6.3 88.6 %collective-permute-start.4 = (bf16[384,2048]{1,0:T(8,128)(2,1)}, bf16[384,2048]{1,0:T(8,128)(2,1)S(1)}, u32[]{:S(2)}, u32[]{:S(2)}) collective-permute-start(bf16[384,2048]{1,0:T(8,128)(2,1)} %right_ref.5), channel_id=1, source_target_pairs={{0,8},{2,10},{4,12},{6,14},{8,0},{10,2},{12,4},{14,6},{16,24},{18,... | collective-permute-start | bytes 4718600 | tf_op jit(solution)/shard_map/ppermute | solution.py:17
  9.3 57.9 %collective-permute-start.6 = (bf16[320,2048]{1,0:T(8,128)(2,1)S(1)}, bf16[320,2048]{1,0:T(8,128)(2,1)S(1)}, u32[]{:S(2)}, u32[]{:S(2)}) collective-permute-start(bf16[320,2048]{1,0:T(8,128)(2,1)S(1)} %slice.21), channel_id=1, source_target_pairs={{0,4},{2,6},{4,0},{6,2},{8,12},{10,14},{12,8},{14,10},{16,20},{18,... | collective-permute-start | bytes 3932168 | tf_op jit(solution)/shard_map/ppermute | solution.py:17
  39.1 1.4 copy-start.2
  40.5 1.8 %copy-start.8 = (bf16[384,2048]{1,0:T(8,128)(2,1)}, bf16[384,2048]{1,0:T(8,128)(2,1)S(1)}, u32[]{:S(2)}) copy-start(bf16[384,2048]{1,0:T(8,128)(2,1)S(1)} %collective-permute-done.refs_1_) | copy-start | bytes 4718596
  42.3 24.9 %copy-start.14 = (f32[2,384,384]{2,1,0:T(8,128)}, f32[2,384,384]{2,1,0:T(8,128)S(1)}, u32[]{:S(2)}) copy-start(f32[2,384,384]{2,1,0:T(8,128)S(1)} %shard_map.67.refs_0_) | copy-start | bytes 3538948
  42.4 50.2 %collective-permute-start.1 = (f32[2,384,384]{2,1,0:T(8,128)S(1)}, f32[2,384,384]{2,1,0:T(8,128)S(1)}, u32[]{:S(2)}, u32[]{:S(2)}) collective-permute-start(f32[2,384,384]{2,1,0:T(8,128)S(1)} %shard_map.67.refs_0_), channel_id=1, source_target_pairs={{0,1},{1,0},{2,3},{3,2},{4,5},{5,4},{6,7},{7,6},{8,9},{9,8},{10,11... | collective-permute-start | bytes 3538952 | tf_op jit(solution)/shard_map/ppermute | solution.py:17
  42.5 29.5 %collective-permute-start.7 = (bf16[64,2048]{1,0:T(8,128)(2,1)S(1)}, bf16[64,2048]{1,0:T(8,128)(2,1)S(1)}, u32[]{:S(2)}, u32[]{:S(2)}) collective-permute-start(bf16[64,2048]{1,0:T(8,128)(2,1)S(1)} %slice.22), channel_id=1, source_target_pairs={{0,4},{2,6},{4,0},{6,2},{8,12},{10,14},{12,8},{14,10},{16,20},{18,... | collective-permute-start | bytes 786440 | tf_op jit(solution)/shard_map/ppermute | solution.py:17
  67.2 6.7 %copy-start.3 = (bf16[384,2048]{1,0:T(8,128)(2,1)S(1)}, bf16[384,2048]{1,0:T(8,128)(2,1)}, u32[]{:S(2)}) copy-start(bf16[384,2048]{1,0:T(8,128)(2,1)} %right_ref.5) | copy-start | bytes 4718596
  67.2 44.4 %collective-permute-start.14 = (bf16[208,2048]{1,0:T(8,128)(2,1)}, bf16[208,2048]{1,0:T(8,128)(2,1)}, u32[]{:S(2)}, u32[]{:S(2)}) collective-permute-start(bf16[208,2048]{1,0:T(8,128)(2,1)} %shard_map.77), channel_id=1, source_target_pairs={{0,16},{2,18},{4,20},{6,22},{8,24},{10,26},{12,28},{14,30},{16,0},... | collective-permute-start | bytes 2555912 | tf_op jit(solution)/shard_map/ppermute | solution.py:17
  72.0 39.7 %collective-permute-start.16 = (bf16[208,2048]{1,0:T(8,128)(2,1)}, bf16[208,2048]{1,0:T(8,128)(2,1)}, u32[]{:S(2)}, u32[]{:S(2)}) collective-permute-start(bf16[208,2048]{1,0:T(8,128)(2,1)} %shard_map.77), channel_id=1, source_target_pairs={{0,8},{2,10},{4,12},{6,14},{8,0},{10,2},{12,4},{14,6},{16,24},{18,... | collective-permute-start | bytes 2555912 | tf_op jit(solution)/shard_map/ppermute | solution.py:17
  73.9 1.9 %copy-start.4 = (bf16[384,2048]{1,0:T(8,128)(2,1)}, bf16[384,2048]{1,0:T(8,128)(2,1)S(1)}, u32[]{:S(2)}) copy-start(bf16[384,2048]{1,0:T(8,128)(2,1)S(1)} %shard_map.70.refs_0_.refs_8_) | copy-start | bytes 4718596
  92.5 1.8 %copy-start.10 = (bf16[384,2048]{1,0:T(8,128)(2,1)}, bf16[384,2048]{1,0:T(8,128)(2,1)S(1)}, u32[]{:S(2)}) copy-start(bf16[384,2048]{1,0:T(8,128)(2,1)S(1)} %collective-permute-done.2.refs_0_.refs_3_) | copy-start | bytes 4718596
  92.5 4.5 %collective-permute-start.8 = (f32[384,384]{1,0:T(8,128)}, f32[384,384]{1,0:T(8,128)}, u32[]{:S(2)}, u32[]{:S(2)}) collective-permute-start(f32[384,384]{1,0:T(8,128)} %shard_map.71.refs_0_), channel_id=1, source_target_pairs={{0,1},{1,0},{2,3},{3,2},{4,5},{5,4},{6,7},{7,6},{8,9},{9,8},{10,11... | collective-permute-start | bytes 1769480 | tf_op jit(solution)/shard_map/ppermute | solution.py:17
  92.5 2.3 %copy-start.6 = (f32[2,384,384]{2,1,0:T(8,128)}, f32[2,384,384]{2,1,0:T(8,128)S(1)}, u32[]{:S(2)}) copy-start(f32[2,384,384]{2,1,0:T(8,128)S(1)} %collective-permute-done.1.refs_1_) | copy-start | bytes 3538948
  94.4 2.4 %copy-start.16 = (s32[1,384]{1,0:T(1,128)S(1)}, s32[1,384]{1,0:T(1,128)}, u32[]{:S(2)}) copy-start(s32[1,384]{1,0:T(1,128)} %param.6) | copy-start | bytes 4612
  94.4 2.7 %collective-permute-start.3 = (f32[1,384,384]{2,1,0:T(8,128)}, f32[1,384,384]{2,1,0:T(8,128)}, u32[]{:S(2)}, u32[]{:S(2)}) collective-permute-start(f32[1,384,384]{2,1,0:T(8,128)} %shard_map.68.refs_2_), channel_id=1, source_target_pairs={{0,1},{1,0},{2,3},{3,2},{4,5},{5,4},{6,7},{7,6},{8,9},{9,8},{10,11... | collective-permute-start | bytes 1769480 | tf_op jit(solution)/shard_map/ppermute | solution.py:17
  94.9 1.8 %copy-start.12 = (bf16[384,2048]{1,0:T(8,128)(2,1)}, bf16[384,2048]{1,0:T(8,128)(2,1)S(1)}, u32[]{:S(2)}) copy-start(bf16[384,2048]{1,0:T(8,128)(2,1)S(1)} %collective-permute-done.4.refs_0_.refs_2_) | copy-start | bytes 4718596
  96.7 2.3 %collective-permute-start.5 = (f32[1,384,384]{2,1,0:T(8,128)}, f32[1,384,384]{2,1,0:T(8,128)}, u32[]{:S(2)}, u32[]{:S(2)}) collective-permute-start(f32[1,384,384]{2,1,0:T(8,128)} %shard_map.69.refs_4_), channel_id=1, source_target_pairs={{0,1},{1,0},{2,3},{3,2},{4,5},{5,4},{6,7},{7,6},{8,9},{9,8},{10,11... | collective-permute-start | bytes 1769480 | tf_op jit(solution)/shard_map/ppermute | solution.py:17
  99.0 1.3 copy-start.7
  100.3 1.3 copy-start.15
  104.6 11.1 %collective-permute-start.10 = (f32[8,384]{1,0:T(8,128)S(1)}, f32[8,384]{1,0:T(8,128)S(1)}, u32[]{:S(2)}, u32[]{:S(2)}) collective-permute-start(f32[8,384]{1,0:T(8,128)S(1)} %get-tuple-element.17.refs_0_), channel_id=1, source_target_pairs={{0,20},{2,22},{4,16},{6,18},{8,28},{10,30},{12,24},{14,26},{16,4},... | collective-permute-start | bytes 36872 | tf_op jit(solution)/shard_map/ppermute | solution.py:17
  104.7 11.0 %collective-permute-start.11 = (f32[8,384]{1,0:T(8,128)S(1)}, f32[8,384]{1,0:T(8,128)S(1)}, u32[]{:S(2)}, u32[]{:S(2)}) collective-permute-start(f32[8,384]{1,0:T(8,128)S(1)} %get-tuple-element.17.refs_0_), channel_id=1, source_target_pairs={{0,28},{2,30},{4,24},{6,26},{8,20},{10,22},{12,16},{14,18},{16,12}... | collective-permute-start | bytes 36872 | tf_op jit(solution)/shard_map/ppermute | solution.py:17
  104.7 10.9 %collective-permute-start.9 = (f32[8,384]{1,0:T(8,128)S(1)}, f32[8,384]{1,0:T(8,128)S(1)}, u32[]{:S(2)}, u32[]{:S(2)}) collective-permute-start(f32[8,384]{1,0:T(8,128)S(1)} %get-tuple-element.17.refs_0_), channel_id=1, source_target_pairs={{0,12},{2,14},{4,8},{6,10},{8,4},{10,6},{12,0},{14,2},{16,28},{18,... | collective-permute-start | bytes 36872 | tf_op jit(solution)/shard_map/ppermute | solution.py:17
  111.7 33.0 %collective-permute-start.15 = (bf16[176,2048]{1,0:T(8,128)(2,1)S(1)}, bf16[176,2048]{1,0:T(8,128)(2,1)S(1)}, u32[]{:S(2)}, u32[]{:S(2)}) collective-permute-start(bf16[176,2048]{1,0:T(8,128)(2,1)S(1)} %shard_map.78), channel_id=1, source_target_pairs={{0,16},{2,18},{4,20},{6,22},{8,24},{10,26},{12,28},{14,30},{16,0},... | collective-permute-start | bytes 2162696 | tf_op jit(solution)/shard_map/ppermute | solution.py:17
  111.8 33.0 %collective-permute-start.17 = (bf16[176,2048]{1,0:T(8,128)(2,1)S(1)}, bf16[176,2048]{1,0:T(8,128)(2,1)S(1)}, u32[]{:S(2)}, u32[]{:S(2)}) collective-permute-start(bf16[176,2048]{1,0:T(8,128)(2,1)S(1)} %shard_map.79), channel_id=1, source_target_pairs={{0,8},{2,10},{4,12},{6,14},{8,0},{10,2},{12,4},{14,6},{16,24},{18,... | collective-permute-start | bytes 2162696 | tf_op jit(solution)/shard_map/ppermute | solution.py:17
  115.7 4.2 %collective-permute-start.12 = (f32[4,8,384]{2,1,0:T(8,128)S(1)}, f32[4,8,384]{2,1,0:T(8,128)S(1)}, u32[]{:S(2)}, u32[]{:S(2)}) collective-permute-start(f32[4,8,384]{2,1,0:T(8,128)S(1)} %shard_map.73.refs_2_), channel_id=1, source_target_pairs={{0,4},{2,6},{4,0},{6,2},{8,12},{10,14},{12,8},{14,10},{16,20},{18,... | collective-permute-start | bytes 147464 | tf_op jit(solution)/shard_map/ppermute | solution.py:17
  118.8 10.3 %collective-permute-start.18 = (f32[208,384]{1,0:T(8,128)S(1)}, f32[208,384]{1,0:T(8,128)S(1)}, u32[]{:S(2)}, u32[]{:S(2)}) collective-permute-start(f32[208,384]{1,0:T(8,128)S(1)} %get-tuple-element.24.refs_2_), channel_id=1, source_target_pairs={{0,1},{1,0},{2,3},{3,2},{4,5},{5,4},{6,7},{7,6},{8,9},{9,8},{10,11... | collective-permute-start | bytes 958472 | tf_op jit(solution)/shard_map/ppermute | solution.py:17
  118.9 10.3 %collective-permute-start.19 = (f32[208,384]{1,0:T(8,128)S(1)}, f32[208,384]{1,0:T(8,128)S(1)}, u32[]{:S(2)}, u32[]{:S(2)}) collective-permute-start(f32[208,384]{1,0:T(8,128)S(1)} %get-tuple-element.25.refs_4_), channel_id=1, source_target_pairs={{0,1},{1,0},{2,3},{3,2},{4,5},{5,4},{6,7},{7,6},{8,9},{9,8},{10,11... | collective-permute-start | bytes 958472 | tf_op jit(solution)/shard_map/ppermute | solution.py:17
  119.9 3.7 %copy-start.9 = (bf16[384,2048]{1,0:T(8,128)(2,1)S(1)}, bf16[384,2048]{1,0:T(8,128)(2,1)}, u32[]{:S(2)}) copy-start(bf16[384,2048]{1,0:T(8,128)(2,1)} %copy-done.8) | copy-start | bytes 4718596
  119.9 3.7 %copy-start.11 = (bf16[384,2048]{1,0:T(8,128)(2,1)S(1)}, bf16[384,2048]{1,0:T(8,128)(2,1)}, u32[]{:S(2)}) copy-start(bf16[384,2048]{1,0:T(8,128)(2,1)} %copy-done.10) | copy-start | bytes 4718596
  119.9 3.7 %copy-start.13 = (bf16[384,2048]{1,0:T(8,128)(2,1)S(1)}, bf16[384,2048]{1,0:T(8,128)(2,1)}, u32[]{:S(2)}) copy-start(bf16[384,2048]{1,0:T(8,128)(2,1)} %copy-done.12) | copy-start | bytes 4718596
  122.1 5.8 %collective-permute-start.13 = (f32[1]{0:T(128)}, f32[1]{0:T(128)}, u32[]{:S(2)}, u32[]{:S(2)}) collective-permute-start(f32[1]{0:T(128)} %bitcast.5), channel_id=1, source_target_pairs={{0,2},{2,0},{4,6},{6,4},{8,10},{10,8},{12,14},{14,12},{16,18},{18,... | collective-permute-start | bytes 20 | tf_op jit(solution)/shard_map/ppermute | solution.py:17
  123.6 5.6 %copy-start.5 = (bf16[384,2048]{1,0:T(8,128)(2,1)S(1)}, bf16[384,2048]{1,0:T(8,128)(2,1)}, u32[]{:S(2)}) copy-start(bf16[384,2048]{1,0:T(8,128)(2,1)} %copy-done.4) | copy-start | bytes 4718596
  146.0 2.0 %collective-permute-start.20 = (f32[2,176,384]{2,1,0:T(8,128)S(1)}, f32[2,176,384]{2,1,0:T(8,128)S(1)}, u32[]{:S(2)}, u32[]{:S(2)}) collective-permute-start(f32[2,176,384]{2,1,0:T(8,128)S(1)} %shard_map.82.refs_0_), channel_id=1, source_target_pairs={{0,1},{1,0},{2,3},{3,2},{4,5},{5,4},{6,7},{7,6},{8,9},{9,8},{10,11... | collective-permute-start | bytes 1622024 | tf_op jit(solution)/shard_map/ppermute | solution.py:17
